TPU v7x, 512 devices: a whole 4x4x16 slice. The times are simulated.
512 devices in a mesh: batch: 16 (over z), proto: 32 (over y, x, core).
Axes of the slice: x: 4, y: 4, z: 16, core: 2. Of those that a mesh axis runs over, the one named last changes fastest.
Arguments:
- embeddings: float32 [4096, 128], P(('batch', 'proto')), may hold values from -6 to 6
- prototypes: float32 [131072, 128], P(('batch', 'proto')), may hold values from -6 to 6
- partner: int32 [4096], P('batch'), may hold values from 0 to 4095, each once
Outputs:
- grad_embeddings: float32 [4096, 128], P(('batch', 'proto'))
- grad_prototypes: float32 [131072, 128], P(('batch', 'proto'))
Inputs may be any that keep to these rules, and one draw needn't show every extreme that they name: partner is a permutation of the 4096 clips.
All inputs are finite; a program needn't handle non-finite values.
Results may differ from a plain program's by a relative error of at most 0.0003.
Values sent between devices are 32-bit elements; how exact they have to be, the bound alone decides.
No kernel may reach another device: no remote copies, remote signals or barrier semaphores. Data moves between devices by JAX's collectives and lax.ppermute only.
A program may use at most 64 MiB of HBM per device.

v0:
```python
import jax
import jax.numpy as jnp
from jax import lax
from jax.sharding import PartitionSpec as P

ITERS = 3


SINK_EPS = 0.05
SOFTMAX_TEMP = 0.1


def unit_rows(values):
    inverse = 1.0 / jnp.sqrt(jnp.sum(values * values, axis=1, keepdims=True) + 1e-06)
    return (values * inverse, inverse)


def pairwise_scores(left, right):
    return lax.dot_general(
        left,
        right,
        (((1,), (1,)), ((), ())),
        precision=lax.Precision.HIGHEST,
        preferred_element_type=jnp.float32,
    )


def finish_rows(units, inverse, grads):
    return inverse * (grads - units * jnp.sum(units * grads, axis=1, keepdims=True))


def local(embeddings, prototypes, partner):
    clip_block = lax.all_gather(embeddings, "proto", axis=0, tiled=True)
    full_protos = lax.all_gather(prototypes, "batch", axis=0, tiled=True)
    normalized_clips = unit_rows(clip_block)[0]
    unit_protos, proto_inverse = unit_rows(full_protos)
    logit_scores = pairwise_scores(normalized_clips, unit_protos)
    kernel = jnp.exp(logit_scores / SINK_EPS)
    softmax_exponent = jnp.exp(logit_scores / SOFTMAX_TEMP)
    soft_part = jnp.sum(softmax_exponent, axis=1)
    clip_count = clip_block.shape[0] * lax.axis_size("batch")
    proto_count = full_protos.shape[0] * lax.axis_size("proto")
    row_scale = jnp.ones((clip_block.shape[0],), jnp.float32)
    for sweep in range(ITERS):
        col_mass = lax.psum(jnp.sum(kernel * row_scale[:, None], axis=0), "batch")
        col_scale = 1.0 / (proto_count * col_mass)
        col_scale, row_part = (col_scale, jnp.sum(kernel * col_scale[None, :], axis=1))
        row_scale = 1.0 / (clip_count * lax.psum(row_part, "proto"))
    softmax_denominator = lax.psum(soft_part, "proto")
    every_clip, every_scale = (
        lax.all_gather(clip_block, "batch", axis=0, tiled=True),
        lax.all_gather(row_scale, "batch", axis=0, tiled=True),
    )
    every_units = unit_rows(every_clip)[0]
    mate_units = jnp.take(every_units, partner, axis=0)
    mate_scale = jnp.take(every_scale, partner, axis=0)
    assigned_target = (
        clip_count
        * jnp.exp(pairwise_scores(mate_units, unit_protos) / SINK_EPS)
        * mate_scale[:, None]
        * col_scale[None, :]
    )
    gradient_patch = (
        softmax_exponent / softmax_denominator[:, None] - assigned_target
    ) / SOFTMAX_TEMP
    clip_grads = lax.psum_scatter(
        jnp.dot(
            gradient_patch,
            unit_protos,
            precision=lax.Precision.HIGHEST,
            preferred_element_type=jnp.float32,
        ),
        "proto",
        scatter_dimension=0,
        tiled=True,
    )
    own_units, own_inverse = unit_rows(embeddings)
    grad_embeddings = finish_rows(own_units, own_inverse, clip_grads)
    proto_term = lax.dot_general(
        gradient_patch,
        normalized_clips,
        (((0,), (0,)), ((), ())),
        precision=lax.Precision.HIGHEST,
        preferred_element_type=jnp.float32,
    )
    proto_term = finish_rows(unit_protos, proto_inverse, proto_term)
    grad_prototypes = lax.psum_scatter(proto_term, "batch", scatter_dimension=0, tiled=True)
    return (grad_embeddings, grad_prototypes)


def solution(mesh):
    in_specs = (P(("batch", "proto"), None), P(("batch", "proto"), None), P("batch"))
    out_specs = (P(("batch", "proto"), None), P(("batch", "proto"), None))
    return jax.shard_map(local, mesh=mesh, in_specs=in_specs, out_specs=out_specs, check_vma=False)
```

profile of v0, /device:TPU:1, one launch (start us, length us, event | category | flops | bytes accessed | tf_op | source)
XLA Modules:
  0.0 708.0 jit_solution(2486582570814242278)
XLA Ops:
  7.2 0.0 all-gather.4.cloned.1.call-start
  7.2 1.7 copy.9
  8.9 0.0 all-gather.4.cloned.1.call-update
  8.9 0.0 all-gather.6.cloned.1.call-start
  8.9 29.8 %all_gather.12 = f32[256,128]{1,0:T(8,128)} all-gather(f32[8,128]{1,0:T(8,128)} %param.3), channel_id=1, replica_groups=mesh['batch'=16,'proto'=32] {'proto'}, dimensions={0}, use_global_device_ids=true | all-gather | bytes 135168 | tf_op jit(solution)/shard_map/all_gather | solution.py:33
  38.8 0.0 all-gather.6.cloned.1.call-update
  38.8 0.0 all-reduce.4.cloned.1.call-start
  38.8 1.0 multiply_reduce_fusion.8
  39.9 0.7 compare_select_fusion
  40.6 40.1 %all-gather.4.cloned.1.call-done = f32[4096,128]{0,1:T(8,128)} async-done(((f32[256,128]{0,1:T(8,128)}), f32[4096,128]{0,1:T(8,128)}) %all-gather.4.cloned.1.call-update) | async-done | bytes 2097168 | tf_op jit(solution)/shard_map/all_gather | solution.py:34
  80.7 1.8 multiply_reduce_fusion.7
  82.4 7.5 %fusion.6 = (f32[4096]{0:T(1024)S(1)}, f32[256,4096]{1,0:T(8,128)}) fusion(f32[4096,128]{0,1:T(8,128)} %all-gather.4.cloned.1.call-done, f32[4096]{0:T(1024)S(1)} %add_rsqrt_fusion.1, f32[256,128]{1,0:T(8,128)} %all_gather.12, f32[256]{0:T(256)S(1)} %add_rsqrt_fusion.2), kind=kOutput, calls=%fused_computation.20 | convolution fusion | flops 1613262848 | bytes 6456320 | tf_op jit(solution)/shard_map/dot_general | solution.py:19
  89.9 42.3 %psum.50 = f32[4096]{0:T(1024)S(1)} all-reduce(f32[4096]{0:T(1024)S(1)} %get-tuple-element.14), channel_id=1, replica_groups=mesh['batch'=16,'proto'=32] {'batch'}, use_global_device_ids=true, to_apply=%region_7.0 | all-reduce | flops 4096 | bytes 32768 | tf_op jit(solution)/shard_map/psum | solution.py:45
  132.3 3.5 fusion.5
  135.8 84.1 %psum.51 = f32[256]{0:T(256)S(1)} all-reduce(f32[256]{0:T(256)S(1)} %get-tuple-element.9), channel_id=1, replica_groups=mesh['batch'=16,'proto'=32] {'proto'}, use_global_device_ids=true, to_apply=%region_9.0 | all-reduce | flops 256 | bytes 2048 | tf_op jit(solution)/shard_map/psum | solution.py:48
  219.9 2.9 multiply_reduce_fusion.3
  222.9 39.2 %psum.52 = f32[4096]{0:T(1024)S(1)} all-reduce(f32[4096]{0:T(1024)S(1)} %multiply_reduce_fusion.3), channel_id=1, replica_groups=mesh['batch'=16,'proto'=32] {'batch'}, use_global_device_ids=true, to_apply=%region_11.0 | all-reduce | flops 4096 | bytes 32768 | tf_op jit(solution)/shard_map/psum | solution.py:45
  262.0 3.0 multiply_reduce_fusion.2
  265.0 76.1 %psum.53 = f32[256]{0:T(256)S(1)} all-reduce(f32[256]{0:T(256)S(1)} %multiply_reduce_fusion.2), channel_id=1, replica_groups=mesh['batch'=16,'proto'=32] {'proto'}, use_global_device_ids=true, to_apply=%region_13.0 | all-reduce | flops 256 | bytes 2048 | tf_op jit(solution)/shard_map/psum | solution.py:48
  341.1 2.9 multiply_reduce_fusion.1
  344.1 39.2 %psum.54 = f32[4096]{0:T(1024)S(1)} all-reduce(f32[4096]{0:T(1024)S(1)} %multiply_reduce_fusion.1), channel_id=1, replica_groups=mesh['batch'=16,'proto'=32] {'batch'}, use_global_device_ids=true, to_apply=%region_15.0 | all-reduce | flops 4096 | bytes 32768 | tf_op jit(solution)/shard_map/psum | solution.py:45
  383.3 3.0 multiply_reduce_fusion
  386.2 76.7 %all-reduce.1 = (f32[256]{0:T(256)S(1)}, f32[256]{0:T(256)S(1)}) all-reduce(f32[256]{0:T(256)S(1)} %multiply_reduce_fusion, f32[256]{0:T(256)S(1)} %get-tuple-element.8), channel_id=1, replica_groups=mesh['batch'=16,'proto'=32] {'proto'}, use_global_device_ids=true, to_apply=%region_17.18 | all-reduce | flops 512 | bytes 4096 | tf_op jit(solution)/shard_map/psum | solution.py:48
  462.9 19.3 %all-gather = f32[16,1,256]{2,1,0:T(1,128)S(1)} all-gather(f32[1,1,256]{2,1,0:T(1,128)S(1)} %bitcast.6), channel_id=1, replica_groups=mesh['batch'=16,'proto'=32] {'batch'}, dimensions={0}, use_global_device_ids=true | all-gather | bytes 17408 | tf_op jit(solution)/shard_map/all_gather | solution.py:52
  482.2 1.7 gather_fusion.1
  483.9 0.0 copy-done.4
  484.0 0.0 all-gather.6.cloned.1.call-done
  484.0 2.2 multiply_reduce_fusion.6
  486.2 3.6 broadcast_multiply_fusion
  489.8 2.3 gather_fusion
  492.1 6.7 fusion.4
  498.8 0.0 copy-start.1
  498.8 1.9 copy-done.1
  500.7 4.1 fusion.7
  504.8 0.0 all-reduce.4.cloned.1.call-update
  504.9 0.0 reduce-scatter.2.cloned.1.call-start
  504.9 4.9 multiply_reduce_fusion.5
  509.8 0.0 copy-start.3
  509.8 1.7 subtract_multiply_fusion
  511.6 0.0 reduce-scatter.2.cloned.1.call-update
  511.6 1.3 dynamic-slice
  513.5 0.0 copy-done.3
  513.5 0.1 multiply_reduce_fusion.10
  513.6 120.4 %all-reduce.4.cloned.1.call-done = f32[256,128]{1,0:T(8,128)} async-done(((f32[256,128]{1,0:T(8,128)}), f32[256,128]{1,0:T(8,128)}) %all-reduce.4.cloned.1.call-update) | async-done | bytes 131088
  634.0 0.9 multiply_reduce_fusion.9
  634.9 1.3 subtract_multiply_fusion.1
  636.2 63.6 %reduce-scatter.2.cloned.1.call-done = f32[256,128]{0,1:T(8,128)} async-done(((f32[4096,128]{0,1:T(8,128)}), f32[256,128]{0,1:T(8,128)}) %reduce-scatter.2.cloned.1.call-update) | async-done | bytes 131088 | tf_op jit(solution)/shard_map/reduce_scatter | solution.py:87
  699.9 1.7 copy.10
  (17 shorter events, 0.1 us)
Async XLA Ops:
  7.2 73.5 %all-gather.4.cloned.1.call-start = ((), (), s32[]{:S(2)}) async-start(), calls=%async_computation.1 | async-start | bytes 2228224 | tf_op jit(solution)/shard_map/all_gather | solution.py:34
  8.9 475.1 %all-gather.6.cloned.1.call-start = ((), (), s32[]{:S(2)}) async-start(), calls=%async_computation.2 | async-start | bytes 2228224 | tf_op jit(solution)/shard_map/all_gather | solution.py:51
  38.8 595.2 %all-reduce.4.cloned.1.call-start = ((), (), s32[]{:S(2)}) async-start(), calls=%async_computation.4 | async-start | bytes 262144
  341.1 142.8 %copy-start.4 = (s32[256]{0:T(256)S(1)}, s32[256]{0:T(256)}, u32[]{:S(2)}) copy-start(s32[256]{0:T(256)} %param.5) | copy-start | bytes 3076
  482.2 9.9 %copy-start = (f32[4096,128]{0,1:T(8,128)S(1)}, f32[4096,128]{0,1:T(8,128)}, u32[]{:S(2)}) copy-start(f32[4096,128]{0,1:T(8,128)} %all-gather.4.cloned.1.call-done) | copy-start | bytes 6291460
  498.8 1.9 copy-start.1
  500.7 4.2 copy-start.2
  504.9 195.0 %reduce-scatter.2.cloned.1.call-start = ((), (), s32[]{:S(2)}) async-start(), calls=%async_computation.3 | async-start | bytes 2228224 | tf_op jit(solution)/shard_map/reduce_scatter | solution.py:87
  509.8 3.7 copy-start.3
Sparse Core Ops, SparseCore 0:
  10.7 69.9 all-gather.3
  82.7 70.2 all-gather.5
  505.0 128.9 all-reduce.3
  636.9 62.8 reduce-scatter.1
where the time goes:
time: 718 us; the launch traced here: 708 us
  blocking collectives  407 us (57%)
  waiting for transfers between devices  224 us (31%)
  other arithmetic  28.7 us (4%)
  matrix products  23.1 us (3%)
  between operations  14.6 us (2%)
  local copies, waits for them, and re-layouts  10.6 us (1%)
    psum x3, blocking collectives, local(): row_scale = 1.0 / (clip_count * lax.psum(row_part, 'proto'))  237 us
    psum x3, blocking collectives, local(): col_mass = lax.psum(jnp.sum(kernel * row_scale[:, None], axis=0), 'batch')  121 us
    unnamed x5, waiting for transfers between devices  120 us
    reduce_scatter x1, waiting for transfers between devices, local(): lax.psum_scatter(proto_term, 'batch', scatter_dimension=0, tiled=True)  63.6 us
    all_gather x1, waiting for transfers between devices, local(): full_protos = lax.all_gather(prototypes, 'batch', axis=0, tiled=True)  40.1 us
    all_gather x1, blocking collectives, local(): clip_block = lax.all_gather(embeddings, 'proto', axis=0, tiled=True)  29.8 us
    all_gather x1, blocking collectives, local(): lax.all_gather(row_scale, 'batch', axis=0, tiled=True)  19.3 us
  transfers between devices with their start and end apart: 4, of which 3 were waited for; matrix products, arithmetic and copies ran while one was open for 5% of the time, Pallas kernels for 0%

commit v1 on v0

v1 whole, which is shorter than its diff:
```python
import functools

import jax
import jax.numpy as jnp
from jax import lax
from jax.experimental import pallas as pl
from jax.experimental.pallas import tpu as pltpu
from jax.sharding import PartitionSpec as P

LANES = 128
PAIR = 2 * LANES
CHUNK = 64
VMEM_BYTES = 24 * 1024 * 1024


def unit_rows(values):
    inverse = 1.0 / jnp.sqrt(jnp.sum(values * values, axis=1, keepdims=True) + 1e-06)
    return (values * inverse, inverse)


def split(values):
    high = values.astype(jnp.bfloat16)
    low = (values - high.astype(jnp.float32)).astype(jnp.bfloat16)
    return high, low


def dot(left, right):
    return jnp.dot(left, right, preferred_element_type=jnp.float32)


def dot_rows(left, right):
    return lax.dot_general(left, right, (((1,), (1,)), ((), ())), preferred_element_type=jnp.float32)


def call(body, out_shape, **kwargs):
    return pl.pallas_call(
        body, out_shape=out_shape, compiler_params=pltpu.CompilerParams(vmem_limit_bytes=VMEM_BYTES), **kwargs
    )


def f32(*shape):
    return jax.ShapeDtypeStruct(shape, jnp.float32)


def exponents(proto_pair, clips):
    high, low = split(clips)
    scores = dot_rows(proto_pair, jnp.concatenate([high, high], axis=1))
    scores = scores + dot_rows(proto_pair, jnp.concatenate([low, low], axis=1))
    return jnp.exp(scores * 10.0)


def scores_body(protos_ref, clips_ref, e_ref, part_ref, total_ref, x_ref):
    protos = protos_ref[...]
    pair = jnp.concatenate(split(protos), axis=1)
    turned_high, turned_low = split(protos.T)
    turned = jnp.concatenate([turned_high, turned_low], axis=0)
    for block in range(clips_ref.shape[0] // PAIR):
        cols = slice(block * PAIR, (block + 1) * PAIR)
        e = exponents(pair, clips_ref[cols, :])
        e_ref[:, cols] = e
        kernel = e * e
        both = kernel[:, :LANES] + kernel[:, LANES:]
        part_ref[...] = both if block == 0 else part_ref[...] + both
        totals = jnp.sum(e, axis=0, keepdims=True)
        high, low = split(e)
        x = dot(turned, high)
        x = x[:LANES] + x[LANES:] + dot(turned_high, low)
        for half in range(2):
            total_ref[2 * block + half : 2 * block + half + 1, :] = totals[:, half * LANES : (half + 1) * LANES]
            x_ref[2 * block + half] = x[:, half * LANES : (half + 1) * LANES]


def mates_body(index_ref, core_ref, protos_ref, own_ref, other_ref, e_ref, table_ref, mate_ref):
    rows = own_ref.shape[0]
    table_ref[:rows] = own_ref[...]
    table_ref[rows:] = other_ref[...]
    pair = jnp.concatenate(split(protos_ref[...]), axis=1)
    tiles = rows // LANES
    core = core_ref[0]
    for block in range(rows // PAIR):
        for half in range(2):
            tile = 2 * block + half

            def fetch(z, carry, tile=tile, half=half):
                start = (z * tiles + tile) * 16 + core * 8
                base = pl.multiple_of(half * LANES + z * 8, 8)
                picked = [table_ref[pl.ds(index_ref[start + r], 1), :] for r in range(8)]
                mate_ref[pl.ds(base, 8), :] = jnp.concatenate(picked, axis=0)
                return carry

            lax.fori_loop(0, LANES // 8, fetch, 0)
        e_ref[:, block * PAIR : (block + 1) * PAIR] = exponents(pair, mate_ref[...])


def column_scale(own_ref, other_ref, protos):
    half = own_ref.shape[0] // 2
    part = jnp.concatenate([own_ref[:half] + other_ref[half:], own_ref[half:] + other_ref[:half]], axis=0)
    return 1.0 / (protos * jnp.sum(part, axis=1, keepdims=True))


def row_mass(e_ref, scale, tile):
    e = e_ref[:, tile * LANES : (tile + 1) * LANES]
    return jnp.sum(e * e * scale, axis=0, keepdims=True)


def rows_body(protos, e_ref, own_ref, other_ref, *rest):
    *extra, out_ref = rest
    scale = jnp.broadcast_to(column_scale(own_ref, other_ref, protos), own_ref.shape)
    blocks, _, _ = out_ref.shape
    tiles = e_ref.shape[1] // LANES
    masses = jnp.concatenate([row_mass(e_ref, scale, tile) for tile in range(tiles)], axis=0)
    for block in range(blocks):
        out_ref[block, :tiles] = masses
        for ref in extra:
            out_ref[block, tiles:] = ref[...]


def cols_body(clips, e_ref, mass_ref, part_ref):
    tiles = e_ref.shape[1] // LANES
    scale = 1.0 / (clips * jnp.sum(mass_ref[:, :tiles, :], axis=0))
    for start in range(0, e_ref.shape[0], CHUNK):
        rows = slice(start, start + CHUNK)
        total = None
        for tile in range(tiles):
            e = e_ref[rows, tile * LANES : (tile + 1) * LANES]
            term = e * e * scale[tile : tile + 1, :]
            total = term if total is None else total + term
        part_ref[rows, :] = total


def mates_rows_body(protos, mate_e_ref, own_ref, other_ref, protos_ref, x_ref, totals_ref, out_ref, scale_ref):
    scale = jnp.broadcast_to(column_scale(own_ref, other_ref, protos), own_ref.shape)
    scale_ref[...] = scale
    wide = jnp.concatenate([scale, scale], axis=1)
    turned_high, turned_low = split(protos_ref[...].T)
    turned = jnp.concatenate([turned_high, turned_low], axis=0)
    tiles = mate_e_ref.shape[1] // LANES
    totals = 1.0 / totals_ref[...]
    masses = []
    for block in range(tiles // 2):
        e = mate_e_ref[:, block * PAIR : (block + 1) * PAIR]
        kernel = e * e * wide
        mass = jnp.sum(kernel, axis=0, keepdims=True)
        high, low = split(kernel)
        y = dot(turned, high)
        y = y[:LANES] + y[LANES:] + dot(turned_high, low)
        for half in range(2):
            tile = 2 * block + half
            lanes = slice(half * LANES, (half + 1) * LANES)
            masses.append(mass[:, lanes])
            out_ref[tile, :LANES] = x_ref[tile] * totals[tile : tile + 1, :]
            out_ref[tile, LANES : 2 * LANES] = y[:, lanes]
    masses = jnp.concatenate(masses, axis=0)
    for tile in range(tiles):
        out_ref[tile, 2 * LANES :] = masses


def turn_body(in_ref, out_ref):
    total = jnp.sum(in_ref[...], axis=0)
    x = total[:LANES].T
    y = total[LANES : 2 * LANES].T
    masses = total[2 * LANES :]
    for z in range(out_ref.shape[0]):
        out_ref[z, :8] = x[z * 8 : z * 8 + 8]
        out_ref[z, 8:16] = y[z * 8 : z * 8 + 8]
        out_ref[z, 16:] = masses


def grads_body(place_ref, e_ref, mate_e_ref, scale_ref, totals_ref, parts_ref, clips_ref, units_ref, inverse_ref,
               clip_ref, own_ref, other_ref, mass_ref):
    sums = jnp.sum(parts_ref[...], axis=0)
    mass_ref[...] = 1.0 / sums[16:]
    masses = mass_ref[...]
    totals = 1.0 / totals_ref[...]
    tiles = e_ref.shape[1] // LANES
    scale = scale_ref[...]
    acc = None
    for block in range(tiles // 2):
        pieces = []
        for half in range(2):
            tile = 2 * block + half
            lanes = slice(tile * LANES, (tile + 1) * LANES)
            mate = mate_e_ref[:, lanes]
            pieces.append(e_ref[:, lanes] * totals[tile : tile + 1, :] - mate * mate * scale * masses[tile : tile + 1, :])
        high, low = split(jnp.concatenate(pieces, axis=1))
        clip_high, clip_low = split(clips_ref[block * PAIR : (block + 1) * PAIR, :])
        term = dot(high, jnp.concatenate([clip_high, clip_low], axis=1))
        term = term[:, :LANES] + term[:, LANES:] + dot(low, clip_high)
        acc = term if acc is None else acc + term
    acc = acc * 10.0
    half = own_ref.shape[0]
    own_ref[...] = acc[:half]
    other_ref[...] = acc[half:]
    row = jnp.broadcast_to(mass_ref[pl.ds(place_ref[0], 1), :], (8, LANES))
    lane = lax.broadcasted_iota(jnp.int32, (8, LANES), 1)
    line = lax.broadcasted_iota(jnp.int32, (8, LANES), 0)
    own_mass = jnp.sum(jnp.where(lane == place_ref[1] * 8 + line, row, 0.0), axis=1, keepdims=True)
    grads = 10.0 * (sums[:8] - sums[8:16] * own_mass)
    units = units_ref[...]
    clip_ref[...] = inverse_ref[...] * (grads - units * jnp.sum(units * grads, axis=1, keepdims=True))


def local(embeddings, prototypes, partner):
    n_batch, n_proto = lax.axis_size("batch"), lax.axis_size("proto")
    n_chip = n_proto // 2
    rows, features = embeddings.shape
    own_protos = prototypes.shape[0]
    clips, protos = rows * n_batch * n_proto, own_protos * n_batch * n_proto
    here, tiles = n_chip * LANES, n_chip
    core = lax.axis_index("proto") % 2
    chip = lax.axis_index("proto") // 2
    layer = lax.axis_index("batch")
    same_core = [[2 * i + c for i in range(n_chip)] for c in range(2)]
    cores = [(i, i ^ 1) for i in range(n_proto)]
    smem = pl.BlockSpec(memory_space=pltpu.SMEM)
    vmem = pl.BlockSpec(memory_space=pltpu.VMEM)

    def swap(values):
        return lax.ppermute(values, "proto", cores)

    def over_chips(blocks):
        return lax.all_to_all(blocks, "proto", 0, 0, tiled=True, axis_index_groups=same_core)

    def over_layers(blocks):
        return lax.all_to_all(blocks, "batch", 0, 0, tiled=True)

    def summed(blocks):
        part = jnp.sum(over_chips(blocks), axis=0)
        return over_layers(jnp.broadcast_to(part[None], (n_batch,) + part.shape))

    units, inverse = unit_rows(embeddings)
    own_units, proto_inverse = unit_rows(prototypes)
    unit_protos = jnp.concatenate([own_units, swap(own_units)], axis=0)

    line, slot, z = partner % rows, (partner // rows) % n_proto, partner // (rows * n_proto)
    place = (slot % 2) * here + (slot // 2) * LANES + z * rows + line
    place = place.astype(jnp.float32).reshape(n_proto * rows // LANES, LANES)
    block = jnp.concatenate([units, jnp.pad(place, ((0, 8 - place.shape[0]), (0, 0)))], axis=0)
    column = over_layers(jnp.broadcast_to(block[None], (n_batch,) + block.shape))
    places = column[:, rows : rows + place.shape[0]].reshape(-1).astype(jnp.int32)
    places = jnp.where(places >= here, places - here, places + here) * core + places * (1 - core)
    column = column[:, :rows].reshape(LANES, features)
    own_clips = over_chips(jnp.broadcast_to(column[None], (n_chip, LANES, features))).reshape(here, features)
    other_clips = swap(own_clips)

    n_here = 2 * own_protos
    e, part, totals, x = call(
        scores_body, (f32(n_here, here), f32(n_here, LANES), f32(tiles, LANES), f32(tiles, features, LANES))
    )(unit_protos, own_clips)
    mate_e = call(
        mates_body,
        f32(n_here, here),
        in_specs=[smem, smem, vmem, vmem, vmem],
        scratch_shapes=[pltpu.VMEM((2 * here, features), jnp.float32), pltpu.VMEM((PAIR, features), jnp.float32)],
    )(places, core.reshape(1), unit_protos, own_clips, other_clips)

    cols = call(functools.partial(cols_body, float(clips)), f32(n_here, LANES))
    blocks = call(functools.partial(rows_body, float(protos)), f32(n_chip, 2 * tiles, LANES))(e, part, swap(part), totals)
    masses = summed(blocks)
    totals = jnp.sum(masses[:, tiles:], axis=0)
    part = cols(e, masses)
    blocks = call(functools.partial(rows_body, float(protos)), f32(n_chip, tiles, LANES))(e, part, swap(part))
    part = cols(e, summed(blocks))

    blocks, scale = call(
        functools.partial(mates_rows_body, float(protos)), (f32(n_chip, 2 * features + tiles, LANES), f32(n_here, LANES))
    )(mate_e, part, swap(part), unit_protos, x, totals)
    blocks = call(turn_body, f32(n_batch, 2 * rows + tiles, LANES))(over_chips(blocks))
    grad_embeddings, own_grads, other_grads = call(
        grads_body,
        (f32(rows, features), f32(own_protos, features), f32(own_protos, features)),
        in_specs=[smem] + [vmem] * 8,
        scratch_shapes=[pltpu.VMEM((tiles, LANES), jnp.float32)],
    )(jnp.stack([chip, layer]), e, mate_e, scale, totals, over_layers(blocks), own_clips, units, inverse)
    grads = own_grads + swap(other_grads)
    grad_prototypes = proto_inverse * (grads - own_units * jnp.sum(own_units * grads, axis=1, keepdims=True))
    return (grad_embeddings, grad_prototypes)


def solution(mesh):
    in_specs = (P(("batch", "proto"), None), P(("batch", "proto"), None), P("batch"))
    out_specs = (P(("batch", "proto"), None), P(("batch", "proto"), None))
    return jax.shard_map(local, mesh=mesh, in_specs=in_specs, out_specs=out_specs, check_vma=False)
```

time: 718 us -> 224 us (0.31); the launches traced: 708 us -> 223 us
  blocking collectives: 407 us -> 99 us
  waiting for transfers between devices: 224 us -> 32.4 us
  starting transfers between devices: 0.16 us -> 53.5 us
  other arithmetic: 28.7 us -> 5.47 us
  matrix products: 23.1 us -> 0 us
  Pallas kernels: 0 us -> 19.1 us
  between operations: 14.6 us -> 0.88 us
    psum x6 -> x0, blocking collectives: 358 us -> none  [the longest x3 237 us: local(): row_scale = 1.0 / (clip_count * lax.psum(row_part, 'proto'))]
    unnamed x5 -> x0, waiting for transfers between devices: 120 us -> none
    all_to_all x0 -> x5, blocking collectives: none -> 99 us  [the longest x3 52.8 us: over_chips(): lax.all_to_all(blocks, 'proto', 0, 0, tiled=True, axis_index_groups=same_...]
    reduce_scatter x1 -> x0, waiting for transfers between devices: 63.6 us -> none  [local(): lax.psum_scatter(proto_term, 'batch', scatter_dimension=0, tiled=True)]
    all_gather x2 -> x0, blocking collectives: 49.1 us -> none  [the longest x1 29.8 us: local(): clip_block = lax.all_gather(embeddings, 'proto', axis=0, tiled=True)]
    all_gather x2 -> x0, waiting for transfers between devices: 40.1 us -> none  [the longest x1 40.1 us: local(): full_protos = lax.all_gather(prototypes, 'batch', axis=0, tiled=True)]
    ppermute x0 -> x6, starting transfers between devices: none -> 38.3 us  [swap(): return lax.ppermute(values, 'proto', cores)]
    all_to_all x0 -> x3, waiting for transfers between devices: none -> 29.3 us  [the longest x2 24.7 us: over_layers(): return lax.all_to_all(blocks, 'batch', 0, 0, tiled=True)]
  transfers between devices with their start and end apart: 4 -> 9, of which waited for: 3 -> 6; matrix products, arithmetic and copies ran while one was open for 5% -> 1% of each run, Pallas kernels for 0% -> 4%
where the time goes in v1:
time: 224 us; the launch traced here: 223 us
  blocking collectives  99 us (44%)
  starting transfers between devices  53.5 us (24%)
  waiting for transfers between devices  32.4 us (14%)
  Pallas kernels  19.1 us (9%)
  local copies, waits for them, and re-layouts  12.6 us (6%)
  other arithmetic  5.47 us (2%)
    all_to_all x3, blocking collectives, over_chips(): lax.all_to_all(blocks, 'proto', 0, 0, tiled=True, axis_index_groups=same_...  52.8 us
    all_to_all x2, blocking collectives, over_layers(): return lax.all_to_all(blocks, 'batch', 0, 0, tiled=True)  46.2 us
    ppermute x6, starting transfers between devices, swap(): return lax.ppermute(values, 'proto', cores)  38.3 us
    all_to_all x2, waiting for transfers between devices, over_layers(): return lax.all_to_all(blocks, 'batch', 0, 0, tiled=True)  24.7 us
    unnamed x14, local copies, waits for them, and re-layouts  10.7 us
    all_to_all x2, starting transfers between devices, over_layers(): return lax.all_to_all(blocks, 'batch', 0, 0, tiled=True)  8.54 us
    pallas_call x1, Pallas kernels, local(): call(mates_body, f32(n_here, here), in_specs=[smem, smem, vmem, vmem, vme...  8.24 us
    all_to_all x1, starting transfers between devices, over_chips(): lax.all_to_all(blocks, 'proto', 0, 0, tiled=True, axis_index_groups=same_...  6.75 us
  transfers between devices with their start and end apart: 9, of which 6 were waited for; matrix products, arithmetic and copies ran while one was open for 1% of the time, Pallas kernels for 4%

profile of v1, /device:TPU:1, one launch (start us, length us, event | category | flops | bytes accessed | tf_op | source)
XLA Modules:
  0.0 222.9 jit_solution(312477747493222878)
XLA Ops:
  0.6 0.7 convert_bitcast_fusion
  1.3 0.8 multiply_reduce_fusion.2
  2.1 0.8 broadcast_multiply_fusion.1.units_ref
  2.9 27.5 %all_to_all.40 = f32[16,16,128]{2,1,0:T(8,128)S(1)} all-to-all(f32[16,16,128]{2,1,0:T(8,128)S(1)} %broadcast_in_dim.10), channel_id=1, replica_groups=mesh['batch'=16,'proto'=32] {'batch'}, dimensions={0} | all-to-all | bytes 262144 | tf_op jit(solution)/shard_map/all_to_all | solution.py:225
  30.5 1.1 broadcast_in_dim.12
  31.6 6.8 %all-to-all-start.1 = ((f32[16,128,128]{2,1,0:T(8,128)}), f32[16,128,128]{2,1,0:T(8,128)S(1)}, u32[]{:S(2)}, u32[]{:S(2)}) async-start(f32[16,128,128]{2,1,0:T(8,128)} %broadcast_in_dim.12), calls=%async_computation.1 | async-start | bytes 2097152 | tf_op jit(solution)/shard_map/all_to_all | solution.py:222
  38.3 1.0 multiply_reduce_fusion.1
  39.3 1.0 broadcast_multiply_fusion
  40.4 5.8 %collective-permute-start = (f32[256,128]{1,0:T(8,128)S(1)}, f32[256,128]{1,0:T(8,128)S(1)}, u32[]{:S(2)}, u32[]{:S(2)}) collective-permute-start(f32[256,128]{1,0:T(8,128)S(1)} %broadcast_multiply_fusion), channel_id=1, source_target_pairs={{0,1},{1,0},{2,3},{3,2},{4,5},{5,4},{6,7},{7,6},{8,9},{9,8},{10,11... | collective-permute-start | bytes 393224 | tf_op jit(solution)/shard_map/ppermute | solution.py:219
  46.2 1.0 collective-permute-done
  47.2 4.6 %all-to-all-done.1 = f32[16,128,128]{2,1,0:T(8,128)S(1)} async-done(((f32[16,128,128]{2,1,0:T(8,128)}), f32[16,128,128]{2,1,0:T(8,128)S(1)}, u32[]{:S(2)}, u32[]{:S(2)}) %all-to-all-start.1) | async-done | bytes 1048608 | tf_op jit(solution)/shard_map/all_to_all | solution.py:222
  51.8 3.9 %shard_map.50 = (f32[512,2048]{1,0:T(8,128)S(1)}, f32[512,128]{1,0:T(8,128)S(1)}, f32[16,128]{1,0:T(8,128)S(1)}, f32[16,128,128]{2,1,0:T(8,128)S(1)}) custom-call(f32[512,128]{1,0:T(8,128)S(1)} %pad_maximum_fusion.protos_ref, f32[2048,128]{1,0:T(8,128)S(1)} %bitcast.11), custom_call_target="tpu_custom_call" | custom-call | tf_op jit(solution)/shard_map/pallas_call | solution.py:247
  55.7 7.0 %collective-permute-start.2 = (f32[512,128]{1,0:T(8,128)S(1)}, f32[512,128]{1,0:T(8,128)S(1)}, u32[]{:S(2)}, u32[]{:S(2)}) collective-permute-start(f32[512,128]{1,0:T(8,128)S(1)} %get-tuple-element.12.own_ref), channel_id=1, source_target_pairs={{0,1},{1,0},{2,3},{3,2},{4,5},{5,4},{6,7},{7,6},{8,9},{9,8},{10,11... | collective-permute-start | bytes 786440 | tf_op jit(solution)/shard_map/ppermute | solution.py:219
  62.7 1.1 collective-permute-done.2.other_ref
  63.8 0.6 shard_map.52
  64.4 1.9 copy-done
  66.3 10.7 %all_to_all.41 = f32[16,32,128]{2,1,0:T(8,128)S(1)} all-to-all(f32[16,32,128]{2,1,0:T(8,128)S(1)} %shard_map.52), channel_id=1, replica_groups={{0,2,4,6,8,10,12,14,16,18,20,22,24,26,28,30},{1,3,5,7,9,11,13,15,17,19,..., dimensions={0} | all-to-all | bytes 524288 | tf_op jit(solution)/shard_map/all_to_all | solution.py:222
  77.1 18.7 %all_to_all.42.mass_ref = f32[16,32,128]{2,1,0:T(8,128)S(1)} all-to-all(f32[16,32,128]{2,1,0:T(8,128)S(1)} %broadcast_in_dim.13), channel_id=1, replica_groups=mesh['batch'=16,'proto'=32] {'batch'}, dimensions={0} | all-to-all | bytes 524288 | tf_op jit(solution)/shard_map/all_to_all | solution.py:225
  95.8 2.2 copy-done.1
  98.0 0.4 shard_map.53.own_ref
  98.4 8.9 %collective-permute-start.3 = (f32[512,128]{1,0:T(8,128)S(1)}, f32[512,128]{1,0:T(8,128)S(1)}, u32[]{:S(2)}, u32[]{:S(2)}) collective-permute-start(f32[512,128]{1,0:T(8,128)S(1)} %shard_map.53.own_ref), channel_id=1, source_target_pairs={{0,1},{1,0},{2,3},{3,2},{4,5},{5,4},{6,7},{7,6},{8,9},{9,8},{10,11... | collective-permute-start | bytes 786440 | tf_op jit(solution)/shard_map/ppermute | solution.py:219
  107.3 1.9 collective-permute-start.1
  109.3 0.0 collective-permute-done.3.other_ref
  109.3 0.5 shard_map.54
  109.8 9.4 %all_to_all.43 = f32[16,16,128]{2,1,0:T(8,128)S(1)} all-to-all(f32[16,16,128]{2,1,0:T(8,128)S(1)} %shard_map.54), channel_id=1, replica_groups={{0,2,4,6,8,10,12,14,16,18,20,22,24,26,28,30},{1,3,5,7,9,11,13,15,17,19,..., dimensions={0} | all-to-all | bytes 262144 | tf_op jit(solution)/shard_map/all_to_all | solution.py:222
  119.3 0.7 broadcast_in_dim.14
  119.9 5.0 %all-to-all-start.5 = ((f32[16,16,128]{2,1,0:T(8,128)}), f32[16,16,128]{2,1,0:T(8,128)S(1)}, u32[]{:S(2)}, u32[]{:S(2)}) async-start(f32[16,16,128]{2,1,0:T(8,128)} %broadcast_in_dim.14), calls=%async_computation.5 | async-start | bytes 262144 | tf_op jit(solution)/shard_map/all_to_all | solution.py:225
  125.0 12.0 %all-to-all-done.5.mass_ref = f32[16,16,128]{2,1,0:T(8,128)S(1)} async-done(((f32[16,16,128]{2,1,0:T(8,128)}), f32[16,16,128]{2,1,0:T(8,128)S(1)}, u32[]{:S(2)}, u32[]{:S(2)}) %all-to-all-start.5) | async-done | bytes 131104 | tf_op jit(solution)/shard_map/all_to_all | solution.py:225
  136.9 2.2 copy-done.2
  139.1 0.4 shard_map.55.own_ref
  139.6 6.1 %collective-permute-start.4 = (f32[512,128]{1,0:T(8,128)S(1)}, f32[512,128]{1,0:T(8,128)S(1)}, u32[]{:S(2)}, u32[]{:S(2)}) collective-permute-start(f32[512,128]{1,0:T(8,128)S(1)} %shard_map.55.own_ref), channel_id=1, source_target_pairs={{0,1},{1,0},{2,3},{3,2},{4,5},{5,4},{6,7},{7,6},{8,9},{9,8},{10,11... | collective-permute-start | bytes 786440 | tf_op jit(solution)/shard_map/ppermute | solution.py:219
  145.7 0.0 collective-permute-done.1.other_ref
  145.7 8.2 %shard_map.51.mate_e_ref = f32[512,2048]{1,0:T(8,128)S(1)} custom-call(s32[4096]{0:T(1024)S(1)} %bitcast.15, s32[1]{0:T(128)} %bitcast.6.core_ref, f32[512,128]{1,0:T(8,128)S(1)} %pad_maximum_fusion.protos_ref, f32[2048,128]{1,0:T(8,128)S(1)} %bitcast.13, f32[2048,128]{1,0:T(8,128)} %collective-permute-done.1.other_ref), custom_call_target="tpu_custom_call" | custom-call | tf_op jit(solution)/shard_map/pallas_call | solution.py:250
  154.0 0.0 collective-permute-done.4.other_ref
  154.0 1.5 shard_map.56
  155.5 32.6 %all_to_all.44.in_ref = f32[16,272,128]{2,1,0:T(8,128)S(1)} all-to-all(f32[16,272,128]{2,1,0:T(8,128)S(1)} %get-tuple-element.16), channel_id=1, replica_groups={{0,2,4,6,8,10,12,14,16,18,20,22,24,26,28,30},{1,3,5,7,9,11,13,15,17,19,..., dimensions={0} | all-to-all | bytes 4456448 | tf_op jit(solution)/shard_map/all_to_all | solution.py:222
  188.1 0.9 shard_map.57
  189.0 3.5 %all-to-all-start.7 = ((f32[16,32,128]{2,1,0:T(8,128)}), f32[16,32,128]{2,1,0:T(8,128)S(1)}, u32[]{:S(2)}, u32[]{:S(2)}) async-start(f32[16,32,128]{2,1,0:T(8,128)} %shard_map.57), calls=%async_computation.7 | async-start | bytes 524288 | tf_op jit(solution)/shard_map/all_to_all | solution.py:225
  192.5 0.1 copy.5.inverse_ref
  192.6 0.1 pad_add_fusion.place_ref
  192.7 12.7 %all-to-all-done.7.parts_ref = f32[16,32,128]{2,1,0:T(8,128)S(1)} async-done(((f32[16,32,128]{2,1,0:T(8,128)}), f32[16,32,128]{2,1,0:T(8,128)S(1)}, u32[]{:S(2)}, u32[]{:S(2)}) %all-to-all-start.7) | async-done | bytes 262176 | tf_op jit(solution)/shard_map/all_to_all | solution.py:225
  205.4 2.2 copy-done.3
  207.6 2.2 copy-done.5
  209.8 2.6 %shard_map.58 = (f32[8,128]{1,0:T(8,128)}, f32[256,128]{1,0:T(8,128)S(1)}, f32[256,128]{1,0:T(8,128)S(1)}) custom-call(s32[2]{0:T(128)S(1)} %pad_add_fusion.place_ref, f32[512,2048]{1,0:T(8,128)S(1)} %copy-done.3, f32[512,2048]{1,0:T(8,128)S(1)} %copy-done.5, f32[512,128]{1,0:T(8,128)S(1)} %get-tuple-element.15.scale_ref, ...), custom_call_target="tpu_custom_call" | custom-call | tf_op jit(solution)/shard_map/pallas_call | solution.py:269
  212.4 8.5 %collective-permute-start.5 = (f32[256,128]{1,0:T(8,128)S(1)}, f32[256,128]{1,0:T(8,128)S(1)}, u32[]{:S(2)}, u32[]{:S(2)}) collective-permute-start(f32[256,128]{1,0:T(8,128)S(1)} %get-tuple-element.19), channel_id=1, source_target_pairs={{0,1},{1,0},{2,3},{3,2},{4,5},{5,4},{6,7},{7,6},{8,9},{9,8},{10,11... | collective-permute-start | bytes 393224 | tf_op jit(solution)/shard_map/ppermute | solution.py:219
  220.9 1.0 collective-permute-done.5
  221.9 0.2 multiply_reduce_fusion
  222.1 0.8 subtract_multiply_fusion
  (20 shorter events, 0.2 us)
Async XLA Ops:
  31.6 20.2 %all-to-all-start.1 = ((f32[16,128,128]{2,1,0:T(8,128)}), f32[16,128,128]{2,1,0:T(8,128)S(1)}, u32[]{:S(2)}, u32[]{:S(2)}) async-start(f32[16,128,128]{2,1,0:T(8,128)} %broadcast_in_dim.12), calls=%async_computation.1 | async-start | bytes 2097152 | tf_op jit(solution)/shard_map/all_to_all | solution.py:222
  40.4 6.8 %collective-permute-start = (f32[256,128]{1,0:T(8,128)S(1)}, f32[256,128]{1,0:T(8,128)S(1)}, u32[]{:S(2)}, u32[]{:S(2)}) collective-permute-start(f32[256,128]{1,0:T(8,128)S(1)} %broadcast_multiply_fusion), channel_id=1, source_target_pairs={{0,1},{1,0},{2,3},{3,2},{4,5},{5,4},{6,7},{7,6},{8,9},{9,8},{10,11... | collective-permute-start | bytes 393224 | tf_op jit(solution)/shard_map/ppermute | solution.py:219
  55.7 8.1 %collective-permute-start.2 = (f32[512,128]{1,0:T(8,128)S(1)}, f32[512,128]{1,0:T(8,128)S(1)}, u32[]{:S(2)}, u32[]{:S(2)}) collective-permute-start(f32[512,128]{1,0:T(8,128)S(1)} %get-tuple-element.12.own_ref), channel_id=1, source_target_pairs={{0,1},{1,0},{2,3},{3,2},{4,5},{5,4},{6,7},{7,6},{8,9},{9,8},{10,11... | collective-permute-start | bytes 786440 | tf_op jit(solution)/shard_map/ppermute | solution.py:219
  64.4 1.9 copy-start
  95.8 2.2 copy-start.1
  98.4 10.9 %collective-permute-start.3 = (f32[512,128]{1,0:T(8,128)S(1)}, f32[512,128]{1,0:T(8,128)S(1)}, u32[]{:S(2)}, u32[]{:S(2)}) collective-permute-start(f32[512,128]{1,0:T(8,128)S(1)} %shard_map.53.own_ref), channel_id=1, source_target_pairs={{0,1},{1,0},{2,3},{3,2},{4,5},{5,4},{6,7},{7,6},{8,9},{9,8},{10,11... | collective-permute-start | bytes 786440 | tf_op jit(solution)/shard_map/ppermute | solution.py:219
  107.3 38.3 %collective-permute-start.1 = (f32[2048,128]{1,0:T(8,128)S(1)}, f32[2048,128]{1,0:T(8,128)}, u32[]{:S(2)}, u32[]{:S(2)}) collective-permute-start(f32[2048,128]{1,0:T(8,128)S(1)} %bitcast.12), channel_id=1, source_target_pairs={{0,1},{1,0},{2,3},{3,2},{4,5},{5,4},{6,7},{7,6},{8,9},{9,8},{10,11... | collective-permute-start | bytes 3145736 | tf_op jit(solution)/shard_map/ppermute | solution.py:219
  119.9 17.0 %all-to-all-start.5 = ((f32[16,16,128]{2,1,0:T(8,128)}), f32[16,16,128]{2,1,0:T(8,128)S(1)}, u32[]{:S(2)}, u32[]{:S(2)}) async-start(f32[16,16,128]{2,1,0:T(8,128)} %broadcast_in_dim.14), calls=%async_computation.5 | async-start | bytes 262144 | tf_op jit(solution)/shard_map/all_to_all | solution.py:225
  136.9 2.2 copy-start.2
  139.6 14.4 %collective-permute-start.4 = (f32[512,128]{1,0:T(8,128)S(1)}, f32[512,128]{1,0:T(8,128)S(1)}, u32[]{:S(2)}, u32[]{:S(2)}) collective-permute-start(f32[512,128]{1,0:T(8,128)S(1)} %shard_map.55.own_ref), channel_id=1, source_target_pairs={{0,1},{1,0},{2,3},{3,2},{4,5},{5,4},{6,7},{7,6},{8,9},{9,8},{10,11... | collective-permute-start | bytes 786440 | tf_op jit(solution)/shard_map/ppermute | solution.py:219
  153.9 34.2 %copy-start.4 = (f32[512,2048]{1,0:T(8,128)}, f32[512,2048]{1,0:T(8,128)S(1)}, u32[]{:S(2)}) copy-start(f32[512,2048]{1,0:T(8,128)S(1)} %shard_map.51.mate_e_ref) | copy-start | bytes 12582916
  189.0 16.5 %all-to-all-start.7 = ((f32[16,32,128]{2,1,0:T(8,128)}), f32[16,32,128]{2,1,0:T(8,128)S(1)}, u32[]{:S(2)}, u32[]{:S(2)}) async-start(f32[16,32,128]{2,1,0:T(8,128)} %shard_map.57), calls=%async_computation.7 | async-start | bytes 524288 | tf_op jit(solution)/shard_map/all_to_all | solution.py:225
  205.4 2.2 copy-start.3
  207.6 2.2 copy-start.5
  209.8 12.1 %copy-start.6 = (f32[256,128]{1,0:T(8,128)S(1)}, f32[256,128]{1,0:T(8,128)}, u32[]{:S(2)}) copy-start(f32[256,128]{1,0:T(8,128)} %param.4) | copy-start | bytes 393220
  212.4 9.5 %collective-permute-start.5 = (f32[256,128]{1,0:T(8,128)S(1)}, f32[256,128]{1,0:T(8,128)S(1)}, u32[]{:S(2)}, u32[]{:S(2)}) collective-permute-start(f32[256,128]{1,0:T(8,128)S(1)} %get-tuple-element.19), channel_id=1, source_target_pairs={{0,1},{1,0},{2,3},{3,2},{4,5},{5,4},{6,7},{7,6},{8,9},{9,8},{10,11... | collective-permute-start | bytes 393224 | tf_op jit(solution)/shard_map/ppermute | solution.py:219

commit v2 on v1

v2 whole, which is shorter than its diff:
```python
import functools

import jax
import jax.numpy as jnp
from jax import lax
from jax.experimental import pallas as pl
from jax.experimental.pallas import tpu as pltpu
from jax.sharding import PartitionSpec as P

LANES = 128
PAIR = 2 * LANES
CHUNK = 64
VMEM_BYTES = 24 * 1024 * 1024


def inverse_norms(values):
    return 1.0 / jnp.sqrt(jnp.sum(values * values, axis=1, keepdims=True) + 1e-06)


def finish_rows(values, grads):
    inverse = inverse_norms(values)
    units = values * inverse
    return inverse * (grads - units * jnp.sum(units * grads, axis=1, keepdims=True))


def split(values):
    high = values.astype(jnp.bfloat16)
    low = (values - high.astype(jnp.float32)).astype(jnp.bfloat16)
    return high, low


def dot(left, right):
    return jnp.dot(left, right, preferred_element_type=jnp.float32)


def dot_rows(left, right):
    return lax.dot_general(left, right, (((1,), (1,)), ((), ())), preferred_element_type=jnp.float32)


def call(body, out_shape, **kwargs):
    return pl.pallas_call(
        body, out_shape=out_shape, compiler_params=pltpu.CompilerParams(vmem_limit_bytes=VMEM_BYTES), **kwargs
    )


def f32(*shape):
    return jax.ShapeDtypeStruct(shape, jnp.float32)


def exponents(proto_pair, clips):
    high, low = split(clips)
    scores = dot_rows(proto_pair, jnp.concatenate([high, high], axis=1))
    scores = scores + dot_rows(proto_pair, jnp.concatenate([low, low], axis=1))
    return jnp.exp(scores * 10.0)


def scores_body(protos_ref, clips_ref, e_ref, part_ref, total_ref, x_ref):
    protos = protos_ref[...]
    pair = jnp.concatenate(split(protos), axis=1)
    turned_high, turned_low = split(protos.T)
    turned = jnp.concatenate([turned_high, turned_low], axis=0)
    for block in range(clips_ref.shape[0] // PAIR):
        cols = slice(block * PAIR, (block + 1) * PAIR)
        e = exponents(pair, clips_ref[cols, :])
        e_ref[:, cols] = e
        kernel = e * e
        both = kernel[:, :LANES] + kernel[:, LANES:]
        part_ref[...] = both if block == 0 else part_ref[...] + both
        totals = jnp.sum(e, axis=0, keepdims=True)
        high, low = split(e)
        x = dot(turned, high)
        x = x[:LANES] + x[LANES:] + dot(turned_high, low)
        for half in range(2):
            total_ref[2 * block + half : 2 * block + half + 1, :] = totals[:, half * LANES : (half + 1) * LANES]
            x_ref[2 * block + half] = x[:, half * LANES : (half + 1) * LANES]


def mates_body(index_ref, spot_ref, protos_ref, own_ref, other_ref, e_ref, table_ref, mate_ref):
    rows = own_ref.shape[0]
    table_ref[:rows] = own_ref[...]
    table_ref[rows:] = other_ref[...]
    pair = jnp.concatenate(split(protos_ref[...]), axis=1)
    tiles = rows // LANES
    first = spot_ref[2] * 8
    for block in range(rows // PAIR):
        slot = block % 2
        for half in range(2):
            for z in range(LANES // 8):
                start = first + (z * tiles + 2 * block + half) * 16
                for r in range(8):
                    mate_ref[slot, half * LANES + z * 8 + r : half * LANES + z * 8 + r + 1, :] = table_ref[
                        pl.ds(index_ref[start + r], 1), :
                    ]
        e_ref[:, block * PAIR : (block + 1) * PAIR] = exponents(pair, mate_ref[slot])


def column_scale(own_ref, other_ref, protos):
    half = own_ref.shape[0] // 2
    part = jnp.concatenate([own_ref[:half] + other_ref[half:], own_ref[half:] + other_ref[:half]], axis=0)
    return 1.0 / (protos * jnp.sum(part, axis=1, keepdims=True))


def row_mass(e_ref, scale, tile):
    e = e_ref[:, tile * LANES : (tile + 1) * LANES]
    return jnp.sum(e * e * scale, axis=0, keepdims=True)


def units_body(in_ref, out_ref):
    values = in_ref[...]
    out_ref[...] = values * inverse_norms(values)


def send_body(n_proto, embeddings_ref, partner_ref, out_ref):
    values = embeddings_ref[...]
    partner = partner_ref[...]
    rows = values.shape[0]
    line = partner & (rows - 1)
    slot = (partner // rows) & (n_proto - 1)
    place = (slot & 1) * (n_proto // 2) + (slot >> 1)
    place = place * LANES + partner // (rows * n_proto) * rows + line
    units = values * inverse_norms(values)
    for layer in range(out_ref.shape[0]):
        out_ref[layer, :rows] = units
        out_ref[layer, rows : rows + place.shape[0]] = place.astype(jnp.float32)
        out_ref[layer, rows + place.shape[0] :] = jnp.zeros((8 - place.shape[0], LANES), jnp.float32)


def column_body(spot_ref, in_ref, out_ref, places_ref):
    n_layers, _, _ = in_ref.shape
    per_layer = places_ref.shape[1]
    for layer in range(n_layers):
        units = in_ref[layer, :8]
        for block in range(out_ref.shape[0]):
            out_ref[block, layer * 8 : layer * 8 + 8] = units
    here = out_ref.shape[0] * LANES
    places = in_ref[:, 8 : 8 + per_layer, :].astype(jnp.int32)
    moved = jnp.where(places >= here, places - here, places + here)
    places_ref[...] = jnp.where(spot_ref[2] > 0, moved, places)


def masses_of(e_ref, scale):
    tiles = e_ref.shape[1] // LANES
    return jnp.concatenate([row_mass(e_ref, scale, tile) for tile in range(tiles)], axis=0)


def rows_first_body(protos, e_ref, own_ref, other_ref, totals_ref, out_ref):
    tiles = e_ref.shape[1] // LANES
    scale = jnp.broadcast_to(column_scale(own_ref, other_ref, protos), own_ref.shape)
    masses = masses_of(e_ref, scale)
    for block in range(tiles):
        out_ref[block, :tiles] = masses
        out_ref[block, tiles:] = jnp.broadcast_to(totals_ref[block : block + 1, :], (8, LANES))


def spread_first_body(in_ref, out_ref):
    tiles = in_ref.shape[0]
    total = jnp.sum(in_ref[...], axis=0)
    size = tiles + 1
    for layer in range(out_ref.shape[0] // size):
        out_ref[layer * size : (layer + 1) * size] = total[:size]


def weigh_columns(e_ref, scale, part_ref):
    tiles = e_ref.shape[1] // LANES
    for start in range(0, e_ref.shape[0], CHUNK):
        rows = slice(start, start + CHUNK)
        total = None
        for tile in range(tiles):
            e = e_ref[rows, tile * LANES : (tile + 1) * LANES]
            term = e * e * scale[tile : tile + 1, :]
            total = term if total is None else total + term
        part_ref[rows, :] = total


def cols_first_body(clips, e_ref, in_ref, part_ref, own_total_ref):
    tiles = e_ref.shape[1] // LANES
    size = tiles + 1
    total = in_ref[:size]
    for layer in range(1, in_ref.shape[0] // size):
        total = total + in_ref[layer * size : (layer + 1) * size]
    own_total_ref[...] = jnp.broadcast_to(total[tiles:], (8, LANES))
    weigh_columns(e_ref, 1.0 / (clips * total[:tiles]), part_ref)


def rows_second_body(protos, e_ref, own_ref, other_ref, x_ref, own_total_ref, out_ref):
    tiles = e_ref.shape[1] // LANES
    scale = jnp.broadcast_to(column_scale(own_ref, other_ref, protos), own_ref.shape)
    masses = masses_of(e_ref, scale)
    for block in range(tiles):
        out_ref[block, :tiles] = masses
        out_ref[block, tiles : tiles + LANES] = x_ref[block]
        out_ref[block, tiles + LANES :] = own_total_ref[...]


def spread_second_body(in_ref, out_ref, x_ref, totals_ref):
    tiles = in_ref.shape[0]
    masses = jnp.sum(in_ref[:, :tiles, :], axis=0)
    for layer in range(out_ref.shape[0] // tiles):
        out_ref[layer * tiles : (layer + 1) * tiles] = masses
    x_ref[...] = jnp.sum(in_ref[:, tiles : tiles + LANES, :], axis=0)
    for block in range(tiles):
        totals_ref[block : block + 1, :] = in_ref[block, tiles + LANES : tiles + LANES + 1, :]


def cols_second_body(clips, e_ref, in_ref, part_ref):
    tiles = e_ref.shape[1] // LANES
    total = in_ref[:tiles]
    for layer in range(1, in_ref.shape[0] // tiles):
        total = total + in_ref[layer * tiles : (layer + 1) * tiles]
    weigh_columns(e_ref, 1.0 / (clips * total), part_ref)


def mates_rows_body(protos, mate_e_ref, own_ref, other_ref, protos_ref, out_ref, scale_ref):
    scale = jnp.broadcast_to(column_scale(own_ref, other_ref, protos), own_ref.shape)
    scale_ref[...] = scale
    wide = jnp.concatenate([scale, scale], axis=1)
    turned_high, turned_low = split(protos_ref[...].T)
    turned = jnp.concatenate([turned_high, turned_low], axis=0)
    tiles = mate_e_ref.shape[1] // LANES
    masses = []
    for block in range(tiles // 2):
        e = mate_e_ref[:, block * PAIR : (block + 1) * PAIR]
        kernel = e * e * wide
        mass = jnp.sum(kernel, axis=0, keepdims=True)
        high, low = split(kernel)
        y = dot(turned, high)
        y = y[:LANES] + y[LANES:] + dot(turned_high, low)
        for half in range(2):
            lanes = slice(half * LANES, (half + 1) * LANES)
            masses.append(mass[:, lanes])
            out_ref[2 * block + half, :LANES] = y[:, lanes]
    masses = jnp.concatenate(masses, axis=0)
    for tile in range(tiles):
        out_ref[tile, LANES:] = masses


def turn_body(in_ref, x_ref, own_total_ref, out_ref):
    tiles = in_ref.shape[0]
    size = 16 + tiles
    total = jnp.sum(in_ref[...], axis=0)
    x = (x_ref[...] / own_total_ref[0:1, :]).T
    y = total[:LANES].T
    masses = total[LANES:]
    for layer in range(out_ref.shape[0] // size):
        base = layer * size
        out_ref[base : base + 8] = x[layer * 8 : layer * 8 + 8]
        out_ref[base + 8 : base + 16] = y[layer * 8 : layer * 8 + 8]
        out_ref[base + 16 : base + size] = masses


def grads_body(spot_ref, e_ref, mate_e_ref, scale_ref, totals_ref, in_ref, clips_ref, embeddings_ref,
               clip_ref, own_ref, other_ref, mass_ref):
    tiles = e_ref.shape[1] // LANES
    size = 16 + tiles
    sums = in_ref[:size]
    for layer in range(1, in_ref.shape[0] // size):
        sums = sums + in_ref[layer * size : (layer + 1) * size]
    mass_ref[...] = 1.0 / sums[16:]
    masses = mass_ref[...]
    totals = 1.0 / totals_ref[...]
    scale = scale_ref[...]
    acc = None
    for block in range(tiles // 2):
        pieces = []
        for half in range(2):
            tile = 2 * block + half
            lanes = slice(tile * LANES, (tile + 1) * LANES)
            mate = mate_e_ref[:, lanes]
            pieces.append(e_ref[:, lanes] * totals[tile : tile + 1, :] - mate * mate * scale * masses[tile : tile + 1, :])
        high, low = split(jnp.concatenate(pieces, axis=1))
        clip_high, clip_low = split(clips_ref[block * PAIR : (block + 1) * PAIR, :])
        term = dot(high, jnp.concatenate([clip_high, clip_low], axis=1))
        term = term[:, :LANES] + term[:, LANES:] + dot(low, clip_high)
        acc = term if acc is None else acc + term
    acc = acc * 10.0
    half = own_ref.shape[0]
    own_ref[...] = acc[:half]
    other_ref[...] = acc[half:]
    row = jnp.broadcast_to(mass_ref[pl.ds(spot_ref[0], 1), :], (8, LANES))
    lane = lax.broadcasted_iota(jnp.int32, (8, LANES), 1)
    line = lax.broadcasted_iota(jnp.int32, (8, LANES), 0)
    own_mass = jnp.sum(jnp.where(lane == spot_ref[1] * 8 + line, row, 0.0), axis=1, keepdims=True)
    clip_ref[...] = finish_rows(embeddings_ref[...], 10.0 * (sums[:8] - sums[8:16] * own_mass))


def finish_body(protos_ref, own_ref, other_ref, out_ref):
    out_ref[...] = finish_rows(protos_ref[...], own_ref[...] + other_ref[...])


def local(embeddings, prototypes, partner):
    n_batch, n_proto = lax.axis_size("batch"), lax.axis_size("proto")
    tiles = n_proto // 2
    rows, features = embeddings.shape
    own_protos = prototypes.shape[0]
    clips, protos = float(rows * n_batch * n_proto), float(own_protos * n_batch * n_proto)
    here, n_here = tiles * LANES, 2 * own_protos
    where = lax.axis_index("proto")
    same_core = [[2 * i + c for i in range(tiles)] for c in range(2)]
    cores = [(i, i ^ 1) for i in range(n_proto)]
    smem = pl.BlockSpec(memory_space=pltpu.SMEM)
    vmem = pl.BlockSpec(memory_space=pltpu.VMEM)

    def swap(values):
        return lax.ppermute(values, "proto", cores)

    def over_chips(blocks):
        return lax.all_to_all(blocks, "proto", 0, 0, tiled=True, axis_index_groups=same_core)

    def over_layers(lines):
        blocks = lax.all_to_all(lines.reshape(n_batch, 1, -1), "batch", 0, 0, tiled=True)
        return blocks.reshape(lines.shape)

    spot = jnp.stack([where >> 1, lax.axis_index("batch"), where & 1])
    partner = partner.reshape(-1, LANES)
    sent = call(functools.partial(send_body, n_proto), f32(n_batch, rows + 8, LANES))(embeddings, partner)
    sent, held, spot = lax.optimization_barrier((sent, prototypes, spot))
    column = lax.all_to_all(sent, "batch", 0, 0, tiled=True)
    own_units = call(units_body, f32(own_protos, features))(held)
    unit_protos = jnp.concatenate([own_units, swap(own_units)], axis=0)
    column, unit_protos = lax.optimization_barrier((column, unit_protos))
    blocks, places = call(
        column_body,
        (f32(tiles, LANES, features), jax.ShapeDtypeStruct((n_batch, partner.shape[0], LANES), jnp.int32)),
        in_specs=[smem, vmem],
    )(spot, column)
    own_clips = over_chips(blocks).reshape(here, features)
    other_clips = swap(own_clips)

    e, part, totals, x = call(
        scores_body, (f32(n_here, here), f32(n_here, LANES), f32(tiles, LANES), f32(tiles, features, LANES))
    )(unit_protos, own_clips)
    part, other_clips = lax.optimization_barrier((part, other_clips))
    mate_e = call(
        mates_body,
        f32(n_here, here),
        in_specs=[smem, smem, vmem, vmem, vmem],
        scratch_shapes=[pltpu.VMEM((2 * here, features), jnp.float32), pltpu.VMEM((2, PAIR, features), jnp.float32)],
    )(places.reshape(-1), spot, unit_protos, own_clips, other_clips)

    blocks = call(functools.partial(rows_first_body, protos), f32(tiles, tiles + 8, LANES))(e, part, swap(part), totals)
    lines = call(spread_first_body, f32(n_batch * (tiles + 1), LANES))(over_chips(blocks))
    part, own_total = call(functools.partial(cols_first_body, clips), (f32(n_here, LANES), f32(8, LANES)))(
        e, over_layers(lines)
    )
    blocks = call(functools.partial(rows_second_body, protos), f32(tiles, tiles + LANES + 8, LANES))(
        e, part, swap(part), x, own_total
    )
    lines, x, totals = call(
        spread_second_body, (f32(n_batch * tiles, LANES), f32(features, LANES), f32(tiles, LANES))
    )(over_chips(blocks))
    part = call(functools.partial(cols_second_body, clips), f32(n_here, LANES))(e, over_layers(lines))
    blocks, scale = call(
        functools.partial(mates_rows_body, protos), (f32(tiles, features + tiles, LANES), f32(n_here, LANES))
    )(mate_e, part, swap(part), unit_protos)
    lines = call(turn_body, f32(n_batch * (16 + tiles), LANES))(over_chips(blocks), x, own_total)
    grad_embeddings, own_grads, other_grads = call(
        grads_body,
        (f32(rows, features), f32(own_protos, features), f32(own_protos, features)),
        in_specs=[smem] + [vmem] * 7,
        scratch_shapes=[pltpu.VMEM((tiles, LANES), jnp.float32)],
    )(spot, e, mate_e, scale, totals, over_layers(lines), own_clips, embeddings)
    grad_prototypes = call(finish_body, f32(own_protos, features))(prototypes, own_grads, swap(other_grads))
    return (grad_embeddings, grad_prototypes)


def solution(mesh):
    in_specs = (P(("batch", "proto"), None), P(("batch", "proto"), None), P("batch"))
    out_specs = (P(("batch", "proto"), None), P(("batch", "proto"), None))
    return jax.shard_map(local, mesh=mesh, in_specs=in_specs, out_specs=out_specs, check_vma=False)
```

time: 224 us -> 201 us (0.90)
  blocking collectives: 99 us -> 123 us
  waiting for transfers between devices: 32.4 us -> 11.7 us
  local copies, waits for them, and re-layouts: 12.6 us -> 2.27 us
  starting transfers between devices: 53.5 us -> 47.2 us
  other arithmetic: 5.47 us -> 0.09 us
  Pallas kernels: 19.1 us -> 16 us
    all_to_all x3 -> x1, waiting for transfers between devices: 29.3 us -> 7.1 us  [local(): column = lax.all_to_all(sent, 'batch', 0, 0, tiled=True)]
    all_to_all x3 -> x4, blocking collectives: 52.8 us -> 73.1 us  [over_chips(): lax.all_to_all(blocks, 'proto', 0, 0, tiled=True, axis_index_groups=same_...]
    unnamed x14 -> x10, local copies, waits for them, and re-layouts: 10.7 us -> 2.27 us
    ppermute x6, starting transfers between devices: 38.3 us -> 31.4 us  [swap(): return lax.ppermute(values, 'proto', cores)]
    pallas_call x1, Pallas kernels: 8.24 us -> 3.6 us  [local(): call(mates_body, f32(n_here, here), in_specs=[smem, smem, vmem, vmem, vme...]
    all_to_all x2 -> x3, blocking collectives: 46.2 us -> 49.5 us  [over_layers(): lax.all_to_all(lines.reshape(n_batch, 1, -1), 'batch', 0, 0, tiled=True)]
    mul x3 -> x0, other arithmetic: 2.57 us -> none  [the longest x2 1.76 us: unit_rows(): return (values * inverse, inverse)]
    pallas_call x6 -> x12, Pallas kernels: 4.37 us -> 5.99 us  [the longest x1 1.36 us: local(): call(functools.partial(mates_rows_body, protos), (f32(tiles, features + t...]
  transfers between devices with their start and end apart: 9 -> 7, of which waited for: 6 -> 5; matrix products, arithmetic and copies ran while one was open for 1% -> 0% of each run, Pallas kernels for 4% -> 4%
where the time goes in v2:
time: 201 us
  blocking collectives  123 us (61%)
  starting transfers between devices  47.2 us (23%)
  Pallas kernels  16 us (8%)
  waiting for transfers between devices  11.7 us (6%)
  local copies, waits for them, and re-layouts  2.27 us (1%)
    all_to_all x4, blocking collectives, over_chips(): lax.all_to_all(blocks, 'proto', 0, 0, tiled=True, axis_index_groups=same_...  73.1 us
    all_to_all x3, blocking collectives, over_layers(): lax.all_to_all(lines.reshape(n_batch, 1, -1), 'batch', 0, 0, tiled=True)  49.5 us
    ppermute x6, starting transfers between devices, swap(): return lax.ppermute(values, 'proto', cores)  31.4 us
    all_to_all x1, starting transfers between devices, local(): column = lax.all_to_all(sent, 'batch', 0, 0, tiled=True)  15.7 us
    all_to_all x1, waiting for transfers between devices, local(): column = lax.all_to_all(sent, 'batch', 0, 0, tiled=True)  7.1 us
    ppermute x6, waiting for transfers between devices, swap(): return lax.ppermute(values, 'proto', cores)  4.57 us
  transfers between devices with their start and end apart: 7, of which 5 were waited for; matrix products, arithmetic and copies ran while one was open for 0% of the time, Pallas kernels for 4%

profile of v2, /device:TPU:1, one launch (start us, length us, event | category | flops | bytes accessed | tf_op | source)
XLA Modules:
  0.0 200.6 jit_solution(7626357198281597926)
XLA Ops:
  0.6 0.0 copy-start.2
  0.6 0.7 copy-done.2
  1.3 0.0 copy-start.4
  1.3 0.7 copy-done.4
  2.0 0.8 shard_map.50
  2.8 0.1 pad_add_fusion.spot_ref
  2.8 15.7 %all-to-all-start = ((f32[16,16,128]{2,1,0:T(8,128)}), f32[16,16,128]{2,1,0:T(8,128)S(1)}, u32[]{:S(2)}, u32[]{:S(2)}) async-start(f32[16,16,128]{2,1,0:T(8,128)} %shard_map.50), calls=%async_computation | async-start | bytes 262144 | tf_op jit(solution)/shard_map/all_to_all | solution.py:317
  18.6 0.0 copy-start
  18.6 0.9 copy-done
  19.5 0.1 shard_map.51
  19.6 2.9 %collective-permute-start = (f32[256,128]{1,0:T(8,128)S(1)}, f32[256,128]{1,0:T(8,128)S(1)}, u32[]{:S(2)}, u32[]{:S(2)}) collective-permute-start(f32[256,128]{1,0:T(8,128)S(1)} %shard_map.51), channel_id=1, source_target_pairs={{0,1},{1,0},{2,3},{3,2},{4,5},{5,4},{6,7},{7,6},{8,9},{9,8},{10,11... | collective-permute-start | bytes 393224 | tf_op jit(solution)/shard_map/ppermute | solution.py:304
  22.5 1.0 collective-permute-done
  23.5 7.1 %all-to-all-done.in_ref = f32[16,16,128]{2,1,0:T(8,128)S(1)} async-done(((f32[16,16,128]{2,1,0:T(8,128)}), f32[16,16,128]{2,1,0:T(8,128)S(1)}, u32[]{:S(2)}, u32[]{:S(2)}) %all-to-all-start) | async-done | bytes 131104 | tf_op jit(solution)/shard_map/all_to_all | solution.py:317
  30.6 0.6 shard_map.52
  31.2 19.9 %all_to_all.40 = f32[16,128,128]{2,1,0:T(8,128)S(1)} all-to-all(f32[16,128,128]{2,1,0:T(8,128)S(1)} %get-tuple-element.30), channel_id=1, replica_groups={{0,2,4,6,8,10,12,14,16,18,20,22,24,26,28,30},{1,3,5,7,9,11,13,15,17,19,..., dimensions={0} | all-to-all | bytes 2097152 | tf_op jit(solution)/shard_map/all_to_all | solution.py:307
  51.2 6.7 %collective-permute-start.1 = (f32[2048,128]{1,0:T(8,128)S(1)}, f32[2048,128]{1,0:T(8,128)S(1)}, u32[]{:S(2)}, u32[]{:S(2)}) collective-permute-start(f32[2048,128]{1,0:T(8,128)S(1)} %bitcast.12), channel_id=1, source_target_pairs={{0,1},{1,0},{2,3},{3,2},{4,5},{5,4},{6,7},{7,6},{8,9},{9,8},{10,11... | collective-permute-start | bytes 3145736 | tf_op jit(solution)/shard_map/ppermute | solution.py:304
  57.9 3.8 %shard_map.53 = (f32[512,2048]{1,0:T(8,128)S(1)}, f32[512,128]{1,0:T(8,128)S(1)}, f32[16,128]{1,0:T(8,128)S(1)}, f32[16,128,128]{2,1,0:T(8,128)S(1)}) custom-call(f32[512,128]{1,0:T(8,128)S(1)} %pad_maximum_fusion.protos_ref, f32[2048,128]{1,0:T(8,128)S(1)} %bitcast.13), custom_call_target="tpu_custom_call" | custom-call | tf_op jit(solution)/shard_map/pallas_call | solution.py:329
  61.7 0.0 collective-permute-done.1.other_ref
  61.7 1.9 collective-permute-start.2
  63.7 1.5 collective-permute-done.2.other_ref
  65.2 0.5 shard_map.55
  65.7 10.3 %all_to_all.41.in_ref = f32[16,24,128]{2,1,0:T(8,128)S(1)} all-to-all(f32[16,24,128]{2,1,0:T(8,128)S(1)} %shard_map.55), channel_id=1, replica_groups={{0,2,4,6,8,10,12,14,16,18,20,22,24,26,28,30},{1,3,5,7,9,11,13,15,17,19,..., dimensions={0} | all-to-all | bytes 393216 | tf_op jit(solution)/shard_map/all_to_all | solution.py:307
  76.0 17.7 %all_to_all.42 = f32[16,1,2176]{2,1,0:T(1,128)S(1)} all-to-all(f32[16,1,2176]{2,1,0:T(1,128)S(1)} %bitcast.19), channel_id=1, replica_groups=mesh['batch'=16,'proto'=32] {'batch'}, dimensions={0} | all-to-all | bytes 278528 | tf_op jit(solution)/shard_map/all_to_all | solution.py:310
  93.8 0.4 shard_map.57
  94.2 5.8 %collective-permute-start.3 = (f32[512,128]{1,0:T(8,128)S(1)}, f32[512,128]{1,0:T(8,128)S(1)}, u32[]{:S(2)}, u32[]{:S(2)}) collective-permute-start(f32[512,128]{1,0:T(8,128)S(1)} %get-tuple-element.37.own_ref), channel_id=1, source_target_pairs={{0,1},{1,0},{2,3},{3,2},{4,5},{5,4},{6,7},{7,6},{8,9},{9,8},{10,11... | collective-permute-start | bytes 786440 | tf_op jit(solution)/shard_map/ppermute | solution.py:304
  100.0 1.1 collective-permute-done.3.other_ref
  101.1 0.6 shard_map.58
  101.7 21.5 %all_to_all.43.in_ref = f32[16,152,128]{2,1,0:T(8,128)S(1)} all-to-all(f32[16,152,128]{2,1,0:T(8,128)S(1)} %shard_map.58), channel_id=1, replica_groups={{0,2,4,6,8,10,12,14,16,18,20,22,24,26,28,30},{1,3,5,7,9,11,13,15,17,19,..., dimensions={0} | all-to-all | bytes 2490368 | tf_op jit(solution)/shard_map/all_to_all | solution.py:307
  123.2 0.1 shard_map.59
  123.2 15.4 %all_to_all.44 = f32[16,1,2048]{2,1,0:T(1,128)S(1)} all-to-all(f32[16,1,2048]{2,1,0:T(1,128)S(1)} %bitcast.21), channel_id=1, replica_groups=mesh['batch'=16,'proto'=32] {'batch'}, dimensions={0} | all-to-all | bytes 262144 | tf_op jit(solution)/shard_map/all_to_all | solution.py:310
  138.7 0.4 shard_map.60.own_ref
  139.1 5.5 %collective-permute-start.4 = (f32[512,128]{1,0:T(8,128)S(1)}, f32[512,128]{1,0:T(8,128)S(1)}, u32[]{:S(2)}, u32[]{:S(2)}) collective-permute-start(f32[512,128]{1,0:T(8,128)S(1)} %shard_map.60.own_ref), channel_id=1, source_target_pairs={{0,1},{1,0},{2,3},{3,2},{4,5},{5,4},{6,7},{7,6},{8,9},{9,8},{10,11... | collective-permute-start | bytes 786440 | tf_op jit(solution)/shard_map/ppermute | solution.py:304
  144.6 3.6 %shard_map.54.mate_e_ref = f32[512,2048]{1,0:T(8,128)S(1)} custom-call(s32[4096]{0:T(1024)S(1)} %bitcast.22, s32[3]{0:T(128)S(1)} %pad_add_fusion.spot_ref, f32[512,128]{1,0:T(8,128)S(1)} %pad_maximum_fusion.protos_ref, f32[2048,128]{1,0:T(8,128)S(1)} %bitcast.14, f32[2048,128]{1,0:T(8,128)S(1)} %collective-permute-done.1.other_ref), custom_call_target="tpu_custom_call" | custom-call | tf_op jit(solution)/shard_map/pallas_call | solution.py:333
  148.2 0.0 collective-permute-done.4.other_ref
  148.2 1.4 shard_map.61
  149.6 21.4 %all_to_all.45.in_ref = f32[16,144,128]{2,1,0:T(8,128)S(1)} all-to-all(f32[16,144,128]{2,1,0:T(8,128)S(1)} %get-tuple-element.43), channel_id=1, replica_groups={{0,2,4,6,8,10,12,14,16,18,20,22,24,26,28,30},{1,3,5,7,9,11,13,15,17,19,..., dimensions={0} | all-to-all | bytes 2359296 | tf_op jit(solution)/shard_map/all_to_all | solution.py:307
  171.0 0.0 copy-start.3
  171.0 0.1 shard_map.62
  171.1 16.4 %all_to_all.46 = f32[16,1,4096]{2,1,0:T(1,128)S(1)} all-to-all(f32[16,1,4096]{2,1,0:T(1,128)S(1)} %bitcast.17), channel_id=1, replica_groups=mesh['batch'=16,'proto'=32] {'batch'}, dimensions={0} | all-to-all | bytes 524288 | tf_op jit(solution)/shard_map/all_to_all | solution.py:310
  187.5 0.0 copy-done.3
  187.5 0.0 copy-start.1
  187.5 2.6 %shard_map.63 = (f32[8,128]{1,0:T(8,128)}, f32[256,128]{1,0:T(8,128)S(1)}, f32[256,128]{1,0:T(8,128)S(1)}) custom-call(s32[3]{0:T(128)S(1)} %pad_add_fusion.spot_ref, f32[512,2048]{1,0:T(8,128)S(1)} %get-tuple-element.31.e_ref, f32[512,2048]{1,0:T(8,128)S(1)} %shard_map.54.mate_e_ref, f32[512,128]{1,0:T(8,128)S(1)} %get-tuple-element.41.scale_ref, ...), custom_call_target="tpu_custom_call" | custom-call | tf_op jit(solution)/shard_map/pallas_call | solution.py:356
  190.1 8.7 %collective-permute-start.5 = (f32[256,128]{1,0:T(8,128)S(1)}, f32[256,128]{1,0:T(8,128)S(1)}, u32[]{:S(2)}, u32[]{:S(2)}) collective-permute-start(f32[256,128]{1,0:T(8,128)S(1)} %get-tuple-element.47), channel_id=1, source_target_pairs={{0,1},{1,0},{2,3},{3,2},{4,5},{5,4},{6,7},{7,6},{8,9},{9,8},{10,11... | collective-permute-start | bytes 393224 | tf_op jit(solution)/shard_map/ppermute | solution.py:304
  198.8 1.0 collective-permute-done.5.other_ref
  199.7 0.0 copy-done.1
  199.7 0.9 shard_map.64
  (2 shorter events, 0.0 us)
Async XLA Ops:
  0.6 0.7 copy-start.2
  1.3 0.7 copy-start.4
  2.8 27.8 %all-to-all-start = ((f32[16,16,128]{2,1,0:T(8,128)}), f32[16,16,128]{2,1,0:T(8,128)S(1)}, u32[]{:S(2)}, u32[]{:S(2)}) async-start(f32[16,16,128]{2,1,0:T(8,128)} %shard_map.50), calls=%async_computation | async-start | bytes 262144 | tf_op jit(solution)/shard_map/all_to_all | solution.py:317
  18.6 0.9 copy-start
  19.6 3.8 %collective-permute-start = (f32[256,128]{1,0:T(8,128)S(1)}, f32[256,128]{1,0:T(8,128)S(1)}, u32[]{:S(2)}, u32[]{:S(2)}) collective-permute-start(f32[256,128]{1,0:T(8,128)S(1)} %shard_map.51), channel_id=1, source_target_pairs={{0,1},{1,0},{2,3},{3,2},{4,5},{5,4},{6,7},{7,6},{8,9},{9,8},{10,11... | collective-permute-start | bytes 393224 | tf_op jit(solution)/shard_map/ppermute | solution.py:304
  51.2 10.6 %collective-permute-start.1 = (f32[2048,128]{1,0:T(8,128)S(1)}, f32[2048,128]{1,0:T(8,128)S(1)}, u32[]{:S(2)}, u32[]{:S(2)}) collective-permute-start(f32[2048,128]{1,0:T(8,128)S(1)} %bitcast.12), channel_id=1, source_target_pairs={{0,1},{1,0},{2,3},{3,2},{4,5},{5,4},{6,7},{7,6},{8,9},{9,8},{10,11... | collective-permute-start | bytes 3145736 | tf_op jit(solution)/shard_map/ppermute | solution.py:304
  61.7 3.4 %collective-permute-start.2 = (f32[512,128]{1,0:T(8,128)S(1)}, f32[512,128]{1,0:T(8,128)S(1)}, u32[]{:S(2)}, u32[]{:S(2)}) collective-permute-start(f32[512,128]{1,0:T(8,128)S(1)} %get-tuple-element.35.own_ref), channel_id=1, source_target_pairs={{0,1},{1,0},{2,3},{3,2},{4,5},{5,4},{6,7},{7,6},{8,9},{9,8},{10,11... | collective-permute-start | bytes 786440 | tf_op jit(solution)/shard_map/ppermute | solution.py:304
  94.2 6.9 %collective-permute-start.3 = (f32[512,128]{1,0:T(8,128)S(1)}, f32[512,128]{1,0:T(8,128)S(1)}, u32[]{:S(2)}, u32[]{:S(2)}) collective-permute-start(f32[512,128]{1,0:T(8,128)S(1)} %get-tuple-element.37.own_ref), channel_id=1, source_target_pairs={{0,1},{1,0},{2,3},{3,2},{4,5},{5,4},{6,7},{7,6},{8,9},{9,8},{10,11... | collective-permute-start | bytes 786440 | tf_op jit(solution)/shard_map/ppermute | solution.py:304
  139.1 9.1 %collective-permute-start.4 = (f32[512,128]{1,0:T(8,128)S(1)}, f32[512,128]{1,0:T(8,128)S(1)}, u32[]{:S(2)}, u32[]{:S(2)}) collective-permute-start(f32[512,128]{1,0:T(8,128)S(1)} %shard_map.60.own_ref), channel_id=1, source_target_pairs={{0,1},{1,0},{2,3},{3,2},{4,5},{5,4},{6,7},{7,6},{8,9},{9,8},{10,11... | collective-permute-start | bytes 786440 | tf_op jit(solution)/shard_map/ppermute | solution.py:304
  171.0 16.5 %copy-start.3 = (f32[8,128]{1,0:T(8,128)S(1)}, f32[8,128]{1,0:T(8,128)}, u32[]{:S(2)}) copy-start(f32[8,128]{1,0:T(8,128)} %embeddings_ref.3) | copy-start | bytes 12292
  187.5 12.2 %copy-start.1 = (f32[256,128]{1,0:T(8,128)S(1)}, f32[256,128]{1,0:T(8,128)}, u32[]{:S(2)}) copy-start(f32[256,128]{1,0:T(8,128)} %protos_ref.1) | copy-start | bytes 393220
  190.1 9.6 %collective-permute-start.5 = (f32[256,128]{1,0:T(8,128)S(1)}, f32[256,128]{1,0:T(8,128)S(1)}, u32[]{:S(2)}, u32[]{:S(2)}) collective-permute-start(f32[256,128]{1,0:T(8,128)S(1)} %get-tuple-element.47), channel_id=1, source_target_pairs={{0,1},{1,0},{2,3},{3,2},{4,5},{5,4},{6,7},{7,6},{8,9},{9,8},{10,11... | collective-permute-start | bytes 393224 | tf_op jit(solution)/shard_map/ppermute | solution.py:304

commit v3 on v2

v3 whole, which is shorter than its diff:
```python
import functools

import jax
import jax.numpy as jnp
from jax import lax
from jax.experimental import pallas as pl
from jax.experimental.pallas import tpu as pltpu
from jax.sharding import PartitionSpec as P

LANES = 128
PAIR = 2 * LANES
CHUNK = 64
VMEM_BYTES = 24 * 1024 * 1024


def inverse_norms(values):
    return 1.0 / jnp.sqrt(jnp.sum(values * values, axis=1, keepdims=True) + 1e-06)


def finish_rows(values, grads):
    inverse = inverse_norms(values)
    units = values * inverse
    return inverse * (grads - units * jnp.sum(units * grads, axis=1, keepdims=True))


def split(values):
    high = values.astype(jnp.bfloat16)
    low = (values - high.astype(jnp.float32)).astype(jnp.bfloat16)
    return high, low


def dot(left, right):
    return jnp.dot(left, right, preferred_element_type=jnp.float32)


def dot_rows(left, right):
    return lax.dot_general(left, right, (((1,), (1,)), ((), ())), preferred_element_type=jnp.float32)


def call(body, out_shape, **kwargs):
    return pl.pallas_call(
        body, out_shape=out_shape, compiler_params=pltpu.CompilerParams(vmem_limit_bytes=VMEM_BYTES), **kwargs
    )


def f32(*shape):
    return jax.ShapeDtypeStruct(shape, jnp.float32)


def exponents(proto_pair, clips):
    high, low = split(clips)
    scores = dot_rows(proto_pair, jnp.concatenate([high, high], axis=1))
    scores = scores + dot_rows(proto_pair, jnp.concatenate([low, low], axis=1))
    return jnp.exp(scores * 10.0)


def scores_body(protos_ref, clips_ref, e_ref, total_ref, bundle_ref):
    n_here = protos_ref.shape[0]
    pair = jnp.concatenate(split(protos_ref[...]), axis=1)
    for block in range(clips_ref.shape[0] // PAIR):
        cols = slice(block * PAIR, (block + 1) * PAIR)
        clips = clips_ref[cols, :]
        bundle_ref[n_here + block * PAIR : n_here + (block + 1) * PAIR] = clips
        e = exponents(pair, clips)
        e_ref[:, cols] = e
        kernel = e * e
        both = kernel[:, :LANES] + kernel[:, LANES:]
        bundle_ref[:n_here] = both if block == 0 else bundle_ref[:n_here] + both
        totals = jnp.sum(e, axis=0, keepdims=True)
        for half in range(2):
            total_ref[2 * block + half : 2 * block + half + 1, :] = totals[:, half * LANES : (half + 1) * LANES]


def turned_protos(protos_ref):
    high, low = split(protos_ref[...].T)
    return jnp.concatenate([high, low], axis=0)


def times_protos(turned, weights):
    high, low = split(weights)
    both = dot(turned, high)
    return both[:LANES] + both[LANES:] + dot(turned[:LANES], low)


def pulls_body(protos_ref, e_ref, x_ref):
    turned = turned_protos(protos_ref)
    for block in range(e_ref.shape[1] // PAIR):
        x = times_protos(turned, e_ref[:, block * PAIR : (block + 1) * PAIR])
        for half in range(2):
            x_ref[2 * block + half] = x[:, half * LANES : (half + 1) * LANES]


def mates_of(part, index_ref, spot_ref, protos_ref, table_ref, e_ref, mate_ref):
    pair = jnp.concatenate(split(protos_ref[...]), axis=1)
    blocks = e_ref.shape[1] // PAIR
    tiles = 4 * blocks
    first = spot_ref[2] * 8
    for block in range(blocks):
        slot = block % 2
        for half in range(2):
            for z in range(LANES // 8):
                start = first + (z * tiles + 2 * (part * blocks + block) + half) * 16
                for r in range(8):
                    row = half * LANES + z * 8 + r
                    mate_ref[slot, row : row + 1, :] = table_ref[pl.ds(index_ref[start + r], 1), :]
        e_ref[:, block * PAIR : (block + 1) * PAIR] = exponents(pair, mate_ref[slot])


def mates_first_body(index_ref, spot_ref, protos_ref, own_ref, other_ref, e_ref, table_ref, mate_ref):
    rows = own_ref.shape[0]
    table_ref[:rows] = own_ref[...]
    table_ref[rows:] = other_ref[protos_ref.shape[0] :]
    mates_of(0, index_ref, spot_ref, protos_ref, table_ref, e_ref, mate_ref)


def mates_second_body(index_ref, spot_ref, protos_ref, table_ref, e_ref, mate_ref):
    mates_of(1, index_ref, spot_ref, protos_ref, table_ref, e_ref, mate_ref)


def column_scale(own_ref, other_ref, rows, protos):
    half = rows // 2
    part = jnp.concatenate([own_ref[:half] + other_ref[half:rows], own_ref[half:rows] + other_ref[:half]], axis=0)
    scale = 1.0 / (protos * jnp.sum(part, axis=1, keepdims=True))
    return jnp.broadcast_to(scale, (rows, LANES))


def row_mass(e_ref, scale, tile):
    e = e_ref[:, tile * LANES : (tile + 1) * LANES]
    return jnp.sum(e * e * scale, axis=0, keepdims=True)


def units_body(in_ref, out_ref):
    values = in_ref[...]
    out_ref[...] = values * inverse_norms(values)


def send_body(n_proto, embeddings_ref, partner_ref, out_ref, values_ref, mates_ref, sems):
    copies = [
        pltpu.make_async_copy(embeddings_ref, values_ref, sems.at[0]),
        pltpu.make_async_copy(partner_ref, mates_ref, sems.at[1]),
    ]
    for copy in copies:
        copy.start()
    for copy in copies:
        copy.wait()
    values = values_ref[...]
    partner = mates_ref[...]
    rows = values.shape[0]
    line = partner & (rows - 1)
    slot = (partner // rows) & (n_proto - 1)
    place = (slot & 1) * (n_proto // 2) + (slot >> 1)
    place = place * LANES + partner // (rows * n_proto) * rows + line
    block = jnp.concatenate([values * inverse_norms(values), place.astype(jnp.float32)], axis=0)
    for layer in range(out_ref.shape[0] // block.shape[0]):
        out_ref[layer * block.shape[0] : (layer + 1) * block.shape[0]] = block


def column_body(spot_ref, in_ref, out_ref, places_ref):
    per_layer = places_ref.shape[1]
    size = 8 + per_layer
    places = []
    for layer in range(places_ref.shape[0]):
        units = in_ref[layer * size : layer * size + 8]
        places.append(in_ref[layer * size + 8 : (layer + 1) * size][None])
        for block in range(out_ref.shape[0]):
            out_ref[block, layer * 8 : layer * 8 + 8] = units
    here = out_ref.shape[0] * LANES
    places = jnp.concatenate(places, axis=0).astype(jnp.int32)
    moved = jnp.where(places >= here, places - here, places + here)
    places_ref[...] = jnp.where(spot_ref[2] > 0, moved, places)


def masses_of(e_ref, scale):
    tiles = e_ref.shape[1] // LANES
    return jnp.concatenate([row_mass(e_ref, scale, tile) for tile in range(tiles)], axis=0)


def rows_first_body(protos, e_ref, own_ref, other_ref, totals_ref, out_ref):
    tiles = e_ref.shape[1] // LANES
    scale = column_scale(own_ref, other_ref, e_ref.shape[0], protos)
    masses = masses_of(e_ref, scale)
    for block in range(tiles):
        out_ref[block, :tiles] = masses
        out_ref[block, tiles:] = jnp.broadcast_to(totals_ref[block : block + 1, :], (8, LANES))


def spread_first_body(in_ref, out_ref):
    tiles = in_ref.shape[0]
    total = jnp.sum(in_ref[...], axis=0)
    size = tiles + 1
    for layer in range(out_ref.shape[0] // size):
        out_ref[layer * size : (layer + 1) * size] = total[:size]


def weigh_columns(e_ref, scale, part_ref):
    tiles = e_ref.shape[1] // LANES
    for start in range(0, e_ref.shape[0], CHUNK):
        rows = slice(start, start + CHUNK)
        total = None
        for tile in range(tiles):
            e = e_ref[rows, tile * LANES : (tile + 1) * LANES]
            term = e * e * scale[tile : tile + 1, :]
            total = term if total is None else total + term
        part_ref[rows, :] = total


def cols_first_body(clips, e_ref, in_ref, part_ref, own_total_ref):
    tiles = e_ref.shape[1] // LANES
    size = tiles + 1
    total = in_ref[:size]
    for layer in range(1, in_ref.shape[0] // size):
        total = total + in_ref[layer * size : (layer + 1) * size]
    own_total_ref[...] = jnp.broadcast_to(total[tiles:], (8, LANES))
    weigh_columns(e_ref, 1.0 / (clips * total[:tiles]), part_ref)


def rows_second_body(protos, e_ref, own_ref, other_ref, x_ref, own_total_ref, out_ref):
    tiles = e_ref.shape[1] // LANES
    scale = column_scale(own_ref, other_ref, e_ref.shape[0], protos)
    masses = masses_of(e_ref, scale)
    for block in range(tiles):
        out_ref[block, :tiles] = masses
        out_ref[block, tiles : tiles + LANES] = x_ref[block]
        out_ref[block, tiles + LANES :] = own_total_ref[...]


def spread_second_body(in_ref, out_ref, totals_ref):
    tiles = in_ref.shape[0]
    size = tiles + 8
    total = jnp.sum(in_ref[:, : tiles + LANES, :], axis=0)
    x = total[tiles:].T
    for layer in range(out_ref.shape[0] // size):
        base = layer * size
        out_ref[base : base + tiles] = total[:tiles]
        out_ref[base + tiles : base + size] = x[layer * 8 : layer * 8 + 8]
    for block in range(tiles):
        totals_ref[block : block + 1, :] = in_ref[block, tiles + LANES : tiles + LANES + 1, :]


def summed_lines(in_ref, size):
    total = in_ref[:size]
    for layer in range(1, in_ref.shape[0] // size):
        total = total + in_ref[layer * size : (layer + 1) * size]
    return total


def cols_second_body(clips, e_ref, in_ref, part_ref, x_ref):
    tiles = e_ref.shape[1] // LANES
    total = summed_lines(in_ref, tiles + 8)
    x_ref[...] = total[tiles:]
    weigh_columns(e_ref, 1.0 / (clips * total[:tiles]), part_ref)


def mates_rows_body(protos, first_ref, second_ref, own_ref, other_ref, protos_ref, out_ref, scale_ref):
    scale = column_scale(own_ref, other_ref, protos_ref.shape[0], protos)
    scale_ref[...] = scale
    wide = jnp.concatenate([scale, scale], axis=1)
    turned = turned_protos(protos_ref)
    masses = []
    blocks = first_ref.shape[1] // PAIR
    for block in range(2 * blocks):
        mate_e_ref = first_ref if block < blocks else second_ref
        start = block % blocks * PAIR
        e = mate_e_ref[:, start : start + PAIR]
        kernel = e * e * wide
        mass = jnp.sum(kernel, axis=0, keepdims=True)
        y = times_protos(turned, kernel)
        for half in range(2):
            lanes = slice(half * LANES, (half + 1) * LANES)
            masses.append(mass[:, lanes])
            out_ref[2 * block + half, :LANES] = y[:, lanes]
    masses = jnp.concatenate(masses, axis=0)
    for tile in range(out_ref.shape[0]):
        out_ref[tile, LANES:] = masses


def turn_body(in_ref, out_ref):
    tiles = in_ref.shape[0]
    size = 8 + tiles
    total = jnp.sum(in_ref[...], axis=0)
    y = total[:LANES].T
    for layer in range(out_ref.shape[0] // size):
        base = layer * size
        out_ref[base : base + 8] = y[layer * 8 : layer * 8 + 8]
        out_ref[base + 8 : base + size] = total[LANES:]


def proto_grads(rows, e_ref, first_ref, second_ref, scale_ref, shares, masses, clips_ref):
    scale = scale_ref[rows, :]
    blocks = first_ref.shape[1] // PAIR
    acc = None
    for block in range(2 * blocks):
        mate_e_ref = first_ref if block < blocks else second_ref
        pieces = []
        for half in range(2):
            tile = 2 * block + half
            mate = mate_e_ref[rows, (block % blocks * 2 + half) * LANES : (block % blocks * 2 + half + 1) * LANES]
            e = e_ref[rows, tile * LANES : (tile + 1) * LANES]
            pieces.append(e * shares[tile : tile + 1, :] - mate * mate * scale * masses[tile : tile + 1, :])
        high, low = split(jnp.concatenate(pieces, axis=1))
        clip_high, clip_low = split(clips_ref[block * PAIR : (block + 1) * PAIR, :])
        term = dot(high, jnp.concatenate([clip_high, clip_low], axis=1))
        term = term[:, :LANES] + term[:, LANES:] + dot(low, clip_high)
        acc = term if acc is None else acc + term
    return acc * 10.0


def other_grads_body(e_ref, first_ref, second_ref, scale_ref, totals_ref, in_ref, clips_ref, out_ref, y_ref, inverse_ref):
    n_rows = out_ref.shape[0]
    tiles = totals_ref.shape[0]
    total = summed_lines(in_ref, 8 + tiles)
    y_ref[...] = total[:8]
    masses = 1.0 / total[8:]
    shares = 1.0 / totals_ref[...]
    inverse_ref[:tiles] = masses
    inverse_ref[tiles:] = shares
    rows = slice(n_rows, 2 * n_rows)
    out_ref[...] = proto_grads(rows, e_ref, first_ref, second_ref, scale_ref, shares, masses, clips_ref)


def own_values(ref, row, layer):
    values = jnp.broadcast_to(ref[pl.ds(row, 1), :], (8, LANES))
    lane = lax.broadcasted_iota(jnp.int32, (8, LANES), 1)
    line = lax.broadcasted_iota(jnp.int32, (8, LANES), 0)
    return jnp.sum(jnp.where(lane == layer * 8 + line, values, 0.0), axis=1, keepdims=True)


def own_grads_body(spot_ref, e_ref, first_ref, second_ref, scale_ref, inverse_ref, x_ref, y_ref, clips_ref,
                   embeddings_ref, clip_ref, out_ref):
    tiles = inverse_ref.shape[0] // 2
    rows = slice(0, out_ref.shape[0])
    out_ref[...] = proto_grads(
        rows, e_ref, first_ref, second_ref, scale_ref, inverse_ref[tiles:], inverse_ref[:tiles], clips_ref
    )
    own_mass = own_values(inverse_ref, spot_ref[0], spot_ref[1])
    own_share = own_values(inverse_ref, spot_ref[0] + tiles, spot_ref[1])
    clip_ref[...] = finish_rows(embeddings_ref[...], 10.0 * (x_ref[...] * own_share - y_ref[...] * own_mass))


def finish_body(protos_ref, own_ref, other_ref, out_ref):
    out_ref[...] = finish_rows(protos_ref[...], own_ref[...] + other_ref[...])


def local(embeddings, prototypes, partner):
    n_batch, n_proto = lax.axis_size("batch"), lax.axis_size("proto")
    tiles = n_proto // 2
    rows, features = embeddings.shape
    own_protos = prototypes.shape[0]
    clips, protos = float(rows * n_batch * n_proto), float(own_protos * n_batch * n_proto)
    here, n_here = tiles * LANES, 2 * own_protos
    where = lax.axis_index("proto")
    same_core = [[2 * i + c for i in range(tiles)] for c in range(2)]
    cores = [(i, i ^ 1) for i in range(n_proto)]
    smem = pl.BlockSpec(memory_space=pltpu.SMEM)
    vmem = pl.BlockSpec(memory_space=pltpu.VMEM)

    def swap(values):
        return lax.ppermute(values, "proto", cores)

    def over_chips(blocks):
        return lax.all_to_all(blocks, "proto", 0, 0, tiled=True, axis_index_groups=same_core)

    def over_layers(lines):
        blocks = lax.all_to_all(lines.reshape(n_batch, 1, -1), "batch", 0, 0, tiled=True)
        return blocks.reshape(lines.shape)

    spot = jnp.stack([where >> 1, lax.axis_index("batch"), where & 1])
    partner = partner.reshape(-1, LANES)
    sent = call(
        functools.partial(send_body, n_proto),
        f32(n_batch * (rows + partner.shape[0]), LANES),
        in_specs=[pl.BlockSpec(memory_space=pltpu.HBM)] * 2,
        scratch_shapes=[
            pltpu.VMEM(embeddings.shape, jnp.float32),
            pltpu.VMEM(partner.shape, jnp.int32),
            pltpu.SemaphoreType.DMA((2,)),
        ],
    )(embeddings, partner)
    sent, held, spot = lax.optimization_barrier((sent, prototypes, spot))
    column = over_layers(sent)
    own_units = call(units_body, f32(own_protos, features))(held)
    unit_protos = jnp.concatenate([own_units, swap(own_units)], axis=0)
    column, unit_protos = lax.optimization_barrier((column, unit_protos))
    blocks, places = call(
        column_body,
        (f32(tiles, LANES, features), jax.ShapeDtypeStruct((n_batch, partner.shape[0], LANES), jnp.int32)),
        in_specs=[smem, vmem],
    )(spot, column)
    own_clips = over_chips(blocks).reshape(here, features)

    e, totals, bundle = call(
        scores_body, (f32(n_here, here), f32(tiles, LANES), f32(n_here + here, features))
    )(unit_protos, own_clips)
    x = call(pulls_body, f32(tiles, features, LANES))(unit_protos, e)
    received, x = lax.optimization_barrier((swap(bundle), x))
    blocks = call(functools.partial(rows_first_body, protos), f32(tiles, tiles + 8, LANES))(e, bundle, received, totals)
    lines = call(spread_first_body, f32(n_batch * (tiles + 1), LANES))(over_chips(blocks))
    part, own_total = call(functools.partial(cols_first_body, clips), (f32(n_here, LANES), f32(8, LANES)))(
        e, over_layers(lines)
    )

    mates = pltpu.VMEM((2, PAIR, features), jnp.float32)
    part, late = lax.optimization_barrier((part, places.reshape(-1)))
    first_e, table = call(
        mates_first_body,
        (f32(n_here, here // 2), f32(2 * here, features)),
        in_specs=[smem, smem, vmem, vmem, vmem],
        scratch_shapes=[mates],
    )(late, spot, unit_protos, own_clips, received)
    other, first_e = lax.optimization_barrier((swap(part), first_e))
    blocks = call(functools.partial(rows_second_body, protos), f32(tiles, tiles + LANES + 8, LANES))(
        e, part, other, x, own_total
    )
    lines, totals = call(spread_second_body, (f32(n_batch * (tiles + 8), LANES), f32(tiles, LANES)))(over_chips(blocks))
    part, x = call(functools.partial(cols_second_body, clips), (f32(n_here, LANES), f32(rows, features)))(
        e, over_layers(lines)
    )
    part, late = lax.optimization_barrier((part, late))
    second_e = call(
        mates_second_body, f32(n_here, here // 2), in_specs=[smem, smem, vmem, vmem], scratch_shapes=[mates]
    )(late, spot, unit_protos, table)
    other, second_e = lax.optimization_barrier((swap(part), second_e))
    blocks, scale = call(
        functools.partial(mates_rows_body, protos), (f32(tiles, features + tiles, LANES), f32(n_here, LANES))
    )(first_e, second_e, part, other, unit_protos)
    lines = call(turn_body, f32(n_batch * (8 + tiles), LANES))(over_chips(blocks))
    other_grads, y, inverse = call(
        other_grads_body, (f32(own_protos, features), f32(rows, features), f32(2 * tiles, LANES))
    )(e, first_e, second_e, scale, totals, over_layers(lines), own_clips)
    grad_embeddings, own_grads = call(
        own_grads_body, (f32(rows, features), f32(own_protos, features)), in_specs=[smem] + [vmem] * 9
    )(spot, e, first_e, second_e, scale, inverse, x, y, own_clips, embeddings)
    grad_prototypes = call(finish_body, f32(own_protos, features))(prototypes, own_grads, swap(other_grads))
    return (grad_embeddings, grad_prototypes)


def solution(mesh):
    in_specs = (P(("batch", "proto"), None), P(("batch", "proto"), None), P("batch"))
    out_specs = (P(("batch", "proto"), None), P(("batch", "proto"), None))
    return jax.shard_map(local, mesh=mesh, in_specs=in_specs, out_specs=out_specs, check_vma=False)
```

time: 201 us -> 197 us (0.980)
  starting transfers between devices: 47.2 us -> 44.3 us
  waiting for transfers between devices: 11.7 us -> 9.36 us
    ppermute x6 -> x5, starting transfers between devices: 31.4 us -> 28.5 us  [swap(): return lax.ppermute(values, 'proto', cores)]
    ppermute x6 -> x5, waiting for transfers between devices: 4.57 us -> 2.48 us  [swap(): return lax.ppermute(values, 'proto', cores)]
    pallas_call x7 -> x10, Pallas kernels: 11.4 us -> 11.8 us  [the longest x1 2.4 us: local(): call(mates_first_body, (f32(n_here, here // 2), f32(2 * here, features)),...]
  transfers between devices with their start and end apart: 7 -> 6, of which waited for: 5 -> 3; matrix products, arithmetic and copies ran while one was open for 0% -> 0% of each run, Pallas kernels for 4% -> 4%
where the time goes in v3:
time: 197 us
  blocking collectives  123 us (62%)
  starting transfers between devices  44.3 us (22%)
  Pallas kernels  16.5 us (8%)
  waiting for transfers between devices  9.36 us (5%)
  local copies, waits for them, and re-layouts  2.27 us (1%)
    all_to_all x4, blocking collectives, over_chips(): lax.all_to_all(blocks, 'proto', 0, 0, tiled=True, axis_index_groups=same_...  74 us
    all_to_all x3, blocking collectives, over_layers(): lax.all_to_all(lines.reshape(n_batch, 1, -1), 'batch', 0, 0, tiled=True)  49.2 us
    ppermute x5, starting transfers between devices, swap(): return lax.ppermute(values, 'proto', cores)  28.5 us
    all_to_all x1, starting transfers between devices, over_layers(): lax.all_to_all(lines.reshape(n_batch, 1, -1), 'batch', 0, 0, tiled=True)  15.7 us
    all_to_all x1, waiting for transfers between devices, over_layers(): lax.all_to_all(lines.reshape(n_batch, 1, -1), 'batch', 0, 0, tiled=True)  6.88 us
  transfers between devices with their start and end apart: 6, of which 3 were waited for; matrix products, arithmetic and copies ran while one was open for 0% of the time, Pallas kernels for 4%

profile of v3, /device:TPU:1, one launch (start us, length us, event | category | flops | bytes accessed | tf_op | source)
XLA Modules:
  0.0 196.5 jit_solution(11741402646033633886)
XLA Ops:
  0.6 0.0 copy-start.2
  0.6 0.7 copy-done.2
  1.3 0.0 copy-start.4
  1.3 0.7 copy-done.4
  2.0 0.8 shard_map.50
  2.8 0.1 pad_add_fusion.spot_ref
  2.8 15.7 %all-to-all-start = ((f32[16,1,1280]{2,1,0:T(1,128)}), f32[16,1,1280]{2,1,0:T(1,128)S(1)}, u32[]{:S(2)}, u32[]{:S(2)}) async-start(f32[16,1,1280]{2,1,0:T(1,128)} %bitcast.4), calls=%async_computation | async-start | bytes 163840 | tf_op jit(solution)/shard_map/all_to_all | solution.py:364
  18.6 0.0 copy-start
  18.6 0.9 copy-done
  19.5 0.1 shard_map.51
  19.6 2.9 %collective-permute-start = (f32[256,128]{1,0:T(8,128)S(1)}, f32[256,128]{1,0:T(8,128)S(1)}, u32[]{:S(2)}, u32[]{:S(2)}) collective-permute-start(f32[256,128]{1,0:T(8,128)S(1)} %shard_map.51), channel_id=1, source_target_pairs={{0,1},{1,0},{2,3},{3,2},{4,5},{5,4},{6,7},{7,6},{8,9},{9,8},{10,11... | collective-permute-start | bytes 393224 | tf_op jit(solution)/shard_map/ppermute | solution.py:358
  22.5 1.0 collective-permute-done
  23.5 6.9 %all-to-all-done = f32[16,1,1280]{2,1,0:T(1,128)S(1)} async-done(((f32[16,1,1280]{2,1,0:T(1,128)}), f32[16,1,1280]{2,1,0:T(1,128)S(1)}, u32[]{:S(2)}, u32[]{:S(2)}) %all-to-all-start) | async-done | bytes 81952 | tf_op jit(solution)/shard_map/all_to_all | solution.py:364
  30.4 0.6 shard_map.52
  31.0 21.2 %all_to_all.40 = f32[16,128,128]{2,1,0:T(8,128)S(1)} all-to-all(f32[16,128,128]{2,1,0:T(8,128)S(1)} %get-tuple-element.42), channel_id=1, replica_groups={{0,2,4,6,8,10,12,14,16,18,20,22,24,26,28,30},{1,3,5,7,9,11,13,15,17,19,..., dimensions={0} | all-to-all | bytes 2097152 | tf_op jit(solution)/shard_map/all_to_all | solution.py:361
  52.2 1.4 shard_map.53
  53.6 5.5 %collective-permute-start.1 = (f32[2560,128]{1,0:T(8,128)S(1)}, f32[2560,128]{1,0:T(8,128)S(1)}, u32[]{:S(2)}, u32[]{:S(2)}) collective-permute-start(f32[2560,128]{1,0:T(8,128)S(1)} %get-tuple-element.44.own_ref), channel_id=1, source_target_pairs={{0,1},{1,0},{2,3},{3,2},{4,5},{5,4},{6,7},{7,6},{8,9},{9,8},{10,11... | collective-permute-start | bytes 3932168 | tf_op jit(solution)/shard_map/ppermute | solution.py:358
  59.1 1.1 shard_map.54.x_ref
  60.2 1.5 collective-permute-done.1.other_ref
  61.7 0.6 shard_map.55
  62.3 9.8 %all_to_all.41.in_ref = f32[16,24,128]{2,1,0:T(8,128)S(1)} all-to-all(f32[16,24,128]{2,1,0:T(8,128)S(1)} %shard_map.55), channel_id=1, replica_groups={{0,2,4,6,8,10,12,14,16,18,20,22,24,26,28,30},{1,3,5,7,9,11,13,15,17,19,..., dimensions={0} | all-to-all | bytes 393216 | tf_op jit(solution)/shard_map/all_to_all | solution.py:361
  72.1 16.7 %all_to_all.42 = f32[16,1,2176]{2,1,0:T(1,128)S(1)} all-to-all(f32[16,1,2176]{2,1,0:T(1,128)S(1)} %bitcast.22), channel_id=1, replica_groups=mesh['batch'=16,'proto'=32] {'batch'}, dimensions={0} | all-to-all | bytes 278528 | tf_op jit(solution)/shard_map/all_to_all | solution.py:364
  88.8 0.4 shard_map.57
  89.3 6.1 %collective-permute-start.2 = (f32[512,128]{1,0:T(8,128)S(1)}, f32[512,128]{1,0:T(8,128)S(1)}, u32[]{:S(2)}, u32[]{:S(2)}) collective-permute-start(f32[512,128]{1,0:T(8,128)S(1)} %get-tuple-element.49.own_ref), channel_id=1, source_target_pairs={{0,1},{1,0},{2,3},{3,2},{4,5},{5,4},{6,7},{7,6},{8,9},{9,8},{10,11... | collective-permute-start | bytes 786440 | tf_op jit(solution)/shard_map/ppermute | solution.py:358
  95.4 2.4 %shard_map.58 = (f32[512,1024]{1,0:T(8,128)S(1)}, f32[4096,128]{1,0:T(8,128)S(1)}) custom-call(s32[4096]{0:T(1024)S(1)} %bitcast.25, s32[3]{0:T(128)S(1)} %pad_add_fusion.spot_ref, f32[512,128]{1,0:T(8,128)S(1)} %pad_maximum_fusion.protos_ref, f32[2048,128]{1,0:T(8,128)S(1)} %bitcast.15, f32[2560,128]{1,0:T(8,128)S(1)} %collective-permute-done.1.other_ref), custom_call_target="tpu_custom_call" | custom-call | tf_op jit(solution)/shard_map/pallas_call | solution.py:404
  97.8 0.0 collective-permute-done.2.other_ref
  97.8 0.6 shard_map.59
  98.4 21.6 %all_to_all.43.in_ref = f32[16,152,128]{2,1,0:T(8,128)S(1)} all-to-all(f32[16,152,128]{2,1,0:T(8,128)S(1)} %shard_map.59), channel_id=1, replica_groups={{0,2,4,6,8,10,12,14,16,18,20,22,24,26,28,30},{1,3,5,7,9,11,13,15,17,19,..., dimensions={0} | all-to-all | bytes 2490368 | tf_op jit(solution)/shard_map/all_to_all | solution.py:361
  120.1 0.1 shard_map.60
  120.2 15.8 %all_to_all.44 = f32[16,1,3072]{2,1,0:T(1,128)S(1)} all-to-all(f32[16,1,3072]{2,1,0:T(1,128)S(1)} %bitcast.24), channel_id=1, replica_groups=mesh['batch'=16,'proto'=32] {'batch'}, dimensions={0} | all-to-all | bytes 393216 | tf_op jit(solution)/shard_map/all_to_all | solution.py:364
  136.0 0.4 shard_map.61
  136.4 7.0 %collective-permute-start.3 = (f32[512,128]{1,0:T(8,128)S(1)}, f32[512,128]{1,0:T(8,128)S(1)}, u32[]{:S(2)}, u32[]{:S(2)}) collective-permute-start(f32[512,128]{1,0:T(8,128)S(1)} %get-tuple-element.58.own_ref), channel_id=1, source_target_pairs={{0,1},{1,0},{2,3},{3,2},{4,5},{5,4},{6,7},{7,6},{8,9},{9,8},{10,11... | collective-permute-start | bytes 786440 | tf_op jit(solution)/shard_map/ppermute | solution.py:358
  143.5 2.3 %shard_map.62.second_ref = f32[512,1024]{1,0:T(8,128)S(1)} custom-call(s32[4096]{0:T(1024)S(1)} %bitcast.26, s32[3]{0:T(128)S(1)} %pad_add_fusion.spot_ref, f32[512,128]{1,0:T(8,128)S(1)} %pad_maximum_fusion.protos_ref, f32[4096,128]{1,0:T(8,128)S(1)} %get-tuple-element.60.table_ref), custom_call_target="tpu_custom_call" | custom-call | tf_op jit(solution)/shard_map/pallas_call | solution.py:419
  145.8 0.0 collective-permute-done.3.other_ref
  145.8 1.4 shard_map.63
  147.2 21.3 %all_to_all.45.in_ref = f32[16,144,128]{2,1,0:T(8,128)S(1)} all-to-all(f32[16,144,128]{2,1,0:T(8,128)S(1)} %get-tuple-element.65), channel_id=1, replica_groups={{0,2,4,6,8,10,12,14,16,18,20,22,24,26,28,30},{1,3,5,7,9,11,13,15,17,19,..., dimensions={0} | all-to-all | bytes 2359296 | tf_op jit(solution)/shard_map/all_to_all | solution.py:361
  168.6 0.1 shard_map.64
  168.7 16.7 %all_to_all.46 = f32[16,1,3072]{2,1,0:T(1,128)S(1)} all-to-all(f32[16,1,3072]{2,1,0:T(1,128)S(1)} %bitcast.19), channel_id=1, replica_groups=mesh['batch'=16,'proto'=32] {'batch'}, dimensions={0} | all-to-all | bytes 393216 | tf_op jit(solution)/shard_map/all_to_all | solution.py:364
  185.4 0.0 copy-start.3
  185.4 1.1 shard_map.65
  186.5 7.0 %collective-permute-start.4 = (f32[256,128]{1,0:T(8,128)S(1)}, f32[256,128]{1,0:T(8,128)S(1)}, u32[]{:S(2)}, u32[]{:S(2)}) collective-permute-start(f32[256,128]{1,0:T(8,128)S(1)} %get-tuple-element.71), channel_id=1, source_target_pairs={{0,1},{1,0},{2,3},{3,2},{4,5},{5,4},{6,7},{7,6},{8,9},{9,8},{10,11... | collective-permute-start | bytes 393224 | tf_op jit(solution)/shard_map/ppermute | solution.py:358
  193.5 0.0 copy-done.3
  193.5 0.0 copy-start.1
  193.6 2.1 %shard_map.66 = (f32[8,128]{1,0:T(8,128)}, f32[256,128]{1,0:T(8,128)S(1)}) custom-call(s32[3]{0:T(128)S(1)} %pad_add_fusion.spot_ref, f32[512,2048]{1,0:T(8,128)S(1)} %get-tuple-element.43.e_ref, f32[512,1024]{1,0:T(8,128)S(1)} %get-tuple-element.52.first_ref, f32[512,1024]{1,0:T(8,128)S(1)} %shard_map.62.second_ref, ...), custom_call_target="tpu_custom_call" | custom-call | tf_op jit(solution)/shard_map/pallas_call | solution.py:430
  195.6 0.0 collective-permute-done.4.other_ref
  195.6 0.0 copy-done.1
  195.6 0.9 shard_map.67
  (2 shorter events, 0.0 us)
Async XLA Ops:
  0.6 0.7 copy-start.2
  1.3 0.7 copy-start.4
  2.8 27.5 %all-to-all-start = ((f32[16,1,1280]{2,1,0:T(1,128)}), f32[16,1,1280]{2,1,0:T(1,128)S(1)}, u32[]{:S(2)}, u32[]{:S(2)}) async-start(f32[16,1,1280]{2,1,0:T(1,128)} %bitcast.4), calls=%async_computation | async-start | bytes 163840 | tf_op jit(solution)/shard_map/all_to_all | solution.py:364
  18.6 0.9 copy-start
  19.6 3.8 %collective-permute-start = (f32[256,128]{1,0:T(8,128)S(1)}, f32[256,128]{1,0:T(8,128)S(1)}, u32[]{:S(2)}, u32[]{:S(2)}) collective-permute-start(f32[256,128]{1,0:T(8,128)S(1)} %shard_map.51), channel_id=1, source_target_pairs={{0,1},{1,0},{2,3},{3,2},{4,5},{5,4},{6,7},{7,6},{8,9},{9,8},{10,11... | collective-permute-start | bytes 393224 | tf_op jit(solution)/shard_map/ppermute | solution.py:358
  53.6 8.1 %collective-permute-start.1 = (f32[2560,128]{1,0:T(8,128)S(1)}, f32[2560,128]{1,0:T(8,128)S(1)}, u32[]{:S(2)}, u32[]{:S(2)}) collective-permute-start(f32[2560,128]{1,0:T(8,128)S(1)} %get-tuple-element.44.own_ref), channel_id=1, source_target_pairs={{0,1},{1,0},{2,3},{3,2},{4,5},{5,4},{6,7},{7,6},{8,9},{9,8},{10,11... | collective-permute-start | bytes 3932168 | tf_op jit(solution)/shard_map/ppermute | solution.py:358
  89.3 8.6 %collective-permute-start.2 = (f32[512,128]{1,0:T(8,128)S(1)}, f32[512,128]{1,0:T(8,128)S(1)}, u32[]{:S(2)}, u32[]{:S(2)}) collective-permute-start(f32[512,128]{1,0:T(8,128)S(1)} %get-tuple-element.49.own_ref), channel_id=1, source_target_pairs={{0,1},{1,0},{2,3},{3,2},{4,5},{5,4},{6,7},{7,6},{8,9},{9,8},{10,11... | collective-permute-start | bytes 786440 | tf_op jit(solution)/shard_map/ppermute | solution.py:358
  136.4 9.4 %collective-permute-start.3 = (f32[512,128]{1,0:T(8,128)S(1)}, f32[512,128]{1,0:T(8,128)S(1)}, u32[]{:S(2)}, u32[]{:S(2)}) collective-permute-start(f32[512,128]{1,0:T(8,128)S(1)} %get-tuple-element.58.own_ref), channel_id=1, source_target_pairs={{0,1},{1,0},{2,3},{3,2},{4,5},{5,4},{6,7},{7,6},{8,9},{9,8},{10,11... | collective-permute-start | bytes 786440 | tf_op jit(solution)/shard_map/ppermute | solution.py:358
  185.4 8.1 %copy-start.3 = (f32[8,128]{1,0:T(8,128)S(1)}, f32[8,128]{1,0:T(8,128)}, u32[]{:S(2)}) copy-start(f32[8,128]{1,0:T(8,128)} %embeddings_ref.3) | copy-start | bytes 12292
  186.5 9.1 %collective-permute-start.4 = (f32[256,128]{1,0:T(8,128)S(1)}, f32[256,128]{1,0:T(8,128)S(1)}, u32[]{:S(2)}, u32[]{:S(2)}) collective-permute-start(f32[256,128]{1,0:T(8,128)S(1)} %get-tuple-element.71), channel_id=1, source_target_pairs={{0,1},{1,0},{2,3},{3,2},{4,5},{5,4},{6,7},{7,6},{8,9},{9,8},{10,11... | collective-permute-start | bytes 393224 | tf_op jit(solution)/shard_map/ppermute | solution.py:358
  193.5 2.1 %copy-start.1 = (f32[256,128]{1,0:T(8,128)S(1)}, f32[256,128]{1,0:T(8,128)}, u32[]{:S(2)}) copy-start(f32[256,128]{1,0:T(8,128)} %protos_ref.1) | copy-start | bytes 393220

commit v4 on v3

--- a/solution.py
+++ b/solution.py
@@ -134,18 +134,9 @@
     out_ref[...] = values * inverse_norms(values)
 
 
-def send_body(n_proto, embeddings_ref, partner_ref, out_ref, values_ref, mates_ref, sems):
-    copies = [
-        pltpu.make_async_copy(embeddings_ref, values_ref, sems.at[0]),
-        pltpu.make_async_copy(partner_ref, mates_ref, sems.at[1]),
-    ]
-    for copy in copies:
-        copy.start()
-    for copy in copies:
-        copy.wait()
-    values = values_ref[...]
-    partner = mates_ref[...]
-    rows = values.shape[0]
+def send_body(n_proto, rows, in_ref, out_ref):
+    values = in_ref[:rows]
+    partner = in_ref[rows:].astype(jnp.int32)
     line = partner & (rows - 1)
     slot = (partner // rows) & (n_proto - 1)
     place = (slot & 1) * (n_proto // 2) + (slot >> 1)
@@ -214,27 +205,21 @@
     weigh_columns(e_ref, 1.0 / (clips * total[:tiles]), part_ref)
 
 
-def rows_second_body(protos, e_ref, own_ref, other_ref, x_ref, own_total_ref, out_ref):
+def rows_second_body(protos, e_ref, own_ref, other_ref, own_total_ref, out_ref):
     tiles = e_ref.shape[1] // LANES
-    scale = column_scale(own_ref, other_ref, e_ref.shape[0], protos)
-    masses = masses_of(e_ref, scale)
+    masses = masses_of(e_ref, column_scale(own_ref, other_ref, e_ref.shape[0], protos))
     for block in range(tiles):
         out_ref[block, :tiles] = masses
-        out_ref[block, tiles : tiles + LANES] = x_ref[block]
-        out_ref[block, tiles + LANES :] = own_total_ref[...]
+        out_ref[block, tiles:] = own_total_ref[...]
 
 
 def spread_second_body(in_ref, out_ref, totals_ref):
     tiles = in_ref.shape[0]
-    size = tiles + 8
-    total = jnp.sum(in_ref[:, : tiles + LANES, :], axis=0)
-    x = total[tiles:].T
-    for layer in range(out_ref.shape[0] // size):
-        base = layer * size
-        out_ref[base : base + tiles] = total[:tiles]
-        out_ref[base + tiles : base + size] = x[layer * 8 : layer * 8 + 8]
+    masses = jnp.sum(in_ref[:, :tiles, :], axis=0)
+    for layer in range(out_ref.shape[0] // tiles):
+        out_ref[layer * tiles : (layer + 1) * tiles] = masses
     for block in range(tiles):
-        totals_ref[block : block + 1, :] = in_ref[block, tiles + LANES : tiles + LANES + 1, :]
+        totals_ref[block : block + 1, :] = in_ref[block, tiles : tiles + 1, :]
 
 
 def summed_lines(in_ref, size):
@@ -244,14 +229,13 @@
     return total
 
 
-def cols_second_body(clips, e_ref, in_ref, part_ref, x_ref):
-    tiles = e_ref.shape[1] // LANES
-    total = summed_lines(in_ref, tiles + 8)
-    x_ref[...] = total[tiles:]
-    weigh_columns(e_ref, 1.0 / (clips * total[:tiles]), part_ref)
-
-
-def mates_rows_body(protos, first_ref, second_ref, own_ref, other_ref, protos_ref, out_ref, scale_ref):
+def cols_second_body(clips, e_ref, in_ref, part_ref):
+    weigh_columns(e_ref, 1.0 / (clips * summed_lines(in_ref, e_ref.shape[1] // LANES)), part_ref)
+
+
+def mates_rows_body(protos, side, spot_ref, first_ref, second_ref, own_ref, other_ref, protos_ref, x_ref, out_ref, scale_ref):
+    size = out_ref.shape[0] // side
+    pair = 2 * LANES
     scale = column_scale(own_ref, other_ref, protos_ref.shape[0], protos)
     scale_ref[...] = scale
     wide = jnp.concatenate([scale, scale], axis=1)
@@ -268,21 +252,34 @@
         for half in range(2):
             lanes = slice(half * LANES, (half + 1) * LANES)
             masses.append(mass[:, lanes])
-            out_ref[2 * block + half, :LANES] = y[:, lanes]
+            chip_y, chip_x = divmod(2 * block + half, side)
+            along_x, along_y = chip_x * size + chip_y * pair, chip_y * size + chip_x * pair
+            start = pl.multiple_of(along_x + spot_ref[2] * (along_y - along_x), 8)
+            out_ref[pl.ds(start, LANES), :] = x_ref[2 * block + half]
+            out_ref[pl.ds(start + LANES, LANES), :] = y[:, lanes]
     masses = jnp.concatenate(masses, axis=0)
-    for tile in range(out_ref.shape[0]):
-        out_ref[tile, LANES:] = masses
+    for block in range(side):
+        out_ref[block * size + side * pair : (block + 1) * size] = masses
+
+
+def cross_body(in_ref, out_ref):
+    side = out_ref.shape[0]
+    pair = 2 * LANES
+    total = jnp.sum(in_ref[...], axis=0)
+    for block in range(side):
+        out_ref[block, :pair] = total[block * pair : (block + 1) * pair]
+        out_ref[block, pair:] = total[side * pair :]
 
 
 def turn_body(in_ref, out_ref):
-    tiles = in_ref.shape[0]
-    size = 8 + tiles
     total = jnp.sum(in_ref[...], axis=0)
-    y = total[:LANES].T
+    x, y, masses = total[:LANES].T, total[LANES : 2 * LANES].T, total[2 * LANES :]
+    size = 16 + masses.shape[0]
     for layer in range(out_ref.shape[0] // size):
         base = layer * size
-        out_ref[base : base + 8] = y[layer * 8 : layer * 8 + 8]
-        out_ref[base + 8 : base + size] = total[LANES:]
+        out_ref[base : base + 8] = x[layer * 8 : layer * 8 + 8]
+        out_ref[base + 8 : base + 16] = y[layer * 8 : layer * 8 + 8]
+        out_ref[base + 16 : base + size] = masses
 
 
 def proto_grads(rows, e_ref, first_ref, second_ref, scale_ref, shares, masses, clips_ref):
@@ -305,12 +302,12 @@
     return acc * 10.0
 
 
-def other_grads_body(e_ref, first_ref, second_ref, scale_ref, totals_ref, in_ref, clips_ref, out_ref, y_ref, inverse_ref):
+def other_grads_body(e_ref, first_ref, second_ref, scale_ref, totals_ref, in_ref, clips_ref, out_ref, sums_ref, inverse_ref):
     n_rows = out_ref.shape[0]
     tiles = totals_ref.shape[0]
-    total = summed_lines(in_ref, 8 + tiles)
-    y_ref[...] = total[:8]
-    masses = 1.0 / total[8:]
+    total = summed_lines(in_ref, 16 + tiles)
+    sums_ref[...] = total[:16]
+    masses = 1.0 / total[16:]
     shares = 1.0 / totals_ref[...]
     inverse_ref[:tiles] = masses
     inverse_ref[tiles:] = shares
@@ -325,20 +322,20 @@
     return jnp.sum(jnp.where(lane == layer * 8 + line, values, 0.0), axis=1, keepdims=True)
 
 
-def own_grads_body(spot_ref, e_ref, first_ref, second_ref, scale_ref, inverse_ref, x_ref, y_ref, clips_ref,
-                   embeddings_ref, clip_ref, out_ref):
+def own_grads_body(e_ref, first_ref, second_ref, scale_ref, inverse_ref, clips_ref, out_ref):
     tiles = inverse_ref.shape[0] // 2
     rows = slice(0, out_ref.shape[0])
     out_ref[...] = proto_grads(
         rows, e_ref, first_ref, second_ref, scale_ref, inverse_ref[tiles:], inverse_ref[:tiles], clips_ref
     )
+
+
+def finish_body(spot_ref, inverse_ref, sums_ref, embeddings_ref, protos_ref, own_ref, other_ref, clip_ref, proto_ref):
+    tiles = inverse_ref.shape[0] // 2
     own_mass = own_values(inverse_ref, spot_ref[0], spot_ref[1])
     own_share = own_values(inverse_ref, spot_ref[0] + tiles, spot_ref[1])
-    clip_ref[...] = finish_rows(embeddings_ref[...], 10.0 * (x_ref[...] * own_share - y_ref[...] * own_mass))
-
-
-def finish_body(protos_ref, own_ref, other_ref, out_ref):
-    out_ref[...] = finish_rows(protos_ref[...], own_ref[...] + other_ref[...])
+    clip_ref[...] = finish_rows(embeddings_ref[...], 10.0 * (sums_ref[:8] * own_share - sums_ref[8:] * own_mass))
+    proto_ref[...] = finish_rows(protos_ref[...], own_ref[...] + other_ref[...])
 
 
 def local(embeddings, prototypes, partner):
@@ -350,6 +347,9 @@
     here, n_here = tiles * LANES, 2 * own_protos
     where = lax.axis_index("proto")
     same_core = [[2 * i + c for i in range(tiles)] for c in range(2)]
+    side = int(tiles**0.5)
+    rows_x = [[[2 * (side * y + x) + c for x in range(side)] for y in range(side)] for c in range(2)]
+    rows_y = [[[2 * (side * y + x) + c for y in range(side)] for x in range(side)] for c in range(2)]
     cores = [(i, i ^ 1) for i in range(n_proto)]
     smem = pl.BlockSpec(memory_space=pltpu.SMEM)
     vmem = pl.BlockSpec(memory_space=pltpu.VMEM)
@@ -360,22 +360,17 @@
     def over_chips(blocks):
         return lax.all_to_all(blocks, "proto", 0, 0, tiled=True, axis_index_groups=same_core)
 
+    def over_ring(blocks, groups):
+        return lax.all_to_all(blocks, "proto", 0, 0, tiled=True, axis_index_groups=groups)
+
     def over_layers(lines):
         blocks = lax.all_to_all(lines.reshape(n_batch, 1, -1), "batch", 0, 0, tiled=True)
         return blocks.reshape(lines.shape)
 
     spot = jnp.stack([where >> 1, lax.axis_index("batch"), where & 1])
     partner = partner.reshape(-1, LANES)
-    sent = call(
-        functools.partial(send_body, n_proto),
-        f32(n_batch * (rows + partner.shape[0]), LANES),
-        in_specs=[pl.BlockSpec(memory_space=pltpu.HBM)] * 2,
-        scratch_shapes=[
-            pltpu.VMEM(embeddings.shape, jnp.float32),
-            pltpu.VMEM(partner.shape, jnp.int32),
-            pltpu.SemaphoreType.DMA((2,)),
-        ],
-    )(embeddings, partner)
+    raw = jnp.concatenate([embeddings, partner.astype(jnp.float32)], axis=0)
+    sent = call(functools.partial(send_body, n_proto, rows), f32(n_batch * raw.shape[0], LANES))(raw)
     sent, held, spot = lax.optimization_barrier((sent, prototypes, spot))
     column = over_layers(sent)
     own_units = call(units_body, f32(own_protos, features))(held)
@@ -408,30 +403,31 @@
         scratch_shapes=[mates],
     )(late, spot, unit_protos, own_clips, received)
     other, first_e = lax.optimization_barrier((swap(part), first_e))
-    blocks = call(functools.partial(rows_second_body, protos), f32(tiles, tiles + LANES + 8, LANES))(
-        e, part, other, x, own_total
-    )
-    lines, totals = call(spread_second_body, (f32(n_batch * (tiles + 8), LANES), f32(tiles, LANES)))(over_chips(blocks))
-    part, x = call(functools.partial(cols_second_body, clips), (f32(n_here, LANES), f32(rows, features)))(
-        e, over_layers(lines)
-    )
+    blocks = call(functools.partial(rows_second_body, protos), f32(tiles, tiles + 8, LANES))(e, part, other, own_total)
+    lines, totals = call(spread_second_body, (f32(n_batch * tiles, LANES), f32(tiles, LANES)))(over_chips(blocks))
+    part = call(functools.partial(cols_second_body, clips), f32(n_here, LANES))(e, over_layers(lines))
     part, late = lax.optimization_barrier((part, late))
     second_e = call(
         mates_second_body, f32(n_here, here // 2), in_specs=[smem, smem, vmem, vmem], scratch_shapes=[mates]
     )(late, spot, unit_protos, table)
     other, second_e = lax.optimization_barrier((swap(part), second_e))
-    blocks, scale = call(
-        functools.partial(mates_rows_body, protos), (f32(tiles, features + tiles, LANES), f32(n_here, LANES))
-    )(first_e, second_e, part, other, unit_protos)
-    lines = call(turn_body, f32(n_batch * (8 + tiles), LANES))(over_chips(blocks))
-    other_grads, y, inverse = call(
-        other_grads_body, (f32(own_protos, features), f32(rows, features), f32(2 * tiles, LANES))
+    size = side * 2 * features + tiles
+    lines, scale = call(
+        functools.partial(mates_rows_body, protos, side),
+        (f32(side * size, LANES), f32(n_here, LANES)),
+        in_specs=[smem] + [vmem] * 6,
+    )(spot, first_e, second_e, part, other, unit_protos, x)
+    blocks = over_ring(lines.reshape(side, size, LANES), rows_x[0] + rows_y[1])
+    blocks = call(cross_body, f32(side, 2 * features + tiles, LANES))(blocks)
+    blocks = over_ring(blocks, rows_y[0] + rows_x[1])
+    lines = call(turn_body, f32(n_batch * (2 * rows + tiles), LANES))(blocks)
+    other_grads, sums, inverse = call(
+        other_grads_body, (f32(own_protos, features), f32(2 * rows, features), f32(2 * tiles, LANES))
     )(e, first_e, second_e, scale, totals, over_layers(lines), own_clips)
-    grad_embeddings, own_grads = call(
-        own_grads_body, (f32(rows, features), f32(own_protos, features)), in_specs=[smem] + [vmem] * 9
-    )(spot, e, first_e, second_e, scale, inverse, x, y, own_clips, embeddings)
-    grad_prototypes = call(finish_body, f32(own_protos, features))(prototypes, own_grads, swap(other_grads))
-    return (grad_embeddings, grad_prototypes)
+    own_grads = call(own_grads_body, f32(own_protos, features))(e, first_e, second_e, scale, inverse, own_clips)
+    return call(
+        finish_body, (f32(rows, features), f32(own_protos, features)), in_specs=[smem] + [vmem] * 6
+    )(spot, inverse, sums, embeddings, prototypes, own_grads, swap(other_grads))
 
 
 def solution(mesh):

time: 197 us -> 192 us (0.975)
  blocking collectives: 123 us -> 118 us
    all_to_all x4 -> x3, blocking collectives: 74 us -> 41.4 us  [over_chips(): lax.all_to_all(blocks, 'proto', 0, 0, tiled=True, axis_index_groups=same_...]
    all_to_all x0 -> x2, blocking collectives: none -> 27.8 us  [over_ring(): lax.all_to_all(blocks, 'proto', 0, 0, tiled=True, axis_index_groups=groups)]
    pallas_call x9 -> x10, Pallas kernels: 7.5 us -> 7.36 us  [the longest x1 2.05 us: local(): call(functools.partial(mates_rows_body, protos, side), (f32(side * size,...]
where the time goes in v4:
time: 192 us; the launch traced here: 191 us
  blocking collectives  118 us (61%)
  starting transfers between devices  44.6 us (23%)
  Pallas kernels  16.3 us (8%)
  waiting for transfers between devices  9.45 us (5%)
    all_to_all x3, blocking collectives, over_layers(): lax.all_to_all(lines.reshape(n_batch, 1, -1), 'batch', 0, 0, tiled=True)  48.4 us
    all_to_all x3, blocking collectives, over_chips(): lax.all_to_all(blocks, 'proto', 0, 0, tiled=True, axis_index_groups=same_...  41.4 us
    ppermute x5, starting transfers between devices, swap(): return lax.ppermute(values, 'proto', cores)  28.9 us
    all_to_all x2, blocking collectives, over_ring(): lax.all_to_all(blocks, 'proto', 0, 0, tiled=True, axis_index_groups=groups)  27.8 us
    all_to_all x1, starting transfers between devices, over_layers(): lax.all_to_all(lines.reshape(n_batch, 1, -1), 'batch', 0, 0, tiled=True)  15.7 us
    all_to_all x1, waiting for transfers between devices, over_layers(): lax.all_to_all(lines.reshape(n_batch, 1, -1), 'batch', 0, 0, tiled=True)  6.88 us
  transfers between devices with their start and end apart: 6, of which 3 were waited for; matrix products, arithmetic and copies ran while one was open for 0% of the time, Pallas kernels for 4%

profile of v4, /device:TPU:1, one launch (start us, length us, event | category | flops | bytes accessed | tf_op | source)
XLA Modules:
  0.0 191.1 jit_solution(9774853718619068846)
XLA Ops:
  0.6 0.7 convert_bitcast_fusion
  1.3 0.7 pad_maximum_fusion.1.in_ref
  2.0 0.7 shard_map.50
  2.7 0.1 pad_add_fusion.spot_ref
  2.8 15.7 %all-to-all-start = ((f32[16,1,1280]{2,1,0:T(1,128)}), f32[16,1,1280]{2,1,0:T(1,128)S(1)}, u32[]{:S(2)}, u32[]{:S(2)}) async-start(f32[16,1,1280]{2,1,0:T(1,128)} %bitcast.4), calls=%async_computation | async-start | bytes 163840 | tf_op jit(solution)/shard_map/all_to_all | solution.py:367
  18.6 0.0 copy-start
  18.6 0.9 copy-done
  19.5 0.1 shard_map.51
  19.6 2.9 %collective-permute-start = (f32[256,128]{1,0:T(8,128)S(1)}, f32[256,128]{1,0:T(8,128)S(1)}, u32[]{:S(2)}, u32[]{:S(2)}) collective-permute-start(f32[256,128]{1,0:T(8,128)S(1)} %shard_map.51), channel_id=1, source_target_pairs={{0,1},{1,0},{2,3},{3,2},{4,5},{5,4},{6,7},{7,6},{8,9},{9,8},{10,11... | collective-permute-start | bytes 393224 | tf_op jit(solution)/shard_map/ppermute | solution.py:358
  22.5 1.0 collective-permute-done
  23.5 6.9 %all-to-all-done = f32[16,1,1280]{2,1,0:T(1,128)S(1)} async-done(((f32[16,1,1280]{2,1,0:T(1,128)}), f32[16,1,1280]{2,1,0:T(1,128)S(1)}, u32[]{:S(2)}, u32[]{:S(2)}) %all-to-all-start) | async-done | bytes 81952 | tf_op jit(solution)/shard_map/all_to_all | solution.py:367
  30.4 0.6 shard_map.52
  31.0 21.2 %all_to_all.45 = f32[16,128,128]{2,1,0:T(8,128)S(1)} all-to-all(f32[16,128,128]{2,1,0:T(8,128)S(1)} %get-tuple-element.38), channel_id=1, replica_groups={{0,2,4,6,8,10,12,14,16,18,20,22,24,26,28,30},{1,3,5,7,9,11,13,15,17,19,..., dimensions={0} | all-to-all | bytes 2097152 | tf_op jit(solution)/shard_map/all_to_all | solution.py:361
  52.2 1.4 shard_map.53
  53.6 5.5 %collective-permute-start.1 = (f32[2560,128]{1,0:T(8,128)S(1)}, f32[2560,128]{1,0:T(8,128)S(1)}, u32[]{:S(2)}, u32[]{:S(2)}) collective-permute-start(f32[2560,128]{1,0:T(8,128)S(1)} %get-tuple-element.40.own_ref), channel_id=1, source_target_pairs={{0,1},{1,0},{2,3},{3,2},{4,5},{5,4},{6,7},{7,6},{8,9},{9,8},{10,11... | collective-permute-start | bytes 3932168 | tf_op jit(solution)/shard_map/ppermute | solution.py:358
  59.1 1.0 shard_map.54.x_ref
  60.1 1.6 collective-permute-done.1.other_ref
  61.7 0.6 shard_map.55
  62.3 9.8 %all_to_all.46.in_ref = f32[16,24,128]{2,1,0:T(8,128)S(1)} all-to-all(f32[16,24,128]{2,1,0:T(8,128)S(1)} %shard_map.55), channel_id=1, replica_groups={{0,2,4,6,8,10,12,14,16,18,20,22,24,26,28,30},{1,3,5,7,9,11,13,15,17,19,..., dimensions={0} | all-to-all | bytes 393216 | tf_op jit(solution)/shard_map/all_to_all | solution.py:361
  72.1 16.7 %all_to_all.47 = f32[16,1,2176]{2,1,0:T(1,128)S(1)} all-to-all(f32[16,1,2176]{2,1,0:T(1,128)S(1)} %bitcast.24), channel_id=1, replica_groups=mesh['batch'=16,'proto'=32] {'batch'}, dimensions={0} | all-to-all | bytes 278528 | tf_op jit(solution)/shard_map/all_to_all | solution.py:367
  88.8 0.4 shard_map.57
  89.2 6.1 %collective-permute-start.2 = (f32[512,128]{1,0:T(8,128)S(1)}, f32[512,128]{1,0:T(8,128)S(1)}, u32[]{:S(2)}, u32[]{:S(2)}) collective-permute-start(f32[512,128]{1,0:T(8,128)S(1)} %get-tuple-element.45.own_ref), channel_id=1, source_target_pairs={{0,1},{1,0},{2,3},{3,2},{4,5},{5,4},{6,7},{7,6},{8,9},{9,8},{10,11... | collective-permute-start | bytes 786440 | tf_op jit(solution)/shard_map/ppermute | solution.py:358
  95.3 2.4 %shard_map.58 = (f32[512,1024]{1,0:T(8,128)S(1)}, f32[4096,128]{1,0:T(8,128)S(1)}) custom-call(s32[4096]{0:T(1024)S(1)} %bitcast.28, s32[3]{0:T(128)S(1)} %pad_add_fusion.spot_ref, f32[512,128]{1,0:T(8,128)S(1)} %pad_maximum_fusion.protos_ref, f32[2048,128]{1,0:T(8,128)S(1)} %bitcast.17, f32[2560,128]{1,0:T(8,128)S(1)} %collective-permute-done.1.other_ref), custom_call_target="tpu_custom_call" | custom-call | tf_op jit(solution)/shard_map/pallas_call | solution.py:399
  97.8 0.0 collective-permute-done.2.other_ref
  97.8 0.5 shard_map.59
  98.3 10.4 %all_to_all.48.in_ref = f32[16,24,128]{2,1,0:T(8,128)S(1)} all-to-all(f32[16,24,128]{2,1,0:T(8,128)S(1)} %shard_map.59), channel_id=1, replica_groups={{0,2,4,6,8,10,12,14,16,18,20,22,24,26,28,30},{1,3,5,7,9,11,13,15,17,19,..., dimensions={0} | all-to-all | bytes 393216 | tf_op jit(solution)/shard_map/all_to_all | solution.py:361
  108.8 15.5 %all_to_all.49 = f32[16,1,2048]{2,1,0:T(1,128)S(1)} all-to-all(f32[16,1,2048]{2,1,0:T(1,128)S(1)} %bitcast.27), channel_id=1, replica_groups=mesh['batch'=16,'proto'=32] {'batch'}, dimensions={0} | all-to-all | bytes 262144 | tf_op jit(solution)/shard_map/all_to_all | solution.py:367
  124.3 0.4 shard_map.61.own_ref
  124.7 5.5 %collective-permute-start.3 = (f32[512,128]{1,0:T(8,128)S(1)}, f32[512,128]{1,0:T(8,128)S(1)}, u32[]{:S(2)}, u32[]{:S(2)}) collective-permute-start(f32[512,128]{1,0:T(8,128)S(1)} %shard_map.61.own_ref), channel_id=1, source_target_pairs={{0,1},{1,0},{2,3},{3,2},{4,5},{5,4},{6,7},{7,6},{8,9},{9,8},{10,11... | collective-permute-start | bytes 786440 | tf_op jit(solution)/shard_map/ppermute | solution.py:358
  130.2 2.3 %shard_map.62.second_ref = f32[512,1024]{1,0:T(8,128)S(1)} custom-call(s32[4096]{0:T(1024)S(1)} %bitcast.29, s32[3]{0:T(128)S(1)} %pad_add_fusion.spot_ref, f32[512,128]{1,0:T(8,128)S(1)} %pad_maximum_fusion.protos_ref, f32[4096,128]{1,0:T(8,128)S(1)} %get-tuple-element.54.table_ref), custom_call_target="tpu_custom_call" | custom-call | tf_op jit(solution)/shard_map/pallas_call | solution.py:410
  132.5 0.0 collective-permute-done.3.other_ref
  132.5 2.0 %shard_map.63 = (f32[4160,128]{1,0:T(8,128)S(1)}, f32[512,128]{1,0:T(8,128)S(1)}) custom-call(s32[3]{0:T(128)S(1)} %pad_add_fusion.spot_ref, f32[512,1024]{1,0:T(8,128)S(1)} %get-tuple-element.48.first_ref, f32[512,1024]{1,0:T(8,128)S(1)} %shard_map.62.second_ref, f32[512,128]{1,0:T(8,128)S(1)} %shard_map.61.own_ref, ...), custom_call_target="tpu_custom_call" | custom-call | tf_op jit(solution)/shard_map/pallas_call | solution.py:415
  134.6 18.3 %all_to_all.50.in_ref = f32[4,1040,128]{2,1,0:T(8,128)S(1)} all-to-all(f32[4,1040,128]{2,1,0:T(8,128)S(1)} %bitcast.20), channel_id=1, replica_groups={{0,2,4,6},{8,10,12,14},{16,18,20,22},{24,26,28,30},{1,9,17,25},{3,11,19..., dimensions={0} | all-to-all | bytes 4259840 | tf_op jit(solution)/shard_map/all_to_all | solution.py:364
  152.8 0.1 shard_map.64
  152.9 9.5 %all_to_all.51.in_ref = f32[4,272,128]{2,1,0:T(8,128)S(1)} all-to-all(f32[4,272,128]{2,1,0:T(8,128)S(1)} %shard_map.64), channel_id=1, replica_groups={{0,8,16,24},{2,10,18,26},{4,12,20,28},{6,14,22,30},{1,3,5,7},{9,11,13,1..., dimensions={0} | all-to-all | bytes 1114112 | tf_op jit(solution)/shard_map/all_to_all | solution.py:364
  162.5 0.1 shard_map.65
  162.6 16.2 %all_to_all.52 = f32[16,1,4096]{2,1,0:T(1,128)S(1)} all-to-all(f32[16,1,4096]{2,1,0:T(1,128)S(1)} %bitcast.22), channel_id=1, replica_groups=mesh['batch'=16,'proto'=32] {'batch'}, dimensions={0} | all-to-all | bytes 524288 | tf_op jit(solution)/shard_map/all_to_all | solution.py:367
  178.8 1.0 shard_map.66
  179.8 8.9 %collective-permute-start.4 = (f32[256,128]{1,0:T(8,128)S(1)}, f32[256,128]{1,0:T(8,128)S(1)}, u32[]{:S(2)}, u32[]{:S(2)}) collective-permute-start(f32[256,128]{1,0:T(8,128)S(1)} %get-tuple-element.63), channel_id=1, source_target_pairs={{0,1},{1,0},{2,3},{3,2},{4,5},{5,4},{6,7},{7,6},{8,9},{9,8},{10,11... | collective-permute-start | bytes 393224 | tf_op jit(solution)/shard_map/ppermute | solution.py:358
  188.7 0.0 copy-start.1
  188.7 0.0 copy-start.2
  188.7 0.9 shard_map.67.own_ref
  189.6 0.0 collective-permute-done.4.other_ref
  189.6 0.0 copy-done.1
  189.7 0.0 copy-done.2
  189.7 1.4 shard_map.68
  (3 shorter events, 0.1 us)
Async XLA Ops:
  2.8 27.5 %all-to-all-start = ((f32[16,1,1280]{2,1,0:T(1,128)}), f32[16,1,1280]{2,1,0:T(1,128)S(1)}, u32[]{:S(2)}, u32[]{:S(2)}) async-start(f32[16,1,1280]{2,1,0:T(1,128)} %bitcast.4), calls=%async_computation | async-start | bytes 163840 | tf_op jit(solution)/shard_map/all_to_all | solution.py:367
  18.6 0.9 copy-start
  19.6 3.8 %collective-permute-start = (f32[256,128]{1,0:T(8,128)S(1)}, f32[256,128]{1,0:T(8,128)S(1)}, u32[]{:S(2)}, u32[]{:S(2)}) collective-permute-start(f32[256,128]{1,0:T(8,128)S(1)} %shard_map.51), channel_id=1, source_target_pairs={{0,1},{1,0},{2,3},{3,2},{4,5},{5,4},{6,7},{7,6},{8,9},{9,8},{10,11... | collective-permute-start | bytes 393224 | tf_op jit(solution)/shard_map/ppermute | solution.py:358
  53.6 8.1 %collective-permute-start.1 = (f32[2560,128]{1,0:T(8,128)S(1)}, f32[2560,128]{1,0:T(8,128)S(1)}, u32[]{:S(2)}, u32[]{:S(2)}) collective-permute-start(f32[2560,128]{1,0:T(8,128)S(1)} %get-tuple-element.40.own_ref), channel_id=1, source_target_pairs={{0,1},{1,0},{2,3},{3,2},{4,5},{5,4},{6,7},{7,6},{8,9},{9,8},{10,11... | collective-permute-start | bytes 3932168 | tf_op jit(solution)/shard_map/ppermute | solution.py:358
  89.2 8.6 %collective-permute-start.2 = (f32[512,128]{1,0:T(8,128)S(1)}, f32[512,128]{1,0:T(8,128)S(1)}, u32[]{:S(2)}, u32[]{:S(2)}) collective-permute-start(f32[512,128]{1,0:T(8,128)S(1)} %get-tuple-element.45.own_ref), channel_id=1, source_target_pairs={{0,1},{1,0},{2,3},{3,2},{4,5},{5,4},{6,7},{7,6},{8,9},{9,8},{10,11... | collective-permute-start | bytes 786440 | tf_op jit(solution)/shard_map/ppermute | solution.py:358
  124.7 7.8 %collective-permute-start.3 = (f32[512,128]{1,0:T(8,128)S(1)}, f32[512,128]{1,0:T(8,128)S(1)}, u32[]{:S(2)}, u32[]{:S(2)}) collective-permute-start(f32[512,128]{1,0:T(8,128)S(1)} %shard_map.61.own_ref), channel_id=1, source_target_pairs={{0,1},{1,0},{2,3},{3,2},{4,5},{5,4},{6,7},{7,6},{8,9},{9,8},{10,11... | collective-permute-start | bytes 786440 | tf_op jit(solution)/shard_map/ppermute | solution.py:358
  179.8 9.8 %collective-permute-start.4 = (f32[256,128]{1,0:T(8,128)S(1)}, f32[256,128]{1,0:T(8,128)S(1)}, u32[]{:S(2)}, u32[]{:S(2)}) collective-permute-start(f32[256,128]{1,0:T(8,128)S(1)} %get-tuple-element.63), channel_id=1, source_target_pairs={{0,1},{1,0},{2,3},{3,2},{4,5},{5,4},{6,7},{7,6},{8,9},{9,8},{10,11... | collective-permute-start | bytes 393224 | tf_op jit(solution)/shard_map/ppermute | solution.py:358
  188.7 1.0 copy-start.1
  188.7 1.0 copy-start.2

commit v5 on v4

--- a/solution.py
+++ b/solution.py
@@ -82,24 +82,33 @@
     return both[:LANES] + both[LANES:] + dot(turned[:LANES], low)
 
 
-def pulls_body(protos_ref, e_ref, x_ref):
+def ring_start(tile, side, size):
+    return tile // side * size + tile % side * 2 * LANES
+
+
+def pulls_body(side, protos_ref, e_ref, out_ref):
     turned = turned_protos(protos_ref)
+    size = out_ref.shape[0] // side
     for block in range(e_ref.shape[1] // PAIR):
         x = times_protos(turned, e_ref[:, block * PAIR : (block + 1) * PAIR])
         for half in range(2):
-            x_ref[2 * block + half] = x[:, half * LANES : (half + 1) * LANES]
+            start = ring_start(2 * block + half, side, size)
+            out_ref[start : start + LANES] = x[:, half * LANES : (half + 1) * LANES]
 
 
 def mates_of(part, index_ref, spot_ref, protos_ref, table_ref, e_ref, mate_ref):
     pair = jnp.concatenate(split(protos_ref[...]), axis=1)
     blocks = e_ref.shape[1] // PAIR
     tiles = 4 * blocks
-    first = spot_ref[2] * 8
+    core, side = spot_ref[2], int(tiles**0.5)
     for block in range(blocks):
         slot = block % 2
         for half in range(2):
+            tile = 2 * (part * blocks + block) + half
+            crossed = tile % side * side + tile // side
+            first = crossed * 16 + core * ((tile - crossed) * 16 + 8)
             for z in range(LANES // 8):
-                start = first + (z * tiles + 2 * (part * blocks + block) + half) * 16
+                start = first + z * tiles * 16
                 for r in range(8):
                     row = half * LANES + z * 8 + r
                     mate_ref[slot, row : row + 1, :] = table_ref[pl.ds(index_ref[start + r], 1), :]
@@ -139,7 +148,10 @@
     partner = in_ref[rows:].astype(jnp.int32)
     line = partner & (rows - 1)
     slot = (partner // rows) & (n_proto - 1)
-    place = (slot & 1) * (n_proto // 2) + (slot >> 1)
+    side = int((n_proto // 2) ** 0.5)
+    chip, core = slot >> 1, slot & 1
+    tile = jnp.where(core > 0, chip, (chip & (side - 1)) * side + chip // side)
+    place = core * (n_proto // 2) + tile
     place = place * LANES + partner // (rows * n_proto) * rows + line
     block = jnp.concatenate([values * inverse_norms(values), place.astype(jnp.float32)], axis=0)
     for layer in range(out_ref.shape[0] // block.shape[0]):
@@ -233,7 +245,7 @@
     weigh_columns(e_ref, 1.0 / (clips * summed_lines(in_ref, e_ref.shape[1] // LANES)), part_ref)
 
 
-def mates_rows_body(protos, side, spot_ref, first_ref, second_ref, own_ref, other_ref, protos_ref, x_ref, out_ref, scale_ref):
+def mates_rows_body(protos, side, first_ref, second_ref, own_ref, other_ref, protos_ref, _, out_ref, scale_ref):
     size = out_ref.shape[0] // side
     pair = 2 * LANES
     scale = column_scale(own_ref, other_ref, protos_ref.shape[0], protos)
@@ -252,11 +264,8 @@
         for half in range(2):
             lanes = slice(half * LANES, (half + 1) * LANES)
             masses.append(mass[:, lanes])
-            chip_y, chip_x = divmod(2 * block + half, side)
-            along_x, along_y = chip_x * size + chip_y * pair, chip_y * size + chip_x * pair
-            start = pl.multiple_of(along_x + spot_ref[2] * (along_y - along_x), 8)
-            out_ref[pl.ds(start, LANES), :] = x_ref[2 * block + half]
-            out_ref[pl.ds(start + LANES, LANES), :] = y[:, lanes]
+            start = ring_start(2 * block + half, side, size) + LANES
+            out_ref[start : start + LANES] = y[:, lanes]
     masses = jnp.concatenate(masses, axis=0)
     for block in range(side):
         out_ref[block * size + side * pair : (block + 1) * size] = masses
@@ -346,8 +355,9 @@
     clips, protos = float(rows * n_batch * n_proto), float(own_protos * n_batch * n_proto)
     here, n_here = tiles * LANES, 2 * own_protos
     where = lax.axis_index("proto")
-    same_core = [[2 * i + c for i in range(tiles)] for c in range(2)]
     side = int(tiles**0.5)
+    crossed = [tile % side * side + tile // side for tile in range(tiles)]
+    same_core = [[2 * chip for chip in crossed], [2 * chip + 1 for chip in range(tiles)]]
     rows_x = [[[2 * (side * y + x) + c for x in range(side)] for y in range(side)] for c in range(2)]
     rows_y = [[[2 * (side * y + x) + c for y in range(side)] for x in range(side)] for c in range(2)]
     cores = [(i, i ^ 1) for i in range(n_proto)]
@@ -367,7 +377,9 @@
         blocks = lax.all_to_all(lines.reshape(n_batch, 1, -1), "batch", 0, 0, tiled=True)
         return blocks.reshape(lines.shape)
 
-    spot = jnp.stack([where >> 1, lax.axis_index("batch"), where & 1])
+    chip, core = where >> 1, where & 1
+    tile = jnp.where(core > 0, chip, chip % side * side + chip // side)
+    spot = jnp.stack([tile, lax.axis_index("batch"), core])
     partner = partner.reshape(-1, LANES)
     raw = jnp.concatenate([embeddings, partner.astype(jnp.float32)], axis=0)
     sent = call(functools.partial(send_body, n_proto, rows), f32(n_batch * raw.shape[0], LANES))(raw)
@@ -386,8 +398,9 @@
     e, totals, bundle = call(
         scores_body, (f32(n_here, here), f32(tiles, LANES), f32(n_here + here, features))
     )(unit_protos, own_clips)
-    x = call(pulls_body, f32(tiles, features, LANES))(unit_protos, e)
-    received, x = lax.optimization_barrier((swap(bundle), x))
+    size = side * 2 * features + tiles
+    pulls = call(functools.partial(pulls_body, side), f32(side * size, LANES))(unit_protos, e)
+    received, pulls = lax.optimization_barrier((swap(bundle), pulls))
     blocks = call(functools.partial(rows_first_body, protos), f32(tiles, tiles + 8, LANES))(e, bundle, received, totals)
     lines = call(spread_first_body, f32(n_batch * (tiles + 1), LANES))(over_chips(blocks))
     part, own_total = call(functools.partial(cols_first_body, clips), (f32(n_here, LANES), f32(8, LANES)))(
@@ -411,12 +424,11 @@
         mates_second_body, f32(n_here, here // 2), in_specs=[smem, smem, vmem, vmem], scratch_shapes=[mates]
     )(late, spot, unit_protos, table)
     other, second_e = lax.optimization_barrier((swap(part), second_e))
-    size = side * 2 * features + tiles
     lines, scale = call(
         functools.partial(mates_rows_body, protos, side),
         (f32(side * size, LANES), f32(n_here, LANES)),
-        in_specs=[smem] + [vmem] * 6,
-    )(spot, first_e, second_e, part, other, unit_protos, x)
+        input_output_aliases={5: 0},
+    )(first_e, second_e, part, other, unit_protos, pulls)
     blocks = over_ring(lines.reshape(side, size, LANES), rows_x[0] + rows_y[1])
     blocks = call(cross_body, f32(side, 2 * features + tiles, LANES))(blocks)
     blocks = over_ring(blocks, rows_y[0] + rows_x[1])

time: 192 us -> 191 us (level)
  no operation moved by 1% of the time
where the time goes in v5:
time: 191 us
  blocking collectives  118 us (62%)
  starting transfers between devices  44.4 us (23%)
  Pallas kernels  15.5 us (8%)
  waiting for transfers between devices  9.46 us (5%)
    all_to_all x3, blocking collectives, over_layers(): lax.all_to_all(lines.reshape(n_batch, 1, -1), 'batch', 0, 0, tiled=True)  48.2 us
    all_to_all x3, blocking collectives, over_chips(): lax.all_to_all(blocks, 'proto', 0, 0, tiled=True, axis_index_groups=same_...  42.1 us
    ppermute x5, starting transfers between devices, swap(): return lax.ppermute(values, 'proto', cores)  28.7 us
    all_to_all x2, blocking collectives, over_ring(): lax.all_to_all(blocks, 'proto', 0, 0, tiled=True, axis_index_groups=groups)  27.8 us
    all_to_all x1, starting transfers between devices, over_layers(): lax.all_to_all(lines.reshape(n_batch, 1, -1), 'batch', 0, 0, tiled=True)  15.7 us
    all_to_all x1, waiting for transfers between devices, over_layers(): lax.all_to_all(lines.reshape(n_batch, 1, -1), 'batch', 0, 0, tiled=True)  6.88 us
  transfers between devices with their start and end apart: 6, of which 3 were waited for; matrix products, arithmetic and copies ran while one was open for 0% of the time, Pallas kernels for 4%

profile of v5, /device:TPU:1, one launch (start us, length us, event | category | flops | bytes accessed | tf_op | source)
XLA Modules:
  0.0 190.7 jit_solution(6883415141887618648)
XLA Ops:
  0.7 0.7 convert_bitcast_fusion
  1.3 0.7 pad_maximum_fusion.1.in_ref
  2.0 0.7 shard_map.50
  2.8 0.1 pad_add_fusion.spot_ref
  2.8 15.7 %all-to-all-start = ((f32[16,1,1280]{2,1,0:T(1,128)}), f32[16,1,1280]{2,1,0:T(1,128)S(1)}, u32[]{:S(2)}, u32[]{:S(2)}) async-start(f32[16,1,1280]{2,1,0:T(1,128)} %bitcast.4), calls=%async_computation | async-start | bytes 163840 | tf_op jit(solution)/shard_map/all_to_all | solution.py:377
  18.6 0.0 copy-start
  18.6 0.9 copy-done
  19.5 0.1 shard_map.51
  19.6 2.9 %collective-permute-start = (f32[256,128]{1,0:T(8,128)S(1)}, f32[256,128]{1,0:T(8,128)S(1)}, u32[]{:S(2)}, u32[]{:S(2)}) collective-permute-start(f32[256,128]{1,0:T(8,128)S(1)} %shard_map.51), channel_id=1, source_target_pairs={{0,1},{1,0},{2,3},{3,2},{4,5},{5,4},{6,7},{7,6},{8,9},{9,8},{10,11... | collective-permute-start | bytes 393224 | tf_op jit(solution)/shard_map/ppermute | solution.py:368
  22.5 1.0 collective-permute-done
  23.5 6.9 %all-to-all-done = f32[16,1,1280]{2,1,0:T(1,128)S(1)} async-done(((f32[16,1,1280]{2,1,0:T(1,128)}), f32[16,1,1280]{2,1,0:T(1,128)S(1)}, u32[]{:S(2)}, u32[]{:S(2)}) %all-to-all-start) | async-done | bytes 81952 | tf_op jit(solution)/shard_map/all_to_all | solution.py:377
  30.4 0.6 shard_map.52
  31.0 20.9 %all_to_all.45 = f32[16,128,128]{2,1,0:T(8,128)S(1)} all-to-all(f32[16,128,128]{2,1,0:T(8,128)S(1)} %get-tuple-element.38), channel_id=1, replica_groups={{0,8,16,24,2,10,18,26,4,12,20,28,6,14,22,30},{1,3,5,7,9,11,13,15,17,19,..., dimensions={0} | all-to-all | bytes 2097152 | tf_op jit(solution)/shard_map/all_to_all | solution.py:371
  52.0 1.4 shard_map.53
  53.4 5.6 %collective-permute-start.1 = (f32[2560,128]{1,0:T(8,128)S(1)}, f32[2560,128]{1,0:T(8,128)S(1)}, u32[]{:S(2)}, u32[]{:S(2)}) collective-permute-start(f32[2560,128]{1,0:T(8,128)S(1)} %get-tuple-element.40.own_ref), channel_id=1, source_target_pairs={{0,1},{1,0},{2,3},{3,2},{4,5},{5,4},{6,7},{7,6},{8,9},{9,8},{10,11... | collective-permute-start | bytes 3932168 | tf_op jit(solution)/shard_map/ppermute | solution.py:368
  59.0 1.0 shard_map.54._
  60.0 1.6 collective-permute-done.1.other_ref
  61.6 0.6 shard_map.55
  62.2 10.3 %all_to_all.46.in_ref = f32[16,24,128]{2,1,0:T(8,128)S(1)} all-to-all(f32[16,24,128]{2,1,0:T(8,128)S(1)} %shard_map.55), channel_id=1, replica_groups={{0,8,16,24,2,10,18,26,4,12,20,28,6,14,22,30},{1,3,5,7,9,11,13,15,17,19,..., dimensions={0} | all-to-all | bytes 393216 | tf_op jit(solution)/shard_map/all_to_all | solution.py:371
  72.5 16.8 %all_to_all.47 = f32[16,1,2176]{2,1,0:T(1,128)S(1)} all-to-all(f32[16,1,2176]{2,1,0:T(1,128)S(1)} %bitcast.24), channel_id=1, replica_groups=mesh['batch'=16,'proto'=32] {'batch'}, dimensions={0} | all-to-all | bytes 278528 | tf_op jit(solution)/shard_map/all_to_all | solution.py:377
  89.3 0.4 shard_map.57
  89.7 5.9 %collective-permute-start.2 = (f32[512,128]{1,0:T(8,128)S(1)}, f32[512,128]{1,0:T(8,128)S(1)}, u32[]{:S(2)}, u32[]{:S(2)}) collective-permute-start(f32[512,128]{1,0:T(8,128)S(1)} %get-tuple-element.45.own_ref), channel_id=1, source_target_pairs={{0,1},{1,0},{2,3},{3,2},{4,5},{5,4},{6,7},{7,6},{8,9},{9,8},{10,11... | collective-permute-start | bytes 786440 | tf_op jit(solution)/shard_map/ppermute | solution.py:368
  95.6 2.4 %shard_map.58 = (f32[512,1024]{1,0:T(8,128)S(1)}, f32[4096,128]{1,0:T(8,128)S(1)}) custom-call(s32[4096]{0:T(1024)S(1)} %bitcast.28, s32[3]{0:T(128)S(1)} %pad_add_fusion.spot_ref, f32[512,128]{1,0:T(8,128)S(1)} %pad_maximum_fusion.protos_ref, f32[2048,128]{1,0:T(8,128)S(1)} %bitcast.17, f32[2560,128]{1,0:T(8,128)S(1)} %collective-permute-done.1.other_ref), custom_call_target="tpu_custom_call" | custom-call | tf_op jit(solution)/shard_map/pallas_call | solution.py:412
  98.0 0.0 collective-permute-done.2.other_ref
  98.0 0.6 shard_map.59
  98.6 10.9 %all_to_all.48.in_ref = f32[16,24,128]{2,1,0:T(8,128)S(1)} all-to-all(f32[16,24,128]{2,1,0:T(8,128)S(1)} %shard_map.59), channel_id=1, replica_groups={{0,8,16,24,2,10,18,26,4,12,20,28,6,14,22,30},{1,3,5,7,9,11,13,15,17,19,..., dimensions={0} | all-to-all | bytes 393216 | tf_op jit(solution)/shard_map/all_to_all | solution.py:371
  109.5 15.1 %all_to_all.49 = f32[16,1,2048]{2,1,0:T(1,128)S(1)} all-to-all(f32[16,1,2048]{2,1,0:T(1,128)S(1)} %bitcast.27), channel_id=1, replica_groups=mesh['batch'=16,'proto'=32] {'batch'}, dimensions={0} | all-to-all | bytes 262144 | tf_op jit(solution)/shard_map/all_to_all | solution.py:377
  124.7 0.4 shard_map.61.own_ref
  125.1 5.4 %collective-permute-start.3 = (f32[512,128]{1,0:T(8,128)S(1)}, f32[512,128]{1,0:T(8,128)S(1)}, u32[]{:S(2)}, u32[]{:S(2)}) collective-permute-start(f32[512,128]{1,0:T(8,128)S(1)} %shard_map.61.own_ref), channel_id=1, source_target_pairs={{0,1},{1,0},{2,3},{3,2},{4,5},{5,4},{6,7},{7,6},{8,9},{9,8},{10,11... | collective-permute-start | bytes 786440 | tf_op jit(solution)/shard_map/ppermute | solution.py:368
  130.5 2.3 %shard_map.62.second_ref = f32[512,1024]{1,0:T(8,128)S(1)} custom-call(s32[4096]{0:T(1024)S(1)} %bitcast.29, s32[3]{0:T(128)S(1)} %pad_add_fusion.spot_ref, f32[512,128]{1,0:T(8,128)S(1)} %pad_maximum_fusion.protos_ref, f32[4096,128]{1,0:T(8,128)S(1)} %get-tuple-element.54.table_ref), custom_call_target="tpu_custom_call" | custom-call | tf_op jit(solution)/shard_map/pallas_call | solution.py:423
  132.8 0.0 collective-permute-done.3.other_ref
  132.8 1.4 shard_map.63
  134.2 18.3 %all_to_all.50.in_ref = f32[4,1040,128]{2,1,0:T(8,128)S(1)} all-to-all(f32[4,1040,128]{2,1,0:T(8,128)S(1)} %bitcast.20), channel_id=1, replica_groups={{0,2,4,6},{8,10,12,14},{16,18,20,22},{24,26,28,30},{1,9,17,25},{3,11,19..., dimensions={0} | all-to-all | bytes 4259840 | tf_op jit(solution)/shard_map/all_to_all | solution.py:374
  152.5 0.1 shard_map.64
  152.6 9.5 %all_to_all.51.in_ref = f32[4,272,128]{2,1,0:T(8,128)S(1)} all-to-all(f32[4,272,128]{2,1,0:T(8,128)S(1)} %shard_map.64), channel_id=1, replica_groups={{0,8,16,24},{2,10,18,26},{4,12,20,28},{6,14,22,30},{1,3,5,7},{9,11,13,1..., dimensions={0} | all-to-all | bytes 1114112 | tf_op jit(solution)/shard_map/all_to_all | solution.py:374
  162.1 0.1 shard_map.65
  162.2 16.3 %all_to_all.52 = f32[16,1,4096]{2,1,0:T(1,128)S(1)} all-to-all(f32[16,1,4096]{2,1,0:T(1,128)S(1)} %bitcast.22), channel_id=1, replica_groups=mesh['batch'=16,'proto'=32] {'batch'}, dimensions={0} | all-to-all | bytes 524288 | tf_op jit(solution)/shard_map/all_to_all | solution.py:377
  178.5 1.0 shard_map.66
  179.5 8.9 %collective-permute-start.4 = (f32[256,128]{1,0:T(8,128)S(1)}, f32[256,128]{1,0:T(8,128)S(1)}, u32[]{:S(2)}, u32[]{:S(2)}) collective-permute-start(f32[256,128]{1,0:T(8,128)S(1)} %get-tuple-element.63), channel_id=1, source_target_pairs={{0,1},{1,0},{2,3},{3,2},{4,5},{5,4},{6,7},{7,6},{8,9},{9,8},{10,11... | collective-permute-start | bytes 393224 | tf_op jit(solution)/shard_map/ppermute | solution.py:368
  188.3 0.0 copy-start.1
  188.3 0.0 copy-start.2
  188.3 0.9 shard_map.67.own_ref
  189.3 0.0 collective-permute-done.4.other_ref
  189.3 0.0 copy-done.1
  189.3 0.0 copy-done.2
  189.3 1.4 shard_map.68
  (3 shorter events, 0.1 us)
Async XLA Ops:
  2.8 27.5 %all-to-all-start = ((f32[16,1,1280]{2,1,0:T(1,128)}), f32[16,1,1280]{2,1,0:T(1,128)S(1)}, u32[]{:S(2)}, u32[]{:S(2)}) async-start(f32[16,1,1280]{2,1,0:T(1,128)} %bitcast.4), calls=%async_computation | async-start | bytes 163840 | tf_op jit(solution)/shard_map/all_to_all | solution.py:377
  18.6 0.9 copy-start
  19.6 3.8 %collective-permute-start = (f32[256,128]{1,0:T(8,128)S(1)}, f32[256,128]{1,0:T(8,128)S(1)}, u32[]{:S(2)}, u32[]{:S(2)}) collective-permute-start(f32[256,128]{1,0:T(8,128)S(1)} %shard_map.51), channel_id=1, source_target_pairs={{0,1},{1,0},{2,3},{3,2},{4,5},{5,4},{6,7},{7,6},{8,9},{9,8},{10,11... | collective-permute-start | bytes 393224 | tf_op jit(solution)/shard_map/ppermute | solution.py:368
  53.4 8.2 %collective-permute-start.1 = (f32[2560,128]{1,0:T(8,128)S(1)}, f32[2560,128]{1,0:T(8,128)S(1)}, u32[]{:S(2)}, u32[]{:S(2)}) collective-permute-start(f32[2560,128]{1,0:T(8,128)S(1)} %get-tuple-element.40.own_ref), channel_id=1, source_target_pairs={{0,1},{1,0},{2,3},{3,2},{4,5},{5,4},{6,7},{7,6},{8,9},{9,8},{10,11... | collective-permute-start | bytes 3932168 | tf_op jit(solution)/shard_map/ppermute | solution.py:368
  89.7 8.4 %collective-permute-start.2 = (f32[512,128]{1,0:T(8,128)S(1)}, f32[512,128]{1,0:T(8,128)S(1)}, u32[]{:S(2)}, u32[]{:S(2)}) collective-permute-start(f32[512,128]{1,0:T(8,128)S(1)} %get-tuple-element.45.own_ref), channel_id=1, source_target_pairs={{0,1},{1,0},{2,3},{3,2},{4,5},{5,4},{6,7},{7,6},{8,9},{9,8},{10,11... | collective-permute-start | bytes 786440 | tf_op jit(solution)/shard_map/ppermute | solution.py:368
  125.1 7.7 %collective-permute-start.3 = (f32[512,128]{1,0:T(8,128)S(1)}, f32[512,128]{1,0:T(8,128)S(1)}, u32[]{:S(2)}, u32[]{:S(2)}) collective-permute-start(f32[512,128]{1,0:T(8,128)S(1)} %shard_map.61.own_ref), channel_id=1, source_target_pairs={{0,1},{1,0},{2,3},{3,2},{4,5},{5,4},{6,7},{7,6},{8,9},{9,8},{10,11... | collective-permute-start | bytes 786440 | tf_op jit(solution)/shard_map/ppermute | solution.py:368
  179.5 9.8 %collective-permute-start.4 = (f32[256,128]{1,0:T(8,128)S(1)}, f32[256,128]{1,0:T(8,128)S(1)}, u32[]{:S(2)}, u32[]{:S(2)}) collective-permute-start(f32[256,128]{1,0:T(8,128)S(1)} %get-tuple-element.63), channel_id=1, source_target_pairs={{0,1},{1,0},{2,3},{3,2},{4,5},{5,4},{6,7},{7,6},{8,9},{9,8},{10,11... | collective-permute-start | bytes 393224 | tf_op jit(solution)/shard_map/ppermute | solution.py:368
  188.3 1.0 copy-start.1
  188.3 1.0 copy-start.2

commit v6 on v5

--- a/solution.py
+++ b/solution.py
@@ -86,7 +86,8 @@
     return tile // side * size + tile % side * 2 * LANES
 
 
-def pulls_body(side, protos_ref, e_ref, out_ref):
+def pulls_body(side, protos_ref, e_ref, clips_ref, out_ref, table_ref):
+    table_ref[: clips_ref.shape[0]] = clips_ref[...]
     turned = turned_protos(protos_ref)
     size = out_ref.shape[0] // side
     for block in range(e_ref.shape[1] // PAIR):
@@ -115,9 +116,8 @@
         e_ref[:, block * PAIR : (block + 1) * PAIR] = exponents(pair, mate_ref[slot])
 
 
-def mates_first_body(index_ref, spot_ref, protos_ref, own_ref, other_ref, e_ref, table_ref, mate_ref):
-    rows = own_ref.shape[0]
-    table_ref[:rows] = own_ref[...]
+def mates_first_body(index_ref, spot_ref, protos_ref, other_ref, _, e_ref, table_ref, mate_ref):
+    rows = table_ref.shape[0] // 2
     table_ref[rows:] = other_ref[protos_ref.shape[0] :]
     mates_of(0, index_ref, spot_ref, protos_ref, table_ref, e_ref, mate_ref)
 
@@ -339,12 +339,21 @@
     )
 
 
-def finish_body(spot_ref, inverse_ref, sums_ref, embeddings_ref, protos_ref, own_ref, other_ref, clip_ref, proto_ref):
+def finish_body(spot_ref, inverse_ref, sums_ref, embeddings_ref, protos_ref, own_ref, other_ref, clip_ref, proto_ref,
+                clip_held, proto_held, sems):
+    copies = [
+        pltpu.make_async_copy(proto_held, proto_ref, sems.at[0]),
+        pltpu.make_async_copy(clip_held, clip_ref, sems.at[1]),
+    ]
+    proto_held[...] = finish_rows(protos_ref[...], own_ref[...] + other_ref[...])
+    copies[0].start()
     tiles = inverse_ref.shape[0] // 2
     own_mass = own_values(inverse_ref, spot_ref[0], spot_ref[1])
     own_share = own_values(inverse_ref, spot_ref[0] + tiles, spot_ref[1])
-    clip_ref[...] = finish_rows(embeddings_ref[...], 10.0 * (sums_ref[:8] * own_share - sums_ref[8:] * own_mass))
-    proto_ref[...] = finish_rows(protos_ref[...], own_ref[...] + other_ref[...])
+    clip_held[...] = finish_rows(embeddings_ref[...], 10.0 * (sums_ref[:8] * own_share - sums_ref[8:] * own_mass))
+    copies[1].start()
+    for copy in copies:
+        copy.wait()
 
 
 def local(embeddings, prototypes, partner):
@@ -399,8 +408,10 @@
         scores_body, (f32(n_here, here), f32(tiles, LANES), f32(n_here + here, features))
     )(unit_protos, own_clips)
     size = side * 2 * features + tiles
-    pulls = call(functools.partial(pulls_body, side), f32(side * size, LANES))(unit_protos, e)
-    received, pulls = lax.optimization_barrier((swap(bundle), pulls))
+    pulls, table = call(functools.partial(pulls_body, side), (f32(side * size, LANES), f32(2 * here, features)))(
+        unit_protos, e, own_clips
+    )
+    received, pulls, table = lax.optimization_barrier((swap(bundle), pulls, table))
     blocks = call(functools.partial(rows_first_body, protos), f32(tiles, tiles + 8, LANES))(e, bundle, received, totals)
     lines = call(spread_first_body, f32(n_batch * (tiles + 1), LANES))(over_chips(blocks))
     part, own_total = call(functools.partial(cols_first_body, clips), (f32(n_here, LANES), f32(8, LANES)))(
@@ -414,7 +425,8 @@
         (f32(n_here, here // 2), f32(2 * here, features)),
         in_specs=[smem, smem, vmem, vmem, vmem],
         scratch_shapes=[mates],
-    )(late, spot, unit_protos, own_clips, received)
+        input_output_aliases={4: 1},
+    )(late, spot, unit_protos, received, table)
     other, first_e = lax.optimization_barrier((swap(part), first_e))
     blocks = call(functools.partial(rows_second_body, protos), f32(tiles, tiles + 8, LANES))(e, part, other, own_total)
     lines, totals = call(spread_second_body, (f32(n_batch * tiles, LANES), f32(tiles, LANES)))(over_chips(blocks))
@@ -438,7 +450,13 @@
     )(e, first_e, second_e, scale, totals, over_layers(lines), own_clips)
     own_grads = call(own_grads_body, f32(own_protos, features))(e, first_e, second_e, scale, inverse, own_clips)
     return call(
-        finish_body, (f32(rows, features), f32(own_protos, features)), in_specs=[smem] + [vmem] * 6
+        finish_body, (f32(rows, features), f32(own_protos, features)), in_specs=[smem] + [vmem] * 6,
+        out_specs=[pl.BlockSpec(memory_space=pl.ANY)] * 2,
+        scratch_shapes=[
+            pltpu.VMEM((rows, features), jnp.float32),
+            pltpu.VMEM((own_protos, features), jnp.float32),
+            pltpu.SemaphoreType.DMA((2,)),
+        ],
     )(spot, inverse, sums, embeddings, prototypes, own_grads, swap(other_grads))
 
 

time: 191 us -> 191 us (level)
  no operation moved by 1% of the time
where the time goes in v6:
time: 191 us
  blocking collectives  118 us (62%)
  starting transfers between devices  44.4 us (23%)
  Pallas kernels  15.5 us (8%)
  waiting for transfers between devices  9.42 us (5%)
    all_to_all x3, blocking collectives, over_layers(): lax.all_to_all(lines.reshape(n_batch, 1, -1), 'batch', 0, 0, tiled=True)  48.2 us
    all_to_all x3, blocking collectives, over_chips(): lax.all_to_all(blocks, 'proto', 0, 0, tiled=True, axis_index_groups=same_...  42.1 us
    ppermute x5, starting transfers between devices, swap(): return lax.ppermute(values, 'proto', cores)  28.7 us
    all_to_all x2, blocking collectives, over_ring(): lax.all_to_all(blocks, 'proto', 0, 0, tiled=True, axis_index_groups=groups)  27.8 us
    all_to_all x1, starting transfers between devices, over_layers(): lax.all_to_all(lines.reshape(n_batch, 1, -1), 'batch', 0, 0, tiled=True)  15.7 us
    all_to_all x1, waiting for transfers between devices, over_layers(): lax.all_to_all(lines.reshape(n_batch, 1, -1), 'batch', 0, 0, tiled=True)  6.88 us
  transfers between devices with their start and end apart: 6, of which 3 were waited for; matrix products, arithmetic and copies ran while one was open for 0% of the time, Pallas kernels for 4%

profile of v6, /device:TPU:1, one launch (start us, length us, event | category | flops | bytes accessed | tf_op | source)
XLA Modules:
  0.0 190.7 jit_solution(5326743765113604459)
XLA Ops:
  0.7 0.7 convert_bitcast_fusion
  1.3 0.7 pad_maximum_fusion.1.in_ref
  2.0 0.7 shard_map.50
  2.8 0.1 pad_add_fusion.spot_ref
  2.8 15.7 %all-to-all-start = ((f32[16,1,1280]{2,1,0:T(1,128)}), f32[16,1,1280]{2,1,0:T(1,128)S(1)}, u32[]{:S(2)}, u32[]{:S(2)}) async-start(f32[16,1,1280]{2,1,0:T(1,128)} %bitcast.4), calls=%async_computation | async-start | bytes 163840 | tf_op jit(solution)/shard_map/all_to_all | solution.py:386
  18.6 0.0 copy-start
  18.6 0.9 copy-done
  19.5 0.1 shard_map.51
  19.6 2.9 %collective-permute-start = (f32[256,128]{1,0:T(8,128)S(1)}, f32[256,128]{1,0:T(8,128)S(1)}, u32[]{:S(2)}, u32[]{:S(2)}) collective-permute-start(f32[256,128]{1,0:T(8,128)S(1)} %shard_map.51), channel_id=1, source_target_pairs={{0,1},{1,0},{2,3},{3,2},{4,5},{5,4},{6,7},{7,6},{8,9},{9,8},{10,11... | collective-permute-start | bytes 393224 | tf_op jit(solution)/shard_map/ppermute | solution.py:377
  22.5 1.0 collective-permute-done
  23.5 6.9 %all-to-all-done = f32[16,1,1280]{2,1,0:T(1,128)S(1)} async-done(((f32[16,1,1280]{2,1,0:T(1,128)}), f32[16,1,1280]{2,1,0:T(1,128)S(1)}, u32[]{:S(2)}, u32[]{:S(2)}) %all-to-all-start) | async-done | bytes 81952 | tf_op jit(solution)/shard_map/all_to_all | solution.py:386
  30.4 0.6 shard_map.52
  31.0 20.9 %all_to_all.45 = f32[16,128,128]{2,1,0:T(8,128)S(1)} all-to-all(f32[16,128,128]{2,1,0:T(8,128)S(1)} %get-tuple-element.41), channel_id=1, replica_groups={{0,8,16,24,2,10,18,26,4,12,20,28,6,14,22,30},{1,3,5,7,9,11,13,15,17,19,..., dimensions={0} | all-to-all | bytes 2097152 | tf_op jit(solution)/shard_map/all_to_all | solution.py:380
  52.0 1.4 shard_map.53
  53.4 5.6 %collective-permute-start.1 = (f32[2560,128]{1,0:T(8,128)S(1)}, f32[2560,128]{1,0:T(8,128)S(1)}, u32[]{:S(2)}, u32[]{:S(2)}) collective-permute-start(f32[2560,128]{1,0:T(8,128)S(1)} %get-tuple-element.43.own_ref), channel_id=1, source_target_pairs={{0,1},{1,0},{2,3},{3,2},{4,5},{5,4},{6,7},{7,6},{8,9},{9,8},{10,11... | collective-permute-start | bytes 3932168 | tf_op jit(solution)/shard_map/ppermute | solution.py:377
  59.0 1.1 shard_map.54
  60.0 1.6 collective-permute-done.1.other_ref
  61.6 0.5 shard_map.55
  62.2 10.3 %all_to_all.46.in_ref = f32[16,24,128]{2,1,0:T(8,128)S(1)} all-to-all(f32[16,24,128]{2,1,0:T(8,128)S(1)} %shard_map.55), channel_id=1, replica_groups={{0,8,16,24,2,10,18,26,4,12,20,28,6,14,22,30},{1,3,5,7,9,11,13,15,17,19,..., dimensions={0} | all-to-all | bytes 393216 | tf_op jit(solution)/shard_map/all_to_all | solution.py:380
  72.5 16.8 %all_to_all.47 = f32[16,1,2176]{2,1,0:T(1,128)S(1)} all-to-all(f32[16,1,2176]{2,1,0:T(1,128)S(1)} %bitcast.24), channel_id=1, replica_groups=mesh['batch'=16,'proto'=32] {'batch'}, dimensions={0} | all-to-all | bytes 278528 | tf_op jit(solution)/shard_map/all_to_all | solution.py:386
  89.2 0.4 shard_map.57
  89.7 5.9 %collective-permute-start.2 = (f32[512,128]{1,0:T(8,128)S(1)}, f32[512,128]{1,0:T(8,128)S(1)}, u32[]{:S(2)}, u32[]{:S(2)}) collective-permute-start(f32[512,128]{1,0:T(8,128)S(1)} %get-tuple-element.50.own_ref), channel_id=1, source_target_pairs={{0,1},{1,0},{2,3},{3,2},{4,5},{5,4},{6,7},{7,6},{8,9},{9,8},{10,11... | collective-permute-start | bytes 786440 | tf_op jit(solution)/shard_map/ppermute | solution.py:377
  95.6 2.4 %shard_map.58 = (f32[512,1024]{1,0:T(8,128)S(1)}, f32[4096,128]{1,0:T(8,128)S(1)}) custom-call(s32[4096]{0:T(1024)S(1)} %bitcast.28, s32[3]{0:T(128)S(1)} %pad_add_fusion.spot_ref, f32[512,128]{1,0:T(8,128)S(1)} %pad_maximum_fusion.protos_ref, f32[2560,128]{1,0:T(8,128)S(1)} %collective-permute-done.1.other_ref, ...), custom_call_target="tpu_custom_call", output_to_operand_aliasing={{1}: (4, {})} | custom-call | tf_op jit(solution)/shard_map/pallas_call | solution.py:423
  98.0 0.0 collective-permute-done.2.other_ref
  98.0 0.6 shard_map.59
  98.5 10.9 %all_to_all.48.in_ref = f32[16,24,128]{2,1,0:T(8,128)S(1)} all-to-all(f32[16,24,128]{2,1,0:T(8,128)S(1)} %shard_map.59), channel_id=1, replica_groups={{0,8,16,24,2,10,18,26,4,12,20,28,6,14,22,30},{1,3,5,7,9,11,13,15,17,19,..., dimensions={0} | all-to-all | bytes 393216 | tf_op jit(solution)/shard_map/all_to_all | solution.py:380
  109.5 15.2 %all_to_all.49 = f32[16,1,2048]{2,1,0:T(1,128)S(1)} all-to-all(f32[16,1,2048]{2,1,0:T(1,128)S(1)} %bitcast.27), channel_id=1, replica_groups=mesh['batch'=16,'proto'=32] {'batch'}, dimensions={0} | all-to-all | bytes 262144 | tf_op jit(solution)/shard_map/all_to_all | solution.py:386
  124.6 0.4 shard_map.61.own_ref
  125.0 5.4 %collective-permute-start.3 = (f32[512,128]{1,0:T(8,128)S(1)}, f32[512,128]{1,0:T(8,128)S(1)}, u32[]{:S(2)}, u32[]{:S(2)}) collective-permute-start(f32[512,128]{1,0:T(8,128)S(1)} %shard_map.61.own_ref), channel_id=1, source_target_pairs={{0,1},{1,0},{2,3},{3,2},{4,5},{5,4},{6,7},{7,6},{8,9},{9,8},{10,11... | collective-permute-start | bytes 786440 | tf_op jit(solution)/shard_map/ppermute | solution.py:377
  130.5 2.3 %shard_map.62.second_ref = f32[512,1024]{1,0:T(8,128)S(1)} custom-call(s32[4096]{0:T(1024)S(1)} %bitcast.29, s32[3]{0:T(128)S(1)} %pad_add_fusion.spot_ref, f32[512,128]{1,0:T(8,128)S(1)} %pad_maximum_fusion.protos_ref, f32[4096,128]{1,0:T(8,128)S(1)} %get-tuple-element.60.table_ref), custom_call_target="tpu_custom_call" | custom-call | tf_op jit(solution)/shard_map/pallas_call | solution.py:435
  132.8 0.0 collective-permute-done.3.other_ref
  132.8 1.3 shard_map.63
  134.2 18.3 %all_to_all.50.in_ref = f32[4,1040,128]{2,1,0:T(8,128)S(1)} all-to-all(f32[4,1040,128]{2,1,0:T(8,128)S(1)} %bitcast.20), channel_id=1, replica_groups={{0,2,4,6},{8,10,12,14},{16,18,20,22},{24,26,28,30},{1,9,17,25},{3,11,19..., dimensions={0} | all-to-all | bytes 4259840 | tf_op jit(solution)/shard_map/all_to_all | solution.py:383
  152.4 0.1 shard_map.64
  152.5 9.5 %all_to_all.51.in_ref = f32[4,272,128]{2,1,0:T(8,128)S(1)} all-to-all(f32[4,272,128]{2,1,0:T(8,128)S(1)} %shard_map.64), channel_id=1, replica_groups={{0,8,16,24},{2,10,18,26},{4,12,20,28},{6,14,22,30},{1,3,5,7},{9,11,13,1..., dimensions={0} | all-to-all | bytes 1114112 | tf_op jit(solution)/shard_map/all_to_all | solution.py:383
  162.1 0.1 shard_map.65
  162.2 16.3 %all_to_all.52 = f32[16,1,4096]{2,1,0:T(1,128)S(1)} all-to-all(f32[16,1,4096]{2,1,0:T(1,128)S(1)} %bitcast.22), channel_id=1, replica_groups=mesh['batch'=16,'proto'=32] {'batch'}, dimensions={0} | all-to-all | bytes 524288 | tf_op jit(solution)/shard_map/all_to_all | solution.py:386
  178.4 1.0 shard_map.66
  179.4 8.9 %collective-permute-start.4 = (f32[256,128]{1,0:T(8,128)S(1)}, f32[256,128]{1,0:T(8,128)S(1)}, u32[]{:S(2)}, u32[]{:S(2)}) collective-permute-start(f32[256,128]{1,0:T(8,128)S(1)} %get-tuple-element.69), channel_id=1, source_target_pairs={{0,1},{1,0},{2,3},{3,2},{4,5},{5,4},{6,7},{7,6},{8,9},{9,8},{10,11... | collective-permute-start | bytes 393224 | tf_op jit(solution)/shard_map/ppermute | solution.py:377
  188.3 0.0 copy-start.1
  188.3 0.0 copy-start.2
  188.3 0.9 shard_map.67.own_ref
  189.2 0.0 collective-permute-done.4.other_ref
  189.2 0.0 copy-done.1
  189.2 0.0 copy-done.2
  189.2 1.5 shard_map.68
  (3 shorter events, 0.1 us)
Async XLA Ops:
  2.8 27.5 %all-to-all-start = ((f32[16,1,1280]{2,1,0:T(1,128)}), f32[16,1,1280]{2,1,0:T(1,128)S(1)}, u32[]{:S(2)}, u32[]{:S(2)}) async-start(f32[16,1,1280]{2,1,0:T(1,128)} %bitcast.4), calls=%async_computation | async-start | bytes 163840 | tf_op jit(solution)/shard_map/all_to_all | solution.py:386
  18.6 0.9 copy-start
  19.6 3.8 %collective-permute-start = (f32[256,128]{1,0:T(8,128)S(1)}, f32[256,128]{1,0:T(8,128)S(1)}, u32[]{:S(2)}, u32[]{:S(2)}) collective-permute-start(f32[256,128]{1,0:T(8,128)S(1)} %shard_map.51), channel_id=1, source_target_pairs={{0,1},{1,0},{2,3},{3,2},{4,5},{5,4},{6,7},{7,6},{8,9},{9,8},{10,11... | collective-permute-start | bytes 393224 | tf_op jit(solution)/shard_map/ppermute | solution.py:377
  53.4 8.2 %collective-permute-start.1 = (f32[2560,128]{1,0:T(8,128)S(1)}, f32[2560,128]{1,0:T(8,128)S(1)}, u32[]{:S(2)}, u32[]{:S(2)}) collective-permute-start(f32[2560,128]{1,0:T(8,128)S(1)} %get-tuple-element.43.own_ref), channel_id=1, source_target_pairs={{0,1},{1,0},{2,3},{3,2},{4,5},{5,4},{6,7},{7,6},{8,9},{9,8},{10,11... | collective-permute-start | bytes 3932168 | tf_op jit(solution)/shard_map/ppermute | solution.py:377
  89.7 8.3 %collective-permute-start.2 = (f32[512,128]{1,0:T(8,128)S(1)}, f32[512,128]{1,0:T(8,128)S(1)}, u32[]{:S(2)}, u32[]{:S(2)}) collective-permute-start(f32[512,128]{1,0:T(8,128)S(1)} %get-tuple-element.50.own_ref), channel_id=1, source_target_pairs={{0,1},{1,0},{2,3},{3,2},{4,5},{5,4},{6,7},{7,6},{8,9},{9,8},{10,11... | collective-permute-start | bytes 786440 | tf_op jit(solution)/shard_map/ppermute | solution.py:377
  125.0 7.7 %collective-permute-start.3 = (f32[512,128]{1,0:T(8,128)S(1)}, f32[512,128]{1,0:T(8,128)S(1)}, u32[]{:S(2)}, u32[]{:S(2)}) collective-permute-start(f32[512,128]{1,0:T(8,128)S(1)} %shard_map.61.own_ref), channel_id=1, source_target_pairs={{0,1},{1,0},{2,3},{3,2},{4,5},{5,4},{6,7},{7,6},{8,9},{9,8},{10,11... | collective-permute-start | bytes 786440 | tf_op jit(solution)/shard_map/ppermute | solution.py:377
  179.4 9.8 %collective-permute-start.4 = (f32[256,128]{1,0:T(8,128)S(1)}, f32[256,128]{1,0:T(8,128)S(1)}, u32[]{:S(2)}, u32[]{:S(2)}) collective-permute-start(f32[256,128]{1,0:T(8,128)S(1)} %get-tuple-element.69), channel_id=1, source_target_pairs={{0,1},{1,0},{2,3},{3,2},{4,5},{5,4},{6,7},{7,6},{8,9},{9,8},{10,11... | collective-permute-start | bytes 393224 | tf_op jit(solution)/shard_map/ppermute | solution.py:377
  188.3 1.0 copy-start.1
  188.3 1.0 copy-start.2

commit v7 on v5

--- a/solution.py
+++ b/solution.py
@@ -381,7 +381,10 @@
     tile = jnp.where(core > 0, chip, chip % side * side + chip // side)
     spot = jnp.stack([tile, lax.axis_index("batch"), core])
     partner = partner.reshape(-1, LANES)
-    raw = jnp.concatenate([embeddings, partner.astype(jnp.float32)], axis=0)
+    n_values, n_mates = embeddings.size, partner.size
+    values = jnp.pad(embeddings.reshape(-1), (0, n_mates))
+    mates = jnp.pad(partner.reshape(-1), (n_values, 0)).astype(jnp.float32)
+    raw = jnp.where(jnp.arange(n_values + n_mates) < n_values, values, mates).reshape(-1, LANES)
     sent = call(functools.partial(send_body, n_proto, rows), f32(n_batch * raw.shape[0], LANES))(raw)
     sent, held, spot = lax.optimization_barrier((sent, prototypes, spot))
     column = over_layers(sent)

time: 191 us -> 191 us (level)
  no operation moved by 1% of the time
where the time goes in v7:
time: 191 us; the launch traced here: 190 us
  blocking collectives  118 us (62%)
  starting transfers between devices  44.4 us (23%)
  Pallas kernels  15.5 us (8%)
  waiting for transfers between devices  9.46 us (5%)
    all_to_all x3, blocking collectives, over_layers(): lax.all_to_all(lines.reshape(n_batch, 1, -1), 'batch', 0, 0, tiled=True)  48.2 us
    all_to_all x3, blocking collectives, over_chips(): lax.all_to_all(blocks, 'proto', 0, 0, tiled=True, axis_index_groups=same_...  42.1 us
    ppermute x5, starting transfers between devices, swap(): return lax.ppermute(values, 'proto', cores)  28.7 us
    all_to_all x2, blocking collectives, over_ring(): lax.all_to_all(blocks, 'proto', 0, 0, tiled=True, axis_index_groups=groups)  27.8 us
    all_to_all x1, starting transfers between devices, over_layers(): lax.all_to_all(lines.reshape(n_batch, 1, -1), 'batch', 0, 0, tiled=True)  15.7 us
    all_to_all x1, waiting for transfers between devices, over_layers(): lax.all_to_all(lines.reshape(n_batch, 1, -1), 'batch', 0, 0, tiled=True)  6.88 us
  transfers between devices with their start and end apart: 6, of which 3 were waited for; matrix products, arithmetic and copies ran while one was open for 0% of the time, Pallas kernels for 4%

profile of v7, /device:TPU:1, one launch (start us, length us, event | category | flops | bytes accessed | tf_op | source)
XLA Modules:
  0.0 190.1 jit_solution(9776026674603999312)
XLA Ops:
  0.7 0.7 select_bitcast_fusion.in_ref
  1.4 0.7 shard_map.50
  2.1 0.1 pad_add_fusion.spot_ref
  2.2 15.7 %all-to-all-start = ((f32[16,1,1280]{2,1,0:T(1,128)}), f32[16,1,1280]{2,1,0:T(1,128)S(1)}, u32[]{:S(2)}, u32[]{:S(2)}) async-start(f32[16,1,1280]{2,1,0:T(1,128)} %bitcast.5), calls=%async_computation | async-start | bytes 163840 | tf_op jit(solution)/shard_map/all_to_all | solution.py:377
  17.9 0.0 copy-start
  17.9 0.9 copy-done
  18.8 0.1 shard_map.51
  19.0 2.9 %collective-permute-start = (f32[256,128]{1,0:T(8,128)S(1)}, f32[256,128]{1,0:T(8,128)S(1)}, u32[]{:S(2)}, u32[]{:S(2)}) collective-permute-start(f32[256,128]{1,0:T(8,128)S(1)} %shard_map.51), channel_id=1, source_target_pairs={{0,1},{1,0},{2,3},{3,2},{4,5},{5,4},{6,7},{7,6},{8,9},{9,8},{10,11... | collective-permute-start | bytes 393224 | tf_op jit(solution)/shard_map/ppermute | solution.py:368
  21.8 1.0 collective-permute-done
  22.8 6.9 %all-to-all-done = f32[16,1,1280]{2,1,0:T(1,128)S(1)} async-done(((f32[16,1,1280]{2,1,0:T(1,128)}), f32[16,1,1280]{2,1,0:T(1,128)S(1)}, u32[]{:S(2)}, u32[]{:S(2)}) %all-to-all-start) | async-done | bytes 81952 | tf_op jit(solution)/shard_map/all_to_all | solution.py:377
  29.7 0.6 shard_map.52
  30.4 20.9 %all_to_all.45 = f32[16,128,128]{2,1,0:T(8,128)S(1)} all-to-all(f32[16,128,128]{2,1,0:T(8,128)S(1)} %get-tuple-element.38), channel_id=1, replica_groups={{0,8,16,24,2,10,18,26,4,12,20,28,6,14,22,30},{1,3,5,7,9,11,13,15,17,19,..., dimensions={0} | all-to-all | bytes 2097152 | tf_op jit(solution)/shard_map/all_to_all | solution.py:371
  51.3 1.4 shard_map.53
  52.7 5.6 %collective-permute-start.1 = (f32[2560,128]{1,0:T(8,128)S(1)}, f32[2560,128]{1,0:T(8,128)S(1)}, u32[]{:S(2)}, u32[]{:S(2)}) collective-permute-start(f32[2560,128]{1,0:T(8,128)S(1)} %get-tuple-element.40.own_ref), channel_id=1, source_target_pairs={{0,1},{1,0},{2,3},{3,2},{4,5},{5,4},{6,7},{7,6},{8,9},{9,8},{10,11... | collective-permute-start | bytes 3932168 | tf_op jit(solution)/shard_map/ppermute | solution.py:368
  58.3 1.0 shard_map.54._
  59.3 1.6 collective-permute-done.1.other_ref
  60.9 0.6 shard_map.55
  61.5 10.3 %all_to_all.46.in_ref = f32[16,24,128]{2,1,0:T(8,128)S(1)} all-to-all(f32[16,24,128]{2,1,0:T(8,128)S(1)} %shard_map.55), channel_id=1, replica_groups={{0,8,16,24,2,10,18,26,4,12,20,28,6,14,22,30},{1,3,5,7,9,11,13,15,17,19,..., dimensions={0} | all-to-all | bytes 393216 | tf_op jit(solution)/shard_map/all_to_all | solution.py:371
  71.8 16.8 %all_to_all.47 = f32[16,1,2176]{2,1,0:T(1,128)S(1)} all-to-all(f32[16,1,2176]{2,1,0:T(1,128)S(1)} %bitcast.25), channel_id=1, replica_groups=mesh['batch'=16,'proto'=32] {'batch'}, dimensions={0} | all-to-all | bytes 278528 | tf_op jit(solution)/shard_map/all_to_all | solution.py:377
  88.6 0.4 shard_map.57
  89.0 5.9 %collective-permute-start.2 = (f32[512,128]{1,0:T(8,128)S(1)}, f32[512,128]{1,0:T(8,128)S(1)}, u32[]{:S(2)}, u32[]{:S(2)}) collective-permute-start(f32[512,128]{1,0:T(8,128)S(1)} %get-tuple-element.45.own_ref), channel_id=1, source_target_pairs={{0,1},{1,0},{2,3},{3,2},{4,5},{5,4},{6,7},{7,6},{8,9},{9,8},{10,11... | collective-permute-start | bytes 786440 | tf_op jit(solution)/shard_map/ppermute | solution.py:368
  94.9 2.4 %shard_map.58 = (f32[512,1024]{1,0:T(8,128)S(1)}, f32[4096,128]{1,0:T(8,128)S(1)}) custom-call(s32[4096]{0:T(1024)S(1)} %bitcast.29, s32[3]{0:T(128)S(1)} %pad_add_fusion.spot_ref, f32[512,128]{1,0:T(8,128)S(1)} %pad_maximum_fusion.protos_ref, f32[2048,128]{1,0:T(8,128)S(1)} %bitcast.18, f32[2560,128]{1,0:T(8,128)S(1)} %collective-permute-done.1.other_ref), custom_call_target="tpu_custom_call" | custom-call | tf_op jit(solution)/shard_map/pallas_call | solution.py:415
  97.4 0.0 collective-permute-done.2.other_ref
  97.4 0.6 shard_map.59
  97.9 10.9 %all_to_all.48.in_ref = f32[16,24,128]{2,1,0:T(8,128)S(1)} all-to-all(f32[16,24,128]{2,1,0:T(8,128)S(1)} %shard_map.59), channel_id=1, replica_groups={{0,8,16,24,2,10,18,26,4,12,20,28,6,14,22,30},{1,3,5,7,9,11,13,15,17,19,..., dimensions={0} | all-to-all | bytes 393216 | tf_op jit(solution)/shard_map/all_to_all | solution.py:371
  108.9 15.1 %all_to_all.49 = f32[16,1,2048]{2,1,0:T(1,128)S(1)} all-to-all(f32[16,1,2048]{2,1,0:T(1,128)S(1)} %bitcast.28), channel_id=1, replica_groups=mesh['batch'=16,'proto'=32] {'batch'}, dimensions={0} | all-to-all | bytes 262144 | tf_op jit(solution)/shard_map/all_to_all | solution.py:377
  124.0 0.4 shard_map.61.own_ref
  124.4 5.4 %collective-permute-start.3 = (f32[512,128]{1,0:T(8,128)S(1)}, f32[512,128]{1,0:T(8,128)S(1)}, u32[]{:S(2)}, u32[]{:S(2)}) collective-permute-start(f32[512,128]{1,0:T(8,128)S(1)} %shard_map.61.own_ref), channel_id=1, source_target_pairs={{0,1},{1,0},{2,3},{3,2},{4,5},{5,4},{6,7},{7,6},{8,9},{9,8},{10,11... | collective-permute-start | bytes 786440 | tf_op jit(solution)/shard_map/ppermute | solution.py:368
  129.9 2.3 %shard_map.62.second_ref = f32[512,1024]{1,0:T(8,128)S(1)} custom-call(s32[4096]{0:T(1024)S(1)} %bitcast.30, s32[3]{0:T(128)S(1)} %pad_add_fusion.spot_ref, f32[512,128]{1,0:T(8,128)S(1)} %pad_maximum_fusion.protos_ref, f32[4096,128]{1,0:T(8,128)S(1)} %get-tuple-element.54.table_ref), custom_call_target="tpu_custom_call" | custom-call | tf_op jit(solution)/shard_map/pallas_call | solution.py:426
  132.2 0.0 collective-permute-done.3.other_ref
  132.2 1.4 shard_map.63
  133.5 18.3 %all_to_all.50.in_ref = f32[4,1040,128]{2,1,0:T(8,128)S(1)} all-to-all(f32[4,1040,128]{2,1,0:T(8,128)S(1)} %bitcast.21), channel_id=1, replica_groups={{0,2,4,6},{8,10,12,14},{16,18,20,22},{24,26,28,30},{1,9,17,25},{3,11,19..., dimensions={0} | all-to-all | bytes 4259840 | tf_op jit(solution)/shard_map/all_to_all | solution.py:374
  151.8 0.1 shard_map.64
  151.9 9.5 %all_to_all.51.in_ref = f32[4,272,128]{2,1,0:T(8,128)S(1)} all-to-all(f32[4,272,128]{2,1,0:T(8,128)S(1)} %shard_map.64), channel_id=1, replica_groups={{0,8,16,24},{2,10,18,26},{4,12,20,28},{6,14,22,30},{1,3,5,7},{9,11,13,1..., dimensions={0} | all-to-all | bytes 1114112 | tf_op jit(solution)/shard_map/all_to_all | solution.py:374
  161.4 0.1 shard_map.65
  161.5 16.3 %all_to_all.52 = f32[16,1,4096]{2,1,0:T(1,128)S(1)} all-to-all(f32[16,1,4096]{2,1,0:T(1,128)S(1)} %bitcast.23), channel_id=1, replica_groups=mesh['batch'=16,'proto'=32] {'batch'}, dimensions={0} | all-to-all | bytes 524288 | tf_op jit(solution)/shard_map/all_to_all | solution.py:377
  177.8 1.0 shard_map.66
  178.8 8.9 %collective-permute-start.4 = (f32[256,128]{1,0:T(8,128)S(1)}, f32[256,128]{1,0:T(8,128)S(1)}, u32[]{:S(2)}, u32[]{:S(2)}) collective-permute-start(f32[256,128]{1,0:T(8,128)S(1)} %get-tuple-element.63), channel_id=1, source_target_pairs={{0,1},{1,0},{2,3},{3,2},{4,5},{5,4},{6,7},{7,6},{8,9},{9,8},{10,11... | collective-permute-start | bytes 393224 | tf_op jit(solution)/shard_map/ppermute | solution.py:368
  187.7 0.0 copy-start.1
  187.7 0.0 copy-start.2
  187.7 0.9 shard_map.67.own_ref
  188.6 0.0 collective-permute-done.4.other_ref
  188.6 0.0 copy-done.1
  188.6 0.0 copy-done.2
  188.6 1.4 shard_map.68
  (3 shorter events, 0.1 us)
Async XLA Ops:
  2.2 27.5 %all-to-all-start = ((f32[16,1,1280]{2,1,0:T(1,128)}), f32[16,1,1280]{2,1,0:T(1,128)S(1)}, u32[]{:S(2)}, u32[]{:S(2)}) async-start(f32[16,1,1280]{2,1,0:T(1,128)} %bitcast.5), calls=%async_computation | async-start | bytes 163840 | tf_op jit(solution)/shard_map/all_to_all | solution.py:377
  17.9 0.9 copy-start
  19.0 3.8 %collective-permute-start = (f32[256,128]{1,0:T(8,128)S(1)}, f32[256,128]{1,0:T(8,128)S(1)}, u32[]{:S(2)}, u32[]{:S(2)}) collective-permute-start(f32[256,128]{1,0:T(8,128)S(1)} %shard_map.51), channel_id=1, source_target_pairs={{0,1},{1,0},{2,3},{3,2},{4,5},{5,4},{6,7},{7,6},{8,9},{9,8},{10,11... | collective-permute-start | bytes 393224 | tf_op jit(solution)/shard_map/ppermute | solution.py:368
  52.7 8.2 %collective-permute-start.1 = (f32[2560,128]{1,0:T(8,128)S(1)}, f32[2560,128]{1,0:T(8,128)S(1)}, u32[]{:S(2)}, u32[]{:S(2)}) collective-permute-start(f32[2560,128]{1,0:T(8,128)S(1)} %get-tuple-element.40.own_ref), channel_id=1, source_target_pairs={{0,1},{1,0},{2,3},{3,2},{4,5},{5,4},{6,7},{7,6},{8,9},{9,8},{10,11... | collective-permute-start | bytes 3932168 | tf_op jit(solution)/shard_map/ppermute | solution.py:368
  89.0 8.4 %collective-permute-start.2 = (f32[512,128]{1,0:T(8,128)S(1)}, f32[512,128]{1,0:T(8,128)S(1)}, u32[]{:S(2)}, u32[]{:S(2)}) collective-permute-start(f32[512,128]{1,0:T(8,128)S(1)} %get-tuple-element.45.own_ref), channel_id=1, source_target_pairs={{0,1},{1,0},{2,3},{3,2},{4,5},{5,4},{6,7},{7,6},{8,9},{9,8},{10,11... | collective-permute-start | bytes 786440 | tf_op jit(solution)/shard_map/ppermute | solution.py:368
  124.4 7.7 %collective-permute-start.3 = (f32[512,128]{1,0:T(8,128)S(1)}, f32[512,128]{1,0:T(8,128)S(1)}, u32[]{:S(2)}, u32[]{:S(2)}) collective-permute-start(f32[512,128]{1,0:T(8,128)S(1)} %shard_map.61.own_ref), channel_id=1, source_target_pairs={{0,1},{1,0},{2,3},{3,2},{4,5},{5,4},{6,7},{7,6},{8,9},{9,8},{10,11... | collective-permute-start | bytes 786440 | tf_op jit(solution)/shard_map/ppermute | solution.py:368
  178.8 9.8 %collective-permute-start.4 = (f32[256,128]{1,0:T(8,128)S(1)}, f32[256,128]{1,0:T(8,128)S(1)}, u32[]{:S(2)}, u32[]{:S(2)}) collective-permute-start(f32[256,128]{1,0:T(8,128)S(1)} %get-tuple-element.63), channel_id=1, source_target_pairs={{0,1},{1,0},{2,3},{3,2},{4,5},{5,4},{6,7},{7,6},{8,9},{9,8},{10,11... | collective-permute-start | bytes 393224 | tf_op jit(solution)/shard_map/ppermute | solution.py:368
  187.7 1.0 copy-start.1
  187.7 1.0 copy-start.2

commit v8 on v7

--- a/solution.py
+++ b/solution.py
@@ -331,19 +331,20 @@
     return jnp.sum(jnp.where(lane == layer * 8 + line, values, 0.0), axis=1, keepdims=True)
 
 
-def own_grads_body(e_ref, first_ref, second_ref, scale_ref, inverse_ref, clips_ref, out_ref):
+def own_grads_body(spot_ref, e_ref, first_ref, second_ref, scale_ref, inverse_ref, clips_ref, sums_ref, embeddings_ref,
+                   out_ref, clip_ref):
     tiles = inverse_ref.shape[0] // 2
+    own_mass = own_values(inverse_ref, spot_ref[0], spot_ref[1])
+    own_share = own_values(inverse_ref, spot_ref[0] + tiles, spot_ref[1])
+    clip_ref[...] = finish_rows(embeddings_ref[...], 10.0 * (sums_ref[:8] * own_share - sums_ref[8:] * own_mass))
     rows = slice(0, out_ref.shape[0])
     out_ref[...] = proto_grads(
         rows, e_ref, first_ref, second_ref, scale_ref, inverse_ref[tiles:], inverse_ref[:tiles], clips_ref
     )
 
 
-def finish_body(spot_ref, inverse_ref, sums_ref, embeddings_ref, protos_ref, own_ref, other_ref, clip_ref, proto_ref):
-    tiles = inverse_ref.shape[0] // 2
-    own_mass = own_values(inverse_ref, spot_ref[0], spot_ref[1])
-    own_share = own_values(inverse_ref, spot_ref[0] + tiles, spot_ref[1])
-    clip_ref[...] = finish_rows(embeddings_ref[...], 10.0 * (sums_ref[:8] * own_share - sums_ref[8:] * own_mass))
+def finish_body(held_ref, protos_ref, own_ref, other_ref, clip_ref, proto_ref):
+    clip_ref[...] = held_ref[...]
     proto_ref[...] = finish_rows(protos_ref[...], own_ref[...] + other_ref[...])
 
 
@@ -439,10 +440,12 @@
     other_grads, sums, inverse = call(
         other_grads_body, (f32(own_protos, features), f32(2 * rows, features), f32(2 * tiles, LANES))
     )(e, first_e, second_e, scale, totals, over_layers(lines), own_clips)
-    own_grads = call(own_grads_body, f32(own_protos, features))(e, first_e, second_e, scale, inverse, own_clips)
-    return call(
-        finish_body, (f32(rows, features), f32(own_protos, features)), in_specs=[smem] + [vmem] * 6
-    )(spot, inverse, sums, embeddings, prototypes, own_grads, swap(other_grads))
+    own_grads, held = call(
+        own_grads_body, (f32(own_protos, features), f32(rows, features)), in_specs=[smem] + [vmem] * 8
+    )(spot, e, first_e, second_e, scale, inverse, own_clips, sums, embeddings)
+    return call(finish_body, (f32(rows, features), f32(own_protos, features)))(
+        held, prototypes, own_grads, swap(other_grads)
+    )
 
 
 def solution(mesh):

time: 191 us -> 191 us (level)
  no operation moved by 1% of the time
where the time goes in v8:
time: 191 us; the launch traced here: 190 us
  blocking collectives  118 us (62%)
  starting transfers between devices  44.4 us (23%)
  Pallas kernels  15.5 us (8%)
  waiting for transfers between devices  9.45 us (5%)
    all_to_all x3, blocking collectives, over_layers(): lax.all_to_all(lines.reshape(n_batch, 1, -1), 'batch', 0, 0, tiled=True)  48.2 us
    all_to_all x3, blocking collectives, over_chips(): lax.all_to_all(blocks, 'proto', 0, 0, tiled=True, axis_index_groups=same_...  42.1 us
    ppermute x5, starting transfers between devices, swap(): return lax.ppermute(values, 'proto', cores)  28.7 us
    all_to_all x2, blocking collectives, over_ring(): lax.all_to_all(blocks, 'proto', 0, 0, tiled=True, axis_index_groups=groups)  27.8 us
    all_to_all x1, starting transfers between devices, over_layers(): lax.all_to_all(lines.reshape(n_batch, 1, -1), 'batch', 0, 0, tiled=True)  15.7 us
    all_to_all x1, waiting for transfers between devices, over_layers(): lax.all_to_all(lines.reshape(n_batch, 1, -1), 'batch', 0, 0, tiled=True)  6.88 us
  transfers between devices with their start and end apart: 6, of which 3 were waited for; matrix products, arithmetic and copies ran while one was open for 0% of the time, Pallas kernels for 4%

profile of v8, /device:TPU:1, one launch (start us, length us, event | category | flops | bytes accessed | tf_op | source)
XLA Modules:
  0.0 190.1 jit_solution(7713448825705912939)
XLA Ops:
  0.7 0.7 select_bitcast_fusion.in_ref
  1.4 0.7 shard_map.50
  2.1 0.1 pad_add_fusion.spot_ref
  2.2 15.7 %all-to-all-start = ((f32[16,1,1280]{2,1,0:T(1,128)}), f32[16,1,1280]{2,1,0:T(1,128)S(1)}, u32[]{:S(2)}, u32[]{:S(2)}) async-start(f32[16,1,1280]{2,1,0:T(1,128)} %bitcast.5), calls=%async_computation | async-start | bytes 163840 | tf_op jit(solution)/shard_map/all_to_all | solution.py:378
  17.9 0.0 copy-start
  17.9 0.9 copy-done
  18.8 0.1 shard_map.51
  19.0 2.9 %collective-permute-start = (f32[256,128]{1,0:T(8,128)S(1)}, f32[256,128]{1,0:T(8,128)S(1)}, u32[]{:S(2)}, u32[]{:S(2)}) collective-permute-start(f32[256,128]{1,0:T(8,128)S(1)} %shard_map.51), channel_id=1, source_target_pairs={{0,1},{1,0},{2,3},{3,2},{4,5},{5,4},{6,7},{7,6},{8,9},{9,8},{10,11... | collective-permute-start | bytes 393224 | tf_op jit(solution)/shard_map/ppermute | solution.py:369
  21.8 1.0 collective-permute-done
  22.8 6.9 %all-to-all-done = f32[16,1,1280]{2,1,0:T(1,128)S(1)} async-done(((f32[16,1,1280]{2,1,0:T(1,128)}), f32[16,1,1280]{2,1,0:T(1,128)S(1)}, u32[]{:S(2)}, u32[]{:S(2)}) %all-to-all-start) | async-done | bytes 81952 | tf_op jit(solution)/shard_map/all_to_all | solution.py:378
  29.7 0.6 shard_map.52
  30.4 20.9 %all_to_all.45 = f32[16,128,128]{2,1,0:T(8,128)S(1)} all-to-all(f32[16,128,128]{2,1,0:T(8,128)S(1)} %get-tuple-element.40), channel_id=1, replica_groups={{0,8,16,24,2,10,18,26,4,12,20,28,6,14,22,30},{1,3,5,7,9,11,13,15,17,19,..., dimensions={0} | all-to-all | bytes 2097152 | tf_op jit(solution)/shard_map/all_to_all | solution.py:372
  51.3 1.4 shard_map.53
  52.7 5.6 %collective-permute-start.1 = (f32[2560,128]{1,0:T(8,128)S(1)}, f32[2560,128]{1,0:T(8,128)S(1)}, u32[]{:S(2)}, u32[]{:S(2)}) collective-permute-start(f32[2560,128]{1,0:T(8,128)S(1)} %get-tuple-element.42.own_ref), channel_id=1, source_target_pairs={{0,1},{1,0},{2,3},{3,2},{4,5},{5,4},{6,7},{7,6},{8,9},{9,8},{10,11... | collective-permute-start | bytes 3932168 | tf_op jit(solution)/shard_map/ppermute | solution.py:369
  58.3 1.0 shard_map.54._
  59.3 1.6 collective-permute-done.1.other_ref
  60.9 0.6 shard_map.55
  61.5 10.3 %all_to_all.46.in_ref = f32[16,24,128]{2,1,0:T(8,128)S(1)} all-to-all(f32[16,24,128]{2,1,0:T(8,128)S(1)} %shard_map.55), channel_id=1, replica_groups={{0,8,16,24,2,10,18,26,4,12,20,28,6,14,22,30},{1,3,5,7,9,11,13,15,17,19,..., dimensions={0} | all-to-all | bytes 393216 | tf_op jit(solution)/shard_map/all_to_all | solution.py:372
  71.8 16.8 %all_to_all.47 = f32[16,1,2176]{2,1,0:T(1,128)S(1)} all-to-all(f32[16,1,2176]{2,1,0:T(1,128)S(1)} %bitcast.25), channel_id=1, replica_groups=mesh['batch'=16,'proto'=32] {'batch'}, dimensions={0} | all-to-all | bytes 278528 | tf_op jit(solution)/shard_map/all_to_all | solution.py:378
  88.6 0.4 shard_map.57
  89.0 5.9 %collective-permute-start.2 = (f32[512,128]{1,0:T(8,128)S(1)}, f32[512,128]{1,0:T(8,128)S(1)}, u32[]{:S(2)}, u32[]{:S(2)}) collective-permute-start(f32[512,128]{1,0:T(8,128)S(1)} %get-tuple-element.47.own_ref), channel_id=1, source_target_pairs={{0,1},{1,0},{2,3},{3,2},{4,5},{5,4},{6,7},{7,6},{8,9},{9,8},{10,11... | collective-permute-start | bytes 786440 | tf_op jit(solution)/shard_map/ppermute | solution.py:369
  94.9 2.4 %shard_map.58 = (f32[512,1024]{1,0:T(8,128)S(1)}, f32[4096,128]{1,0:T(8,128)S(1)}) custom-call(s32[4096]{0:T(1024)S(1)} %bitcast.29, s32[3]{0:T(128)S(1)} %pad_add_fusion.spot_ref, f32[512,128]{1,0:T(8,128)S(1)} %pad_maximum_fusion.protos_ref, f32[2048,128]{1,0:T(8,128)S(1)} %bitcast.18, f32[2560,128]{1,0:T(8,128)S(1)} %collective-permute-done.1.other_ref), custom_call_target="tpu_custom_call" | custom-call | tf_op jit(solution)/shard_map/pallas_call | solution.py:416
  97.4 0.0 collective-permute-done.2.other_ref
  97.4 0.6 shard_map.59
  97.9 10.9 %all_to_all.48.in_ref = f32[16,24,128]{2,1,0:T(8,128)S(1)} all-to-all(f32[16,24,128]{2,1,0:T(8,128)S(1)} %shard_map.59), channel_id=1, replica_groups={{0,8,16,24,2,10,18,26,4,12,20,28,6,14,22,30},{1,3,5,7,9,11,13,15,17,19,..., dimensions={0} | all-to-all | bytes 393216 | tf_op jit(solution)/shard_map/all_to_all | solution.py:372
  108.9 15.1 %all_to_all.49 = f32[16,1,2048]{2,1,0:T(1,128)S(1)} all-to-all(f32[16,1,2048]{2,1,0:T(1,128)S(1)} %bitcast.28), channel_id=1, replica_groups=mesh['batch'=16,'proto'=32] {'batch'}, dimensions={0} | all-to-all | bytes 262144 | tf_op jit(solution)/shard_map/all_to_all | solution.py:378
  124.0 0.4 shard_map.61.own_ref
  124.4 5.4 %collective-permute-start.3 = (f32[512,128]{1,0:T(8,128)S(1)}, f32[512,128]{1,0:T(8,128)S(1)}, u32[]{:S(2)}, u32[]{:S(2)}) collective-permute-start(f32[512,128]{1,0:T(8,128)S(1)} %shard_map.61.own_ref), channel_id=1, source_target_pairs={{0,1},{1,0},{2,3},{3,2},{4,5},{5,4},{6,7},{7,6},{8,9},{9,8},{10,11... | collective-permute-start | bytes 786440 | tf_op jit(solution)/shard_map/ppermute | solution.py:369
  129.9 2.3 %shard_map.62.second_ref = f32[512,1024]{1,0:T(8,128)S(1)} custom-call(s32[4096]{0:T(1024)S(1)} %bitcast.30, s32[3]{0:T(128)S(1)} %pad_add_fusion.spot_ref, f32[512,128]{1,0:T(8,128)S(1)} %pad_maximum_fusion.protos_ref, f32[4096,128]{1,0:T(8,128)S(1)} %get-tuple-element.56.table_ref), custom_call_target="tpu_custom_call" | custom-call | tf_op jit(solution)/shard_map/pallas_call | solution.py:427
  132.2 0.0 collective-permute-done.3.other_ref
  132.2 1.4 shard_map.63
  133.6 18.3 %all_to_all.50.in_ref = f32[4,1040,128]{2,1,0:T(8,128)S(1)} all-to-all(f32[4,1040,128]{2,1,0:T(8,128)S(1)} %bitcast.21), channel_id=1, replica_groups={{0,2,4,6},{8,10,12,14},{16,18,20,22},{24,26,28,30},{1,9,17,25},{3,11,19..., dimensions={0} | all-to-all | bytes 4259840 | tf_op jit(solution)/shard_map/all_to_all | solution.py:375
  151.8 0.1 shard_map.64
  151.9 9.5 %all_to_all.51.in_ref = f32[4,272,128]{2,1,0:T(8,128)S(1)} all-to-all(f32[4,272,128]{2,1,0:T(8,128)S(1)} %shard_map.64), channel_id=1, replica_groups={{0,8,16,24},{2,10,18,26},{4,12,20,28},{6,14,22,30},{1,3,5,7},{9,11,13,1..., dimensions={0} | all-to-all | bytes 1114112 | tf_op jit(solution)/shard_map/all_to_all | solution.py:375
  161.5 0.1 shard_map.65
  161.6 16.3 %all_to_all.52 = f32[16,1,4096]{2,1,0:T(1,128)S(1)} all-to-all(f32[16,1,4096]{2,1,0:T(1,128)S(1)} %bitcast.23), channel_id=1, replica_groups=mesh['batch'=16,'proto'=32] {'batch'}, dimensions={0} | all-to-all | bytes 524288 | tf_op jit(solution)/shard_map/all_to_all | solution.py:378
  177.8 0.0 copy-start.2
  177.9 1.0 shard_map.66
  178.8 8.9 %collective-permute-start.4 = (f32[256,128]{1,0:T(8,128)S(1)}, f32[256,128]{1,0:T(8,128)S(1)}, u32[]{:S(2)}, u32[]{:S(2)}) collective-permute-start(f32[256,128]{1,0:T(8,128)S(1)} %get-tuple-element.67), channel_id=1, source_target_pairs={{0,1},{1,0},{2,3},{3,2},{4,5},{5,4},{6,7},{7,6},{8,9},{9,8},{10,11... | collective-permute-start | bytes 393224 | tf_op jit(solution)/shard_map/ppermute | solution.py:369
  187.7 0.0 copy-done.2
  187.7 0.0 copy-start.1
  187.7 1.5 shard_map.67
  189.2 0.0 collective-permute-done.4.other_ref
  189.2 0.0 copy-done.1
  189.2 0.9 shard_map.68
  (3 shorter events, 0.1 us)
Async XLA Ops:
  2.2 27.5 %all-to-all-start = ((f32[16,1,1280]{2,1,0:T(1,128)}), f32[16,1,1280]{2,1,0:T(1,128)S(1)}, u32[]{:S(2)}, u32[]{:S(2)}) async-start(f32[16,1,1280]{2,1,0:T(1,128)} %bitcast.5), calls=%async_computation | async-start | bytes 163840 | tf_op jit(solution)/shard_map/all_to_all | solution.py:378
  17.9 0.9 copy-start
  19.0 3.8 %collective-permute-start = (f32[256,128]{1,0:T(8,128)S(1)}, f32[256,128]{1,0:T(8,128)S(1)}, u32[]{:S(2)}, u32[]{:S(2)}) collective-permute-start(f32[256,128]{1,0:T(8,128)S(1)} %shard_map.51), channel_id=1, source_target_pairs={{0,1},{1,0},{2,3},{3,2},{4,5},{5,4},{6,7},{7,6},{8,9},{9,8},{10,11... | collective-permute-start | bytes 393224 | tf_op jit(solution)/shard_map/ppermute | solution.py:369
  52.7 8.2 %collective-permute-start.1 = (f32[2560,128]{1,0:T(8,128)S(1)}, f32[2560,128]{1,0:T(8,128)S(1)}, u32[]{:S(2)}, u32[]{:S(2)}) collective-permute-start(f32[2560,128]{1,0:T(8,128)S(1)} %get-tuple-element.42.own_ref), channel_id=1, source_target_pairs={{0,1},{1,0},{2,3},{3,2},{4,5},{5,4},{6,7},{7,6},{8,9},{9,8},{10,11... | collective-permute-start | bytes 3932168 | tf_op jit(solution)/shard_map/ppermute | solution.py:369
  89.0 8.4 %collective-permute-start.2 = (f32[512,128]{1,0:T(8,128)S(1)}, f32[512,128]{1,0:T(8,128)S(1)}, u32[]{:S(2)}, u32[]{:S(2)}) collective-permute-start(f32[512,128]{1,0:T(8,128)S(1)} %get-tuple-element.47.own_ref), channel_id=1, source_target_pairs={{0,1},{1,0},{2,3},{3,2},{4,5},{5,4},{6,7},{7,6},{8,9},{9,8},{10,11... | collective-permute-start | bytes 786440 | tf_op jit(solution)/shard_map/ppermute | solution.py:369
  124.4 7.8 %collective-permute-start.3 = (f32[512,128]{1,0:T(8,128)S(1)}, f32[512,128]{1,0:T(8,128)S(1)}, u32[]{:S(2)}, u32[]{:S(2)}) collective-permute-start(f32[512,128]{1,0:T(8,128)S(1)} %shard_map.61.own_ref), channel_id=1, source_target_pairs={{0,1},{1,0},{2,3},{3,2},{4,5},{5,4},{6,7},{7,6},{8,9},{9,8},{10,11... | collective-permute-start | bytes 786440 | tf_op jit(solution)/shard_map/ppermute | solution.py:369
  177.8 9.8 %copy-start.2 = (f32[8,128]{1,0:T(8,128)S(1)}, f32[8,128]{1,0:T(8,128)}, u32[]{:S(2)}) copy-start(f32[8,128]{1,0:T(8,128)} %embeddings_ref.1) | copy-start | bytes 12292
  178.8 10.4 %collective-permute-start.4 = (f32[256,128]{1,0:T(8,128)S(1)}, f32[256,128]{1,0:T(8,128)S(1)}, u32[]{:S(2)}, u32[]{:S(2)}) collective-permute-start(f32[256,128]{1,0:T(8,128)S(1)} %get-tuple-element.67), channel_id=1, source_target_pairs={{0,1},{1,0},{2,3},{3,2},{4,5},{5,4},{6,7},{7,6},{8,9},{9,8},{10,11... | collective-permute-start | bytes 393224 | tf_op jit(solution)/shard_map/ppermute | solution.py:369
  187.7 1.5 copy-start.1
